TPU v7x, 256 devices: a whole 4x4x8 slice. The times are simulated.
256 devices in a mesh: section: 4 (over x_hi, core), seq: 64 (over y, z, x_lo).
Axes of the slice: x: 4 (x_hi: 2, x_lo: 2; x = x_hi * 2 + x_lo), y: 4, z: 8, core: 2. Of those that a mesh axis runs over, the one named last changes fastest.
Arguments:
- stream: bfloat16 [4, 18432, 2560], P('section', 'seq'), may hold values from -6 to 6
- query: bfloat16 [4, 18432, 2560], P('section', 'seq'), may hold values from -60 to 60
- short_key: bfloat16 [4, 2048, 2560], P('section', 'seq'), may hold values from -8 to 8
- short_value: bfloat16 [4, 2048, 2560], P('section', 'seq'), may hold values from -16 to 16
- short_out: bfloat16 [4, 2048, 2560], P('section', 'seq'), may hold values from -6 to 6
Outputs:
- output: bfloat16 [4, 18432, 2560], P('section', 'seq')
- bottleneck: bfloat16 [4, 2048, 2560], P('section', 'seq')
All inputs are finite; a program needn't handle non-finite values.
Results may differ from a plain program's by a relative error of at most 0.0085.
Values may be sent and summed in bfloat16 or wider, within the bound.
No kernel may reach another device: no remote copies, remote signals or barrier semaphores. Data moves between devices by JAX's collectives and lax.ppermute only.
A program may use at most 128 MiB of HBM per device.

v0:
```python
import functools
import math

import jax
import jax.numpy as jnp
from jax import lax
from jax.experimental import pallas as pl
from jax.experimental.pallas import tpu as pltpu
from jax.sharding import PartitionSpec as P

HEADS = 20
HEAD = 128
NY, NZ, NX = 4, 8, 2
GROUP = HEADS // NY
PHASES = ((0, 3), (3, 2))
SCALE = math.log2(math.e) / math.sqrt(HEAD)
VMEM = 20 * 1024 * 1024


def seq_pairs(dy, dz, dx):
    pairs = []
    for y in range(NY):
        for z in range(NZ):
            for x in range(NX):
                to = (((y + dy) % NY) * NZ + (z + dz) % NZ) * NX + (x + dx) % NX
                pairs.append(((y * NZ + z) * NX + x, to))
    return pairs


def move(block, dy=0, dz=0, dx=0):
    return lax.ppermute(block, "seq", seq_pairs(dy, dz, dx))


def section_shift(block, by):
    count = lax.axis_size("section")
    return lax.ppermute(block, "section", [(i, (i + by) % count) for i in range(count)])


def after(value, *others):
    return lax.optimization_barrier((value,) + others)[0]


def pack_kernel(where_ref, key_ref, value_ref, *out_refs):
    part = GROUP * HEAD
    for d in range(NY):
        group = lax.rem(where_ref[0] + d, NY)
        columns = pl.ds(pl.multiple_of(group * part, part), part)
        out_refs[d][0] = key_ref[:, columns]
        out_refs[d][1] = value_ref[:, columns]


def pack(where, keys, values):
    piece = jax.ShapeDtypeStruct((2, keys.shape[0], GROUP * HEAD), jnp.bfloat16)
    return pl.pallas_call(
        pack_kernel,
        in_specs=[pl.BlockSpec(memory_space=pltpu.SMEM)] + [pl.BlockSpec(memory_space=pltpu.VMEM)] * 2,
        out_specs=[pl.BlockSpec(memory_space=pltpu.VMEM)] * NY,
        out_shape=[piece] * NY,
        compiler_params=pltpu.CompilerParams(vmem_limit_bytes=VMEM),
        cost_estimate=pl.CostEstimate(flops=0, bytes_accessed=8 * keys.size, transcendentals=0),
    )(where, keys, values)


def pool_kernel(rim_ref, rows_ref, out_ref):
    count, rows = out_ref.shape[0], rows_ref.shape[0]
    j = lax.broadcasted_iota(jnp.int32, (count, rows), 0)
    r = lax.broadcasted_iota(jnp.int32, (count, rows), 1)
    inside = ((r <= 9 * j) & (r >= 9 * j - 8)).astype(jnp.bfloat16)
    first = (lax.broadcasted_iota(jnp.int32, (count, 8), 0) == 0).astype(jnp.bfloat16)
    total = jnp.dot(inside, rows_ref[...], preferred_element_type=jnp.float32)
    total += jnp.dot(first, rim_ref[...], preferred_element_type=jnp.float32)
    out_ref[...] = (total / 9.0).astype(out_ref.dtype)


def pool(rim, rows):
    count, width = rows.shape[0] // 9, rows.shape[1]
    return pl.pallas_call(
        pool_kernel,
        out_shape=jax.ShapeDtypeStruct((count, width), jnp.bfloat16),
        compiler_params=pltpu.CompilerParams(vmem_limit_bytes=VMEM),
        cost_estimate=pl.CostEstimate(
            flops=2 * count * rows.size, bytes_accessed=2 * rows.size + 2 * count * width, transcendentals=0
        ),
    )(rim, rows)


def attend_kernel(n_kv, first, where_ref, *refs):
    q_refs, refs = refs[:NY], refs[NY:]
    kv_refs, refs = refs[:n_kv], refs[n_kv:]
    out_refs, (qs, ks, vs, ss) = refs[:NY], refs[NY:]
    y, z, xl = where_ref[0], where_ref[1], where_ref[2]
    rows, keys = qs.shape[1], ks.shape[1]
    ones = jnp.ones((keys, HEAD), jnp.bfloat16)
    base = (z * NX + xl) * rows
    for h in range(out_refs[0].shape[1] // HEAD):
        for d in range(NY):
            g = lax.rem(y + NY - d, NY)
            if d == 0:
                own = pl.ds(pl.multiple_of((y * GROUP + first + h) * HEAD, HEAD), HEAD)
                qs[g] = q_refs[d][:, own]
            else:
                qs[g] = q_refs[d][:, (first + h) * HEAD : (first + h + 1) * HEAD]
            for n, (shift, slots) in enumerate(KV_ORDER):
                zz = lax.rem(z + shift, NZ)
                at_head = first + h if kv_refs[n].shape[-1] == GROUP * HEAD else h
                column = slice(at_head * HEAD, at_head * HEAD + HEAD)
                for at, slot in enumerate(slots):
                    xx = xl if slot == 0 else 1 - xl
                    place = pl.ds(pl.multiple_of((zz * NX + xx) * 32, 32), 32)
                    ks[g, place, :] = kv_refs[n][d, 0, at * 32 : at * 32 + 32, column]
                    vs[g, place, :] = kv_refs[n][d, 1, at * 32 : at * 32 + 32, column]
        tops = [None] * NY
        for k in range(NY):
            q = qs[k:].reshape((NY - k) * rows, HEAD)
            s = lax.dot_general(q, ks[k], (((1,), (1,)), ((), ())), preferred_element_type=jnp.float32)
            for g in range(k, NY):
                part = s[(g - k) * rows : (g - k + 1) * rows]
                if k == g:
                    col = lax.broadcasted_iota(jnp.int32, part.shape, 1)
                    row = lax.broadcasted_iota(jnp.int32, part.shape, 0)
                    part = jnp.where(9 * col - row <= base, part, -1e30)
                ss[k, g * rows : (g + 1) * rows, :] = part
                here = jnp.max(part, axis=-1, keepdims=True)
                tops[g] = here if k == 0 else jnp.maximum(tops[g], here)
        sums = [jnp.zeros((rows, 2 * HEAD), jnp.float32) for _ in range(NY)]
        for k in range(NY):
            values = jnp.concatenate([vs[k], ones], axis=1)
            for g in range(k, NY):
                p = jnp.exp2((ss[k, g * rows : (g + 1) * rows, :] - tops[g]) * SCALE)
                sums[g] += jnp.dot(p.astype(jnp.bfloat16), values, preferred_element_type=jnp.float32)
        for g in range(NY):
            qs[g] = (sums[g][:, :HEAD] / sums[g][:, HEAD:]).astype(jnp.bfloat16)
        for d in range(NY):
            out_refs[d][:, h * HEAD : h * HEAD + HEAD] = qs[lax.rem(y + NY - d, NY)]


KV_ORDER = (
    (0, (0, 1)), (7, (0, 1)), (1, (0, 1)), (6, (0, 1)), (2, (0, 1)), (5, (0, 1)), (3, (0, 1)), (4, (0,)), (4, (1,)),
)


def attend(where, query, q_slots, arrivals, first, count):
    rows = query.shape[0]
    keys = NZ * NX * 32
    pairs = NY * (NY + 1) // 2 * rows * keys * count
    n_in = NY + len(arrivals)
    return pl.pallas_call(
        functools.partial(attend_kernel, len(arrivals), first),
        in_specs=[pl.BlockSpec(memory_space=pltpu.SMEM)] + [pl.BlockSpec(memory_space=pltpu.VMEM)] * n_in,
        out_specs=[pl.BlockSpec(memory_space=pltpu.VMEM)] * NY,
        out_shape=[jax.ShapeDtypeStruct((rows, count * HEAD), jnp.bfloat16)] * NY,
        scratch_shapes=[
            pltpu.VMEM((NY, rows, HEAD), jnp.bfloat16),
            pltpu.VMEM((NY, keys, HEAD), jnp.bfloat16),
            pltpu.VMEM((NY, keys, HEAD), jnp.bfloat16),
            pltpu.VMEM((NY, NY * rows, keys), jnp.float32),
        ],
        compiler_params=pltpu.CompilerParams(vmem_limit_bytes=VMEM),
        cost_estimate=pl.CostEstimate(
            flops=6 * pairs * HEAD, bytes_accessed=4 * NY * keys * HEAD * count, transcendentals=pairs
        ),
    )(where, query, *q_slots, *arrivals)


def base_kernel(mirrored_ref, short_ref, out_ref):
    rows, count = out_ref.shape[0], short_ref.shape[0]
    i = lax.broadcasted_iota(jnp.int32, (rows, count), 0)
    j = lax.broadcasted_iota(jnp.int32, (rows, count), 1)
    spread = ((i >= 9 * j) & (i < 9 * j + 9)).astype(jnp.bfloat16)
    total = jnp.dot(spread, short_ref[...], preferred_element_type=jnp.float32)
    out_ref[...] = mirrored_ref[...].astype(jnp.float32) + total


def base(mirrored, short_rows):
    return pl.pallas_call(
        base_kernel,
        in_specs=[pl.BlockSpec(memory_space=pltpu.VMEM)] * 2,
        out_specs=pl.BlockSpec(memory_space=pltpu.VMEM),
        out_shape=jax.ShapeDtypeStruct(mirrored.shape, jnp.float32),
        compiler_params=pltpu.CompilerParams(vmem_limit_bytes=VMEM),
        cost_estimate=pl.CostEstimate(
            flops=2 * short_rows.shape[0] * mirrored.size, bytes_accessed=6 * mirrored.size, transcendentals=0
        ),
    )(mirrored, short_rows)


def finish_kernel(where_ref, base_ref, pooled_ref, *refs):
    o_refs, (out_ref, bottle_ref, total, sems) = refs[:-4], refs[-4:]
    y, part = where_ref[0], GROUP * HEAD
    copies = [pltpu.make_async_copy(pooled_ref, bottle_ref, sems.at[NY])]
    copies[0].start()
    for d in range(NY):
        g = lax.rem(y + d, NY)
        for n, (first, heads) in enumerate(PHASES):
            columns = pl.ds(pl.multiple_of((g * GROUP + first) * HEAD, HEAD), heads * HEAD)
            summed = base_ref[:, columns] + o_refs[n * NY + d][...].astype(jnp.float32)
            total[:, columns] = summed.astype(out_ref.dtype)
        columns = pl.ds(pl.multiple_of(g * part, part), part)
        copies.append(pltpu.make_async_copy(total.at[:, columns], out_ref.at[:, columns], sems.at[d]))
        copies[-1].start()
    for copy in copies:
        copy.wait()


def finish(where, total, pooled, o_slots):
    in_specs = [pl.BlockSpec(memory_space=pltpu.SMEM)]
    in_specs += [pl.BlockSpec(memory_space=pltpu.VMEM)] * (2 + len(o_slots))
    return pl.pallas_call(
        finish_kernel,
        in_specs=in_specs,
        out_specs=[pl.BlockSpec(memory_space=pltpu.HBM)] * 2,
        out_shape=[
            jax.ShapeDtypeStruct(total.shape, jnp.bfloat16),
            jax.ShapeDtypeStruct(pooled.shape, jnp.bfloat16),
        ],
        scratch_shapes=[pltpu.VMEM(total.shape, jnp.bfloat16), pltpu.SemaphoreType.DMA((NY + 1,))],
        compiler_params=pltpu.CompilerParams(vmem_limit_bytes=VMEM),
        cost_estimate=pl.CostEstimate(flops=total.size, bytes_accessed=8 * total.size, transcendentals=0),
    )(where, total, pooled, *o_slots)


def ring_step(step, ahead, back):
    if step == 4:
        half = ahead.shape[2] // 2
        ahead, back = ahead[:, :, :half], back[:, :, half:]
    return [move(ahead, dz=1), move(back, dz=-1)]


def ring_steps(arrived, steps):
    for step in steps:
        arrived = arrived + ring_step(step, *(arrived[-2:] if step > 1 else arrived * 2))
    return arrived


def body(stream, query, short_key, short_value, short_out):
    stream_rows, query_rows = stream[0], query[0]
    rows = stream_rows.shape[0]
    seq = lax.axis_index("seq")
    y, z, xl = seq // (NZ * NX), seq // NX % NZ, seq % NX
    where = jnp.stack([y, z, xl]).astype(jnp.int32)
    part = GROUP * HEAD

    pieces = pack(where, short_key[0], short_value[0])
    own = [pieces[0]] + [move(pieces[d], dy=d) for d in range(1, NY)]
    other = [move(pieces[d], dy=d, dx=1) for d in range(NY)]
    block = jnp.concatenate([jnp.stack(own), jnp.stack(other)], axis=2)

    query_late = after(query_rows, block)
    q_slots = [
        move(lax.dynamic_slice_in_dim(query_late, (y + d) % NY * part, part, 1), dy=d)
        for d in range(1, NY)
    ]
    mirrored = section_shift(after(stream_rows, block), 2)

    def attended(phase, arrivals):
        results = attend(where, query_rows, q_slots, arrivals, *PHASES[phase])
        return results[0], [results[0]] + [move(results[d], dy=-d) for d in range(1, NY)]

    rim = lax.ppermute(
        after(stream_rows[rows - 8 :], block), "seq", [(i, i + 1) for i in range(NY * NZ * NX - 1)]
    )
    both = ring_steps([block], [1, 2])
    ends = [after(v, rim) for v in both[-2:]]
    a, b = [[v[..., first * HEAD : (first + heads) * HEAD] for v in ends] for first, heads in PHASES]
    a = both + ring_steps(a, [3, 4])[2:]
    b = both + ring_steps(b, [3])[2:]
    done, a_slots = attended(0, a)
    b = ring_steps([*b[:-2], *[after(v, done) for v in b[-2:]]], [4])
    pooled = pool(after(rim, done), stream_rows)
    done, b_slots = attended(1, [after(b[0], mirrored), *b[1:]])
    o_slots = a_slots + b_slots
    bottleneck = section_shift(after(pooled, done), 1)
    total = base(after(mirrored, done), short_out[0])
    output, bottleneck = finish(where, total, bottleneck, o_slots)
    return (output[None], bottleneck[None])


def solution(mesh):
    spec = P("section", "seq", None)
    return jax.shard_map(
        body, mesh=mesh, in_specs=(spec,) * 5, out_specs=(spec, spec), check_vma=False
    )
```

profile of v0, /device:TPU:2, one launch (start us, length us, event | category | flops | bytes accessed | tf_op | source)
XLA Modules:
  0.0 125.6 jit_solution(17222504764852837300)
XLA Ops:
  0.7 0.1 pad_add_fusion.where_ref
  0.8 1.0 copy-done.7
  1.8 0.9 copy-done.8
  2.7 0.6 shard_map.68
  3.3 3.1 %collective-permute-start.6 = (bf16[2,32,640]{2,1,0:T(8,128)(2,1)S(1)}, bf16[2,32,640]{2,1,0:T(8,128)(2,1)S(1)}, u32[]{:S(2)}, u32[]{:S(2)}) collective-permute-start(bf16[2,32,640]{2,1,0:T(8,128)(2,1)S(1)} %get-tuple-element.30), channel_id=1, source_target_pairs={{0,49},{1,48},{2,51},{3,50},{4,53},{5,52},{6,55},{7,54},{8,57},{9,... | collective-permute-start | bytes 245768 | tf_op jit(solution)/shard_map/ppermute | solution.py:31
  6.3 1.6 %collective-permute-start.5 = (bf16[2,32,640]{2,1,0:T(8,128)(2,1)S(1)}, bf16[2,32,640]{2,1,0:T(8,128)(2,1)S(1)}, u32[]{:S(2)}, u32[]{:S(2)}) collective-permute-start(bf16[2,32,640]{2,1,0:T(8,128)(2,1)S(1)} %get-tuple-element.29), channel_id=1, source_target_pairs={{0,33},{1,32},{2,35},{3,34},{4,37},{5,36},{6,39},{7,38},{8,41},{9,... | collective-permute-start | bytes 245768 | tf_op jit(solution)/shard_map/ppermute | solution.py:31
  7.9 1.1 collective-permute-start.2
  8.9 0.9 collective-permute-start.4
  9.9 1.5 %collective-permute-start.3 = (bf16[2,32,640]{2,1,0:T(8,128)(2,1)S(1)}, bf16[2,32,640]{2,1,0:T(8,128)(2,1)S(1)}, u32[]{:S(2)}, u32[]{:S(2)}) collective-permute-start(bf16[2,32,640]{2,1,0:T(8,128)(2,1)S(1)} %get-tuple-element.27), channel_id=1, source_target_pairs={{0,1},{1,0},{2,3},{3,2},{4,5},{5,4},{6,7},{7,6},{8,9},{9,8},{10,11... | collective-permute-start | bytes 245768 | tf_op jit(solution)/shard_map/ppermute | solution.py:31
  11.4 2.9 %collective-permute-start.1 = (bf16[2,32,640]{2,1,0:T(8,128)(2,1)S(1)}, bf16[2,32,640]{2,1,0:T(8,128)(2,1)S(1)}, u32[]{:S(2)}, u32[]{:S(2)}) collective-permute-start(bf16[2,32,640]{2,1,0:T(8,128)(2,1)S(1)} %get-tuple-element.29), channel_id=1, source_target_pairs={{0,32},{1,33},{2,34},{3,35},{4,36},{5,37},{6,38},{7,39},{8,40},{9,... | collective-permute-start | bytes 245768 | tf_op jit(solution)/shard_map/ppermute | solution.py:31
  14.3 0.6 collective-permute-start
  14.9 1.0 collective-permute-done.4
  15.9 0.0 collective-permute-done.3
  15.9 0.0 collective-permute-done.2
  15.9 2.1 %collective-permute-done.1 = bf16[2,32,640]{2,1,0:T(8,128)(2,1)S(1)} collective-permute-done((bf16[2,32,640]{2,1,0:T(8,128)(2,1)S(1)}, bf16[2,32,640]{2,1,0:T(8,128)(2,1)S(1)}, u32[]{:S(2)}, u32[]{:S(2)}) %collective-permute-start.1) | collective-permute-done | bytes 81952 | tf_op jit(solution)/shard_map/ppermute | solution.py:31
  18.0 1.9 %collective-permute-done = bf16[2,32,640]{2,1,0:T(8,128)(2,1)S(1)} collective-permute-done((bf16[2,32,640]{2,1,0:T(8,128)(2,1)S(1)}, bf16[2,32,640]{2,1,0:T(8,128)(2,1)S(1)}, u32[]{:S(2)}, u32[]{:S(2)}) %collective-permute-start) | collective-permute-done | bytes 81952 | tf_op jit(solution)/shard_map/ppermute | solution.py:31
  19.9 0.1 maximum_maximum_fusion.refs_4_
  20.0 2.0 %collective-permute-start.11 = (bf16[4,2,64,640]{3,2,1,0:T(8,128)(2,1)S(1)}, bf16[4,2,64,640]{3,2,1,0:T(8,128)(2,1)S(1)}, u32[]{:S(2)}, u32[]{:S(2)}) collective-permute-start(bf16[4,2,64,640]{3,2,1,0:T(8,128)(2,1)S(1)} %maximum_maximum_fusion.refs_4_), channel_id=1, source_target_pairs={{0,2},{1,3},{2,4},{3,5},{4,6},{5,7},{6,8},{7,9},{8,10},{9,11},{10,... | collective-permute-start | bytes 1966088 | tf_op jit(solution)/shard_map/ppermute | solution.py:31
  22.0 4.0 %collective-permute-start.12 = (bf16[4,2,64,640]{3,2,1,0:T(8,128)(2,1)S(1)}, bf16[4,2,64,640]{3,2,1,0:T(8,128)(2,1)}, u32[]{:S(2)}, u32[]{:S(2)}) collective-permute-start(bf16[4,2,64,640]{3,2,1,0:T(8,128)(2,1)S(1)} %maximum_maximum_fusion.refs_4_), channel_id=1, source_target_pairs={{0,14},{1,15},{2,0},{3,1},{4,2},{5,3},{6,4},{7,5},{8,6},{9,7},{10,... | collective-permute-start | bytes 1966088 | tf_op jit(solution)/shard_map/ppermute | solution.py:31
  26.0 0.8 copy-done.2
  26.9 2.2 %collective-permute-start.7 = (bf16[288,2560]{1,0:T(8,128)(2,1)S(1)}, bf16[288,2560]{1,0:T(8,128)(2,1)S(1)}, u32[]{:S(2)}, u32[]{:S(2)}) collective-permute-start(bf16[288,2560]{1,0:T(8,128)(2,1)S(1)} %bitcast.20), channel_id=1, source_target_pairs={{0,128},{64,192},{128,0},{192,64},{1,129},{65,193},{129,1},{193,65... | collective-permute-start | bytes 4423688 | tf_op jit(solution)/shard_map/ppermute | solution.py:36
  29.0 9.8 %collective-permute-done.11.refs_5_ = bf16[4,2,64,640]{3,2,1,0:T(8,128)(2,1)S(1)} collective-permute-done((bf16[4,2,64,640]{3,2,1,0:T(8,128)(2,1)S(1)}, bf16[4,2,64,640]{3,2,1,0:T(8,128)(2,1)S(1)}, u32[]{:S(2)}, u32[]{:S(2)}) %collective-permute-start.11) | collective-permute-done | bytes 655392 | tf_op jit(solution)/shard_map/ppermute | solution.py:31
  38.9 0.8 copy-done.9
  39.7 0.0 collective-permute-done.12.refs_6_
  39.7 3.2 %collective-permute-start.14 = (bf16[4,2,64,640]{3,2,1,0:T(8,128)(2,1)}, bf16[4,2,64,640]{3,2,1,0:T(8,128)(2,1)}, u32[]{:S(2)}, u32[]{:S(2)}) collective-permute-start(bf16[4,2,64,640]{3,2,1,0:T(8,128)(2,1)} %collective-permute-done.12.refs_6_), channel_id=1, source_target_pairs={{0,14},{1,15},{2,0},{3,1},{4,2},{5,3},{6,4},{7,5},{8,6},{9,7},{10,... | collective-permute-start | bytes 1966088 | tf_op jit(solution)/shard_map/ppermute | solution.py:31
  43.0 1.9 %collective-permute-start.15 = (bf16[8,2560]{1,0:T(8,128)(2,1)S(1)}, bf16[8,2560]{1,0:T(8,128)(2,1)S(1)}, u32[]{:S(2)}, u32[]{:S(2)}) collective-permute-start(bf16[8,2560]{1,0:T(8,128)(2,1)S(1)} %slice_bitcast_fusion), channel_id=1, source_target_pairs={{0,1},{1,2},{2,3},{3,4},{4,5},{5,6},{6,7},{7,8},{8,9},{9,10},{10,1... | collective-permute-start | bytes 122888 | tf_op jit(solution)/shard_map/ppermute | solution.py:259
  44.9 16.2 %collective-permute-done.15.rim_ref = bf16[8,2560]{1,0:T(8,128)(2,1)S(1)} collective-permute-done((bf16[8,2560]{1,0:T(8,128)(2,1)S(1)}, bf16[8,2560]{1,0:T(8,128)(2,1)S(1)}, u32[]{:S(2)}, u32[]{:S(2)}) %collective-permute-start.15) | collective-permute-done | bytes 40992 | tf_op jit(solution)/shard_map/ppermute | solution.py:259
  61.1 0.0 collective-permute-done.13.refs_7_
  61.1 0.8 copy-done.4
  61.9 0.8 slice.33
  62.7 0.0 collective-permute-start.17
  62.7 0.0 collective-permute-done.14.refs_8_
  62.7 1.0 slice.34
  63.8 3.3 %collective-permute-start.18 = (bf16[4,2,64,384]{3,2,1,0:T(8,128)(2,1)S(1)}, bf16[4,2,64,384]{3,2,1,0:T(8,128)(2,1)S(1)}, u32[]{:S(2)}, u32[]{:S(2)}) collective-permute-start(bf16[4,2,64,384]{3,2,1,0:T(8,128)(2,1)S(1)} %slice.34), channel_id=1, source_target_pairs={{0,14},{1,15},{2,0},{3,1},{4,2},{5,3},{6,4},{7,5},{8,6},{9,7},{10,... | collective-permute-start | bytes 1179656 | tf_op jit(solution)/shard_map/ppermute | solution.py:31
  67.1 1.4 %constant_dynamic-slice_fusion = (bf16[288,640]{1,0:T(8,128)(2,1)S(1)}, bf16[288,640]{1,0:T(8,128)(2,1)S(1)}, bf16[288,640]{1,0:T(8,128)(2,1)S(1)}) fusion(bf16[288,2560]{1,0:T(8,128)(2,1)} %bitcast.22, s32[]{:T(128)S(6)} %select_n.48, s32[]{:T(128)S(6)} %select_n.46, s32[]{:T(128)S(6)} %select_n.44), kind=kLoop, calls=%fused_computation.2 | loop fusion | bytes 2211852 | tf_op jit(solution)/shard_map/dynamic_slice | solution.py:250
  68.5 0.0 copy-start.1
  68.5 0.1 collective-permute-start.8
  68.6 2.0 %collective-permute-start.9 = (bf16[288,640]{1,0:T(8,128)(2,1)S(1)}, bf16[288,640]{1,0:T(8,128)(2,1)S(1)}, u32[]{:S(2)}, u32[]{:S(2)}) collective-permute-start(bf16[288,640]{1,0:T(8,128)(2,1)S(1)} %get-tuple-element.53), channel_id=1, source_target_pairs={{0,32},{1,33},{2,34},{3,35},{4,36},{5,37},{6,38},{7,39},{8,40},{9,... | collective-permute-start | bytes 1105928 | tf_op jit(solution)/shard_map/ppermute | solution.py:31
  70.7 1.3 %collective-permute-done.17.refs_9_ = bf16[4,2,64,384]{3,2,1,0:T(8,128)(2,1)S(1)} collective-permute-done((bf16[4,2,64,384]{3,2,1,0:T(8,128)(2,1)}, bf16[4,2,64,384]{3,2,1,0:T(8,128)(2,1)S(1)}, u32[]{:S(2)}, u32[]{:S(2)}) %collective-permute-start.17) | collective-permute-done | bytes 393248 | tf_op jit(solution)/shard_map/ppermute | solution.py:31
  71.9 1.1 collective-permute-start.10
  73.1 0.1 collective-permute-start.19
  73.2 11.1 %collective-permute-done.8.refs_1_ = bf16[288,640]{1,0:T(8,128)(2,1)S(1)} collective-permute-done((bf16[288,640]{1,0:T(8,128)(2,1)S(1)}, bf16[288,640]{1,0:T(8,128)(2,1)S(1)}, u32[]{:S(2)}, u32[]{:S(2)}) %collective-permute-start.8) | collective-permute-done | bytes 368672 | tf_op jit(solution)/shard_map/ppermute | solution.py:31
  84.3 0.3 collective-permute-start.20
  84.7 1.0 slice.37
  85.7 1.8 %collective-permute-start.16 = (bf16[4,2,64,256]{3,2,1,0:T(8,128)(2,1)S(1)}, bf16[4,2,64,256]{3,2,1,0:T(8,128)(2,1)S(1)}, u32[]{:S(2)}, u32[]{:S(2)}) collective-permute-start(bf16[4,2,64,256]{3,2,1,0:T(8,128)(2,1)S(1)} %slice.32), channel_id=1, source_target_pairs={{0,2},{1,3},{2,4},{3,5},{4,6},{5,7},{6,8},{7,9},{8,10},{9,11},{10,... | collective-permute-start | bytes 786440 | tf_op jit(solution)/shard_map/ppermute | solution.py:31
  87.4 1.5 %collective-permute-start.21 = (bf16[4,2,64,256]{3,2,1,0:T(8,128)(2,1)S(1)}, bf16[4,2,64,256]{3,2,1,0:T(8,128)(2,1)S(1)}, u32[]{:S(2)}, u32[]{:S(2)}) collective-permute-start(bf16[4,2,64,256]{3,2,1,0:T(8,128)(2,1)S(1)} %slice.37), channel_id=1, source_target_pairs={{0,14},{1,15},{2,0},{3,1},{4,2},{5,3},{6,4},{7,5},{8,6},{9,7},{10,... | collective-permute-start | bytes 786440 | tf_op jit(solution)/shard_map/ppermute | solution.py:31
  89.0 1.0 collective-permute-done.20.refs_12_
  90.0 8.1 %shard_map.69 = (bf16[288,384]{1,0:T(8,128)(2,1)S(1)}, bf16[288,384]{1,0:T(8,128)(2,1)S(1)}, bf16[288,384]{1,0:T(8,128)(2,1)S(1)}, bf16[288,384]{1,0:T(8,128)(2,1)S(1)}) custom-call(s32[3]{0:T(128)S(1)} %pad_add_fusion.where_ref, bf16[288,2560]{1,0:T(8,128)(2,1)S(1)} %bitcast.23, bf16[288,640]{1,0:T(8,128)(2,1)S(1)} %collective-permute-done.8.refs_1_, ...), custom_call_target="tpu_custom_call" | custom-call | flops 3397386240 | bytes 3145728 | tf_op jit(solution)/shard_map/pallas_call | solution.py:147
  98.2 0.1 collective-permute-start.22
  98.3 3.3 %collective-permute-start.23 = (bf16[4,2,32,256]{3,2,1,0:T(8,128)(2,1)S(1)}, bf16[4,2,32,256]{3,2,1,0:T(8,128)(2,1)S(1)}, u32[]{:S(2)}, u32[]{:S(2)}) collective-permute-start(bf16[4,2,32,256]{3,2,1,0:T(8,128)(2,1)S(1)} %slice.39), channel_id=1, source_target_pairs={{0,14},{1,15},{2,0},{3,1},{4,2},{5,3},{6,4},{7,5},{8,6},{9,7},{10,... | collective-permute-start | bytes 393224 | tf_op jit(solution)/shard_map/ppermute | solution.py:31
  101.6 0.9 collective-permute-start.25
  102.4 1.2 collective-permute-start.27
  103.6 0.4 shard_map.72
  104.0 0.4 collective-permute-done.22.refs_11_
  104.4 5.9 %shard_map.70 = (bf16[288,256]{1,0:T(8,128)(2,1)S(1)}, bf16[288,256]{1,0:T(8,128)(2,1)S(1)}, bf16[288,256]{1,0:T(8,128)(2,1)S(1)}, bf16[288,256]{1,0:T(8,128)(2,1)S(1)}) custom-call(s32[3]{0:T(128)S(1)} %pad_add_fusion.where_ref, bf16[288,2560]{1,0:T(8,128)(2,1)S(1)} %bitcast.24, bf16[288,640]{1,0:T(8,128)(2,1)S(1)} %collective-permute-done.8.refs_1_, ...), custom_call_target="tpu_custom_call" | custom-call | flops 2264924160 | bytes 2097152 | tf_op jit(solution)/shard_map/pallas_call | solution.py:147
  110.3 0.1 collective-permute-start.24
  110.4 2.5 %collective-permute-start.28 = (bf16[288,256]{1,0:T(8,128)(2,1)S(1)}, bf16[288,256]{1,0:T(8,128)(2,1)S(1)}, u32[]{:S(2)}, u32[]{:S(2)}) collective-permute-start(bf16[288,256]{1,0:T(8,128)(2,1)S(1)} %get-tuple-element.47), channel_id=1, source_target_pairs={{0,48},{1,49},{2,50},{3,51},{4,52},{5,53},{6,54},{7,55},{8,56},{9,... | collective-permute-start | bytes 442376 | tf_op jit(solution)/shard_map/ppermute | solution.py:31
  112.9 1.7 %collective-permute-start.29 = (bf16[288,256]{1,0:T(8,128)(2,1)S(1)}, bf16[288,256]{1,0:T(8,128)(2,1)S(1)}, u32[]{:S(2)}, u32[]{:S(2)}) collective-permute-start(bf16[288,256]{1,0:T(8,128)(2,1)S(1)} %get-tuple-element.48), channel_id=1, source_target_pairs={{0,32},{1,33},{2,34},{3,35},{4,36},{5,37},{6,38},{7,39},{8,40},{9,... | collective-permute-start | bytes 442376 | tf_op jit(solution)/shard_map/ppermute | solution.py:31
  114.6 1.1 collective-permute-start.30
  115.7 0.5 shard_map.71.base_ref
  116.3 3.7 %collective-permute-done.28.refs_5_ = bf16[288,256]{1,0:T(8,128)(2,1)S(1)} collective-permute-done((bf16[288,256]{1,0:T(8,128)(2,1)S(1)}, bf16[288,256]{1,0:T(8,128)(2,1)S(1)}, u32[]{:S(2)}, u32[]{:S(2)}) %collective-permute-start.28) | collective-permute-done | bytes 147488 | tf_op jit(solution)/shard_map/ppermute | solution.py:31
  120.0 1.1 collective-permute-done.29.refs_6_
  121.1 2.6 %collective-permute-done.30.refs_7_ = bf16[288,256]{1,0:T(8,128)(2,1)S(1)} collective-permute-done((bf16[288,256]{1,0:T(8,128)(2,1)S(1)}, bf16[288,256]{1,0:T(8,128)(2,1)S(1)}, u32[]{:S(2)}, u32[]{:S(2)}) %collective-permute-start.30) | collective-permute-done | bytes 147488 | tf_op jit(solution)/shard_map/ppermute | solution.py:31
  123.7 1.8 %shard_map.73 = (bf16[288,2560]{1,0:T(8,128)(2,1)}, bf16[32,2560]{1,0:T(8,128)(2,1)}) custom-call(s32[3]{0:T(128)S(1)} %pad_add_fusion.where_ref, f32[288,2560]{1,0:T(8,128)S(1)} %shard_map.71.base_ref, bf16[32,2560]{1,0:T(8,128)(2,1)S(1)} %collective-permute-done.24.pooled_ref, bf16[288,384]{1,0:T(8,128)(2,1)S(1)} %get-tuple-element.37.refs_0_, ...), custom_call_target="tpu_custom_call" | custom-call | flops 737280 | bytes 5898240 | tf_op jit(solution)/shard_map/pallas_call | solution.py:208
  (38 shorter events, 0.2 us)
Async XLA Ops:
  0.6 26.2 %copy-start = (bf16[1,288,2560]{2,1,0:T(8,128)(2,1)S(1)}, bf16[1,288,2560]{2,1,0:T(8,128)(2,1)}, u32[]{:S(2)}) copy-start(bf16[1,288,2560]{2,1,0:T(8,128)(2,1)} %param.5) | copy-start | bytes 4423684
  0.8 1.0 copy-start.7
  1.8 0.9 copy-start.8
  3.3 8.1 %collective-permute-start.6 = (bf16[2,32,640]{2,1,0:T(8,128)(2,1)S(1)}, bf16[2,32,640]{2,1,0:T(8,128)(2,1)S(1)}, u32[]{:S(2)}, u32[]{:S(2)}) collective-permute-start(bf16[2,32,640]{2,1,0:T(8,128)(2,1)S(1)} %get-tuple-element.30), channel_id=1, source_target_pairs={{0,49},{1,48},{2,51},{3,50},{4,53},{5,52},{6,55},{7,54},{8,57},{9,... | collective-permute-start | bytes 245768 | tf_op jit(solution)/shard_map/ppermute | solution.py:31
  6.3 8.0 %collective-permute-start.5 = (bf16[2,32,640]{2,1,0:T(8,128)(2,1)S(1)}, bf16[2,32,640]{2,1,0:T(8,128)(2,1)S(1)}, u32[]{:S(2)}, u32[]{:S(2)}) collective-permute-start(bf16[2,32,640]{2,1,0:T(8,128)(2,1)S(1)} %get-tuple-element.29), channel_id=1, source_target_pairs={{0,33},{1,32},{2,35},{3,34},{4,37},{5,36},{6,39},{7,38},{8,41},{9,... | collective-permute-start | bytes 245768 | tf_op jit(solution)/shard_map/ppermute | solution.py:31
  7.9 8.0 %collective-permute-start.2 = (bf16[2,32,640]{2,1,0:T(8,128)(2,1)S(1)}, bf16[2,32,640]{2,1,0:T(8,128)(2,1)S(1)}, u32[]{:S(2)}, u32[]{:S(2)}) collective-permute-start(bf16[2,32,640]{2,1,0:T(8,128)(2,1)S(1)} %get-tuple-element.30), channel_id=1, source_target_pairs={{0,48},{1,49},{2,50},{3,51},{4,52},{5,53},{6,54},{7,55},{8,56},{9,... | collective-permute-start | bytes 245768 | tf_op jit(solution)/shard_map/ppermute | solution.py:31
  8.9 7.0 %collective-permute-start.4 = (bf16[2,32,640]{2,1,0:T(8,128)(2,1)S(1)}, bf16[2,32,640]{2,1,0:T(8,128)(2,1)S(1)}, u32[]{:S(2)}, u32[]{:S(2)}) collective-permute-start(bf16[2,32,640]{2,1,0:T(8,128)(2,1)S(1)} %get-tuple-element.28), channel_id=1, source_target_pairs={{0,17},{1,16},{2,19},{3,18},{4,21},{5,20},{6,23},{7,22},{8,25},{9,... | collective-permute-start | bytes 245768 | tf_op jit(solution)/shard_map/ppermute | solution.py:31
  9.9 6.0 %collective-permute-start.3 = (bf16[2,32,640]{2,1,0:T(8,128)(2,1)S(1)}, bf16[2,32,640]{2,1,0:T(8,128)(2,1)S(1)}, u32[]{:S(2)}, u32[]{:S(2)}) collective-permute-start(bf16[2,32,640]{2,1,0:T(8,128)(2,1)S(1)} %get-tuple-element.27), channel_id=1, source_target_pairs={{0,1},{1,0},{2,3},{3,2},{4,5},{5,4},{6,7},{7,6},{8,9},{9,8},{10,11... | collective-permute-start | bytes 245768 | tf_op jit(solution)/shard_map/ppermute | solution.py:31
  11.4 6.6 %collective-permute-start.1 = (bf16[2,32,640]{2,1,0:T(8,128)(2,1)S(1)}, bf16[2,32,640]{2,1,0:T(8,128)(2,1)S(1)}, u32[]{:S(2)}, u32[]{:S(2)}) collective-permute-start(bf16[2,32,640]{2,1,0:T(8,128)(2,1)S(1)} %get-tuple-element.29), channel_id=1, source_target_pairs={{0,32},{1,33},{2,34},{3,35},{4,36},{5,37},{6,38},{7,39},{8,40},{9,... | collective-permute-start | bytes 245768 | tf_op jit(solution)/shard_map/ppermute | solution.py:31
  14.3 5.7 %collective-permute-start = (bf16[2,32,640]{2,1,0:T(8,128)(2,1)S(1)}, bf16[2,32,640]{2,1,0:T(8,128)(2,1)S(1)}, u32[]{:S(2)}, u32[]{:S(2)}) collective-permute-start(bf16[2,32,640]{2,1,0:T(8,128)(2,1)S(1)} %get-tuple-element.28), channel_id=1, source_target_pairs={{0,16},{1,17},{2,18},{3,19},{4,20},{5,21},{6,22},{7,23},{8,24},{9,... | collective-permute-start | bytes 245768 | tf_op jit(solution)/shard_map/ppermute | solution.py:31
  20.0 18.9 %collective-permute-start.11 = (bf16[4,2,64,640]{3,2,1,0:T(8,128)(2,1)S(1)}, bf16[4,2,64,640]{3,2,1,0:T(8,128)(2,1)S(1)}, u32[]{:S(2)}, u32[]{:S(2)}) collective-permute-start(bf16[4,2,64,640]{3,2,1,0:T(8,128)(2,1)S(1)} %maximum_maximum_fusion.refs_4_), channel_id=1, source_target_pairs={{0,2},{1,3},{2,4},{3,5},{4,6},{5,7},{6,8},{7,9},{8,10},{9,11},{10,... | collective-permute-start | bytes 1966088 | tf_op jit(solution)/shard_map/ppermute | solution.py:31
  22.0 17.7 %collective-permute-start.12 = (bf16[4,2,64,640]{3,2,1,0:T(8,128)(2,1)S(1)}, bf16[4,2,64,640]{3,2,1,0:T(8,128)(2,1)}, u32[]{:S(2)}, u32[]{:S(2)}) collective-permute-start(bf16[4,2,64,640]{3,2,1,0:T(8,128)(2,1)S(1)} %maximum_maximum_fusion.refs_4_), channel_id=1, source_target_pairs={{0,14},{1,15},{2,0},{3,1},{4,2},{5,3},{6,4},{7,5},{8,6},{9,7},{10,... | collective-permute-start | bytes 1966088 | tf_op jit(solution)/shard_map/ppermute | solution.py:31
  26.0 0.8 copy-start.2
  26.9 74.7 %collective-permute-start.7 = (bf16[288,2560]{1,0:T(8,128)(2,1)S(1)}, bf16[288,2560]{1,0:T(8,128)(2,1)S(1)}, u32[]{:S(2)}, u32[]{:S(2)}) collective-permute-start(bf16[288,2560]{1,0:T(8,128)(2,1)S(1)} %bitcast.20), channel_id=1, source_target_pairs={{0,128},{64,192},{128,0},{192,64},{1,129},{65,193},{129,1},{193,65... | collective-permute-start | bytes 4423688 | tf_op jit(solution)/shard_map/ppermute | solution.py:36
  38.9 22.2 %collective-permute-start.13 = (bf16[4,2,64,640]{3,2,1,0:T(8,128)(2,1)S(1)}, bf16[4,2,64,640]{3,2,1,0:T(8,128)(2,1)S(1)}, u32[]{:S(2)}, u32[]{:S(2)}) collective-permute-start(bf16[4,2,64,640]{3,2,1,0:T(8,128)(2,1)S(1)} %collective-permute-done.11.refs_5_), channel_id=1, source_target_pairs={{0,2},{1,3},{2,4},{3,5},{4,6},{5,7},{6,8},{7,9},{8,10},{9,11},{10,... | collective-permute-start | bytes 1966088 | tf_op jit(solution)/shard_map/ppermute | solution.py:31
  38.9 0.8 copy-start.9
  39.7 23.0 %collective-permute-start.14 = (bf16[4,2,64,640]{3,2,1,0:T(8,128)(2,1)}, bf16[4,2,64,640]{3,2,1,0:T(8,128)(2,1)}, u32[]{:S(2)}, u32[]{:S(2)}) collective-permute-start(bf16[4,2,64,640]{3,2,1,0:T(8,128)(2,1)} %collective-permute-done.12.refs_6_), channel_id=1, source_target_pairs={{0,14},{1,15},{2,0},{3,1},{4,2},{5,3},{6,4},{7,5},{8,6},{9,7},{10,... | collective-permute-start | bytes 1966088 | tf_op jit(solution)/shard_map/ppermute | solution.py:31
  43.0 18.1 %collective-permute-start.15 = (bf16[8,2560]{1,0:T(8,128)(2,1)S(1)}, bf16[8,2560]{1,0:T(8,128)(2,1)S(1)}, u32[]{:S(2)}, u32[]{:S(2)}) collective-permute-start(bf16[8,2560]{1,0:T(8,128)(2,1)S(1)} %slice_bitcast_fusion), channel_id=1, source_target_pairs={{0,1},{1,2},{2,3},{3,4},{4,5},{5,6},{6,7},{7,8},{8,9},{9,10},{10,1... | collective-permute-start | bytes 122888 | tf_op jit(solution)/shard_map/ppermute | solution.py:259
  61.1 0.8 copy-start.4
  62.7 9.2 %collective-permute-start.17 = (bf16[4,2,64,384]{3,2,1,0:T(8,128)(2,1)}, bf16[4,2,64,384]{3,2,1,0:T(8,128)(2,1)S(1)}, u32[]{:S(2)}, u32[]{:S(2)}) collective-permute-start(bf16[4,2,64,384]{3,2,1,0:T(8,128)(2,1)} %slice.33), channel_id=1, source_target_pairs={{0,2},{1,3},{2,4},{3,5},{4,6},{5,7},{6,8},{7,9},{8,10},{9,11},{10,... | collective-permute-start | bytes 1179656 | tf_op jit(solution)/shard_map/ppermute | solution.py:31
  63.8 20.9 %copy-start.5 = (bf16[4,2,64,640]{3,2,1,0:T(8,128)(2,1)S(1)}, bf16[4,2,64,640]{3,2,1,0:T(8,128)(2,1)}, u32[]{:S(2)}) copy-start(bf16[4,2,64,640]{3,2,1,0:T(8,128)(2,1)} %copy-done.4) | copy-start | bytes 1966084
  63.8 9.3 %collective-permute-start.18 = (bf16[4,2,64,384]{3,2,1,0:T(8,128)(2,1)S(1)}, bf16[4,2,64,384]{3,2,1,0:T(8,128)(2,1)S(1)}, u32[]{:S(2)}, u32[]{:S(2)}) collective-permute-start(bf16[4,2,64,384]{3,2,1,0:T(8,128)(2,1)S(1)} %slice.34), channel_id=1, source_target_pairs={{0,14},{1,15},{2,0},{3,1},{4,2},{5,3},{6,4},{7,5},{8,6},{9,7},{10,... | collective-permute-start | bytes 1179656 | tf_op jit(solution)/shard_map/ppermute | solution.py:31
  67.1 22.9 %copy-start.3 = (bf16[4,2,64,640]{3,2,1,0:T(8,128)(2,1)S(1)}, bf16[4,2,64,640]{3,2,1,0:T(8,128)(2,1)}, u32[]{:S(2)}) copy-start(bf16[4,2,64,640]{3,2,1,0:T(8,128)(2,1)} %copy-done.2) | copy-start | bytes 1966084
  67.1 22.9 %copy-start.10 = (bf16[4,2,64,640]{3,2,1,0:T(8,128)(2,1)S(1)}, bf16[4,2,64,640]{3,2,1,0:T(8,128)(2,1)}, u32[]{:S(2)}) copy-start(bf16[4,2,64,640]{3,2,1,0:T(8,128)(2,1)} %copy-done.9) | copy-start | bytes 1966084
  68.5 21.5 %copy-start.1 = (bf16[1,288,2560]{2,1,0:T(8,128)(2,1)S(1)}, bf16[1,288,2560]{2,1,0:T(8,128)(2,1)}, u32[]{:S(2)}) copy-start(bf16[1,288,2560]{2,1,0:T(8,128)(2,1)} %param.6) | copy-start | bytes 4423684
  68.5 15.8 %collective-permute-start.8 = (bf16[288,640]{1,0:T(8,128)(2,1)S(1)}, bf16[288,640]{1,0:T(8,128)(2,1)S(1)}, u32[]{:S(2)}, u32[]{:S(2)}) collective-permute-start(bf16[288,640]{1,0:T(8,128)(2,1)S(1)} %get-tuple-element.54), channel_id=1, source_target_pairs={{0,16},{1,17},{2,18},{3,19},{4,20},{5,21},{6,22},{7,23},{8,24},{9,... | collective-permute-start | bytes 1105928 | tf_op jit(solution)/shard_map/ppermute | solution.py:31
  68.6 17.0 %collective-permute-start.9 = (bf16[288,640]{1,0:T(8,128)(2,1)S(1)}, bf16[288,640]{1,0:T(8,128)(2,1)S(1)}, u32[]{:S(2)}, u32[]{:S(2)}) collective-permute-start(bf16[288,640]{1,0:T(8,128)(2,1)S(1)} %get-tuple-element.53), channel_id=1, source_target_pairs={{0,32},{1,33},{2,34},{3,35},{4,36},{5,37},{6,38},{7,39},{8,40},{9,... | collective-permute-start | bytes 1105928 | tf_op jit(solution)/shard_map/ppermute | solution.py:31
  71.9 15.5 %collective-permute-start.10 = (bf16[288,640]{1,0:T(8,128)(2,1)S(1)}, bf16[288,640]{1,0:T(8,128)(2,1)S(1)}, u32[]{:S(2)}, u32[]{:S(2)}) collective-permute-start(bf16[288,640]{1,0:T(8,128)(2,1)S(1)} %get-tuple-element.52), channel_id=1, source_target_pairs={{0,48},{1,49},{2,50},{3,51},{4,52},{5,53},{6,54},{7,55},{8,56},{9,... | collective-permute-start | bytes 1105928 | tf_op jit(solution)/shard_map/ppermute | solution.py:31
  73.1 15.9 %collective-permute-start.19 = (bf16[4,2,32,384]{3,2,1,0:T(8,128)(2,1)S(1)}, bf16[4,2,32,384]{3,2,1,0:T(8,128)(2,1)S(1)}, u32[]{:S(2)}, u32[]{:S(2)}) collective-permute-start(bf16[4,2,32,384]{3,2,1,0:T(8,128)(2,1)S(1)} %slice.40), channel_id=1, source_target_pairs={{0,2},{1,3},{2,4},{3,5},{4,6},{5,7},{6,8},{7,9},{8,10},{9,11},{10,... | collective-permute-start | bytes 589832 | tf_op jit(solution)/shard_map/ppermute | solution.py:31
  84.3 5.7 %collective-permute-start.20 = (bf16[4,2,32,384]{3,2,1,0:T(8,128)(2,1)S(1)}, bf16[4,2,32,384]{3,2,1,0:T(8,128)(2,1)S(1)}, u32[]{:S(2)}, u32[]{:S(2)}) collective-permute-start(bf16[4,2,32,384]{3,2,1,0:T(8,128)(2,1)S(1)} %slice.41), channel_id=1, source_target_pairs={{0,14},{1,15},{2,0},{3,1},{4,2},{5,3},{6,4},{7,5},{8,6},{9,7},{10,... | collective-permute-start | bytes 589832 | tf_op jit(solution)/shard_map/ppermute | solution.py:31
  85.7 12.5 %collective-permute-start.16 = (bf16[4,2,64,256]{3,2,1,0:T(8,128)(2,1)S(1)}, bf16[4,2,64,256]{3,2,1,0:T(8,128)(2,1)S(1)}, u32[]{:S(2)}, u32[]{:S(2)}) collective-permute-start(bf16[4,2,64,256]{3,2,1,0:T(8,128)(2,1)S(1)} %slice.32), channel_id=1, source_target_pairs={{0,2},{1,3},{2,4},{3,5},{4,6},{5,7},{6,8},{7,9},{8,10},{9,11},{10,... | collective-permute-start | bytes 786440 | tf_op jit(solution)/shard_map/ppermute | solution.py:31
  87.4 10.7 %collective-permute-start.21 = (bf16[4,2,64,256]{3,2,1,0:T(8,128)(2,1)S(1)}, bf16[4,2,64,256]{3,2,1,0:T(8,128)(2,1)S(1)}, u32[]{:S(2)}, u32[]{:S(2)}) collective-permute-start(bf16[4,2,64,256]{3,2,1,0:T(8,128)(2,1)S(1)} %slice.37), channel_id=1, source_target_pairs={{0,14},{1,15},{2,0},{3,1},{4,2},{5,3},{6,4},{7,5},{8,6},{9,7},{10,... | collective-permute-start | bytes 786440 | tf_op jit(solution)/shard_map/ppermute | solution.py:31
  98.2 6.3 %collective-permute-start.22 = (bf16[4,2,32,256]{3,2,1,0:T(8,128)(2,1)S(1)}, bf16[4,2,32,256]{3,2,1,0:T(8,128)(2,1)S(1)}, u32[]{:S(2)}, u32[]{:S(2)}) collective-permute-start(bf16[4,2,32,256]{3,2,1,0:T(8,128)(2,1)S(1)} %slice.38), channel_id=1, source_target_pairs={{0,2},{1,3},{2,4},{3,5},{4,6},{5,7},{6,8},{7,9},{8,10},{9,11},{10,... | collective-permute-start | bytes 393224 | tf_op jit(solution)/shard_map/ppermute | solution.py:31
  98.3 6.1 %collective-permute-start.23 = (bf16[4,2,32,256]{3,2,1,0:T(8,128)(2,1)S(1)}, bf16[4,2,32,256]{3,2,1,0:T(8,128)(2,1)S(1)}, u32[]{:S(2)}, u32[]{:S(2)}) collective-permute-start(bf16[4,2,32,256]{3,2,1,0:T(8,128)(2,1)S(1)} %slice.39), channel_id=1, source_target_pairs={{0,14},{1,15},{2,0},{3,1},{4,2},{5,3},{6,4},{7,5},{8,6},{9,7},{10,... | collective-permute-start | bytes 393224 | tf_op jit(solution)/shard_map/ppermute | solution.py:31
  101.6 11.3 %collective-permute-start.25 = (bf16[288,384]{1,0:T(8,128)(2,1)S(1)}, bf16[288,384]{1,0:T(8,128)(2,1)S(1)}, u32[]{:S(2)}, u32[]{:S(2)}) collective-permute-start(bf16[288,384]{1,0:T(8,128)(2,1)S(1)} %get-tuple-element.44), channel_id=1, source_target_pairs={{0,48},{1,49},{2,50},{3,51},{4,52},{5,53},{6,54},{7,55},{8,56},{9,... | collective-permute-start | bytes 663560 | tf_op jit(solution)/shard_map/ppermute | solution.py:31
  102.4 12.2 %collective-permute-start.26 = (bf16[288,384]{1,0:T(8,128)(2,1)S(1)}, bf16[288,384]{1,0:T(8,128)(2,1)S(1)}, u32[]{:S(2)}, u32[]{:S(2)}) collective-permute-start(bf16[288,384]{1,0:T(8,128)(2,1)S(1)} %get-tuple-element.45), channel_id=1, source_target_pairs={{0,32},{1,33},{2,34},{3,35},{4,36},{5,37},{6,38},{7,39},{8,40},{9,... | collective-permute-start | bytes 663560 | tf_op jit(solution)/shard_map/ppermute | solution.py:31
  102.4 13.8 %collective-permute-start.27 = (bf16[288,384]{1,0:T(8,128)(2,1)S(1)}, bf16[288,384]{1,0:T(8,128)(2,1)S(1)}, u32[]{:S(2)}, u32[]{:S(2)}) collective-permute-start(bf16[288,384]{1,0:T(8,128)(2,1)S(1)} %get-tuple-element.46), channel_id=1, source_target_pairs={{0,16},{1,17},{2,18},{3,19},{4,20},{5,21},{6,22},{7,23},{8,24},{9,... | collective-permute-start | bytes 663560 | tf_op jit(solution)/shard_map/ppermute | solution.py:31
  104.0 11.7 %copy-start.6 = (bf16[1,32,2560]{2,1,0:T(8,128)(2,1)S(1)}, bf16[1,32,2560]{2,1,0:T(8,128)(2,1)}, u32[]{:S(2)}) copy-start(bf16[1,32,2560]{2,1,0:T(8,128)(2,1)} %param.9) | copy-start | bytes 491524
  110.3 13.4 %collective-permute-start.24 = (bf16[32,2560]{1,0:T(8,128)(2,1)S(1)}, bf16[32,2560]{1,0:T(8,128)(2,1)S(1)}, u32[]{:S(2)}, u32[]{:S(2)}) collective-permute-start(bf16[32,2560]{1,0:T(8,128)(2,1)S(1)} %shard_map.72), channel_id=1, source_target_pairs={{0,64},{64,128},{128,192},{192,0},{1,65},{65,129},{129,193},{193,1... | collective-permute-start | bytes 491528 | tf_op jit(solution)/shard_map/ppermute | solution.py:36
  110.4 9.6 %collective-permute-start.28 = (bf16[288,256]{1,0:T(8,128)(2,1)S(1)}, bf16[288,256]{1,0:T(8,128)(2,1)S(1)}, u32[]{:S(2)}, u32[]{:S(2)}) collective-permute-start(bf16[288,256]{1,0:T(8,128)(2,1)S(1)} %get-tuple-element.47), channel_id=1, source_target_pairs={{0,48},{1,49},{2,50},{3,51},{4,52},{5,53},{6,54},{7,55},{8,56},{9,... | collective-permute-start | bytes 442376 | tf_op jit(solution)/shard_map/ppermute | solution.py:31
  112.9 8.2 %collective-permute-start.29 = (bf16[288,256]{1,0:T(8,128)(2,1)S(1)}, bf16[288,256]{1,0:T(8,128)(2,1)S(1)}, u32[]{:S(2)}, u32[]{:S(2)}) collective-permute-start(bf16[288,256]{1,0:T(8,128)(2,1)S(1)} %get-tuple-element.48), channel_id=1, source_target_pairs={{0,32},{1,33},{2,34},{3,35},{4,36},{5,37},{6,38},{7,39},{8,40},{9,... | collective-permute-start | bytes 442376 | tf_op jit(solution)/shard_map/ppermute | solution.py:31
  114.6 9.1 %collective-permute-start.30 = (bf16[288,256]{1,0:T(8,128)(2,1)S(1)}, bf16[288,256]{1,0:T(8,128)(2,1)S(1)}, u32[]{:S(2)}, u32[]{:S(2)}) collective-permute-start(bf16[288,256]{1,0:T(8,128)(2,1)S(1)} %get-tuple-element.49), channel_id=1, source_target_pairs={{0,16},{1,17},{2,18},{3,19},{4,20},{5,21},{6,22},{7,23},{8,24},{9,... | collective-permute-start | bytes 442376 | tf_op jit(solution)/shard_map/ppermute | solution.py:31
where the time goes:
time: 127 us; the launch traced here: 126 us
  waiting for transfers between devices  52.2 us (41%)
  starting transfers between devices  46.1 us (36%)
  Pallas kernels  17.3 us (14%)
  local copies, waits for them, and re-layouts  8.76 us (7%)
    ppermute x28, starting transfers between devices, move(): return lax.ppermute(block, 'seq', seq_pairs(dy, dz, dx))  41.9 us
    ppermute x28, waiting for transfers between devices, move(): return lax.ppermute(block, 'seq', seq_pairs(dy, dz, dx))  36 us
    ppermute x1, waiting for transfers between devices, body(): lax.ppermute(after(stream_rows[rows - 8:], block), 'seq', [(i, i + 1) for...  16.2 us
    pallas_call x2, Pallas kernels, attend(): pl.pallas_call(functools.partial(attend_kernel, len(arrivals), first), in...  14 us
    unnamed x22, local copies, waits for them, and re-layouts  4.47 us
    slice x4, local copies, waits for them, and re-layouts, body(): v[..., first * HEAD:(first + heads) * HEAD]  2.82 us
  transfers between devices with their start and end apart: 31, of which 12 were waited for; matrix products, arithmetic and copies ran while one was open for 3% of the time, Pallas kernels for 12%

commit v1 on v0

--- a/solution.py
+++ b/solution.py
@@ -14,7 +14,7 @@
 GROUP = HEADS // NY
 PHASES = ((0, 3), (3, 2))
 SCALE = math.log2(math.e) / math.sqrt(HEAD)
-VMEM = 20 * 1024 * 1024
+VMEM = 15 * 1024 * 1024
 
 
 def seq_pairs(dy, dz, dx):
@@ -36,6 +36,14 @@
     return lax.ppermute(block, "section", [(i, (i + by) % count) for i in range(count)])
 
 
+def next_rows(block):
+    sections, count = lax.axis_size("section"), lax.axis_size("seq")
+    pairs = [
+        (s * count + i, (s + 1) % sections * count + i + 1) for s in range(sections) for i in range(count - 1)
+    ]
+    return lax.ppermute(block, ("section", "seq"), pairs)
+
+
 def after(value, *others):
     return lax.optimization_barrier((value,) + others)[0]
 
@@ -61,18 +69,17 @@
     )(where, keys, values)
 
 
-def pool_kernel(rim_ref, rows_ref, out_ref):
+def pool_kernel(rows_ref, out_ref):
     count, rows = out_ref.shape[0], rows_ref.shape[0]
     j = lax.broadcasted_iota(jnp.int32, (count, rows), 0)
     r = lax.broadcasted_iota(jnp.int32, (count, rows), 1)
     inside = ((r <= 9 * j) & (r >= 9 * j - 8)).astype(jnp.bfloat16)
-    first = (lax.broadcasted_iota(jnp.int32, (count, 8), 0) == 0).astype(jnp.bfloat16)
     total = jnp.dot(inside, rows_ref[...], preferred_element_type=jnp.float32)
-    total += jnp.dot(first, rim_ref[...], preferred_element_type=jnp.float32)
-    out_ref[...] = (total / 9.0).astype(out_ref.dtype)
-
-
-def pool(rim, rows):
+    whole = lax.broadcasted_iota(jnp.int32, total.shape, 0) > 0
+    out_ref[...] = jnp.where(whole, total / 9.0, total).astype(out_ref.dtype)
+
+
+def pool(rows):
     count, width = rows.shape[0] // 9, rows.shape[1]
     return pl.pallas_call(
         pool_kernel,
@@ -81,7 +88,7 @@
         cost_estimate=pl.CostEstimate(
             flops=2 * count * rows.size, bytes_accessed=2 * rows.size + 2 * count * width, transcendentals=0
         ),
-    )(rim, rows)
+    )(rows)
 
 
 def attend_kernel(n_kv, first, where_ref, *refs):
@@ -119,14 +126,14 @@
                     col = lax.broadcasted_iota(jnp.int32, part.shape, 1)
                     row = lax.broadcasted_iota(jnp.int32, part.shape, 0)
                     part = jnp.where(9 * col - row <= base, part, -1e30)
-                ss[k, g * rows : (g + 1) * rows, :] = part
+                ss[g * (g + 1) // 2 + k] = part
                 here = jnp.max(part, axis=-1, keepdims=True)
                 tops[g] = here if k == 0 else jnp.maximum(tops[g], here)
         sums = [jnp.zeros((rows, 2 * HEAD), jnp.float32) for _ in range(NY)]
         for k in range(NY):
             values = jnp.concatenate([vs[k], ones], axis=1)
             for g in range(k, NY):
-                p = jnp.exp2((ss[k, g * rows : (g + 1) * rows, :] - tops[g]) * SCALE)
+                p = jnp.exp2((ss[g * (g + 1) // 2 + k] - tops[g]) * SCALE)
                 sums[g] += jnp.dot(p.astype(jnp.bfloat16), values, preferred_element_type=jnp.float32)
         for g in range(NY):
             qs[g] = (sums[g][:, :HEAD] / sums[g][:, HEAD:]).astype(jnp.bfloat16)
@@ -153,7 +160,7 @@
             pltpu.VMEM((NY, rows, HEAD), jnp.bfloat16),
             pltpu.VMEM((NY, keys, HEAD), jnp.bfloat16),
             pltpu.VMEM((NY, keys, HEAD), jnp.bfloat16),
-            pltpu.VMEM((NY, NY * rows, keys), jnp.float32),
+            pltpu.VMEM((NY * (NY + 1) // 2, rows, keys), jnp.float32),
         ],
         compiler_params=pltpu.CompilerParams(vmem_limit_bytes=VMEM),
         cost_estimate=pl.CostEstimate(
@@ -184,10 +191,14 @@
     )(mirrored, short_rows)
 
 
-def finish_kernel(where_ref, base_ref, pooled_ref, *refs):
-    o_refs, (out_ref, bottle_ref, total, sems) = refs[:-4], refs[-4:]
+def finish_kernel(where_ref, base_ref, pooled_ref, rim_ref, *refs):
+    o_refs, (out_ref, bottle_ref, total, pooled, sems) = refs[:-5], refs[-5:]
     y, part = where_ref[0], GROUP * HEAD
-    copies = [pltpu.make_async_copy(pooled_ref, bottle_ref, sems.at[NY])]
+    rows = pooled_ref[...].astype(jnp.float32)
+    rim = jnp.sum(rim_ref[...].astype(jnp.float32), axis=0, keepdims=True)
+    top = lax.broadcasted_iota(jnp.int32, rows.shape, 0) == 0
+    pooled[...] = jnp.where(top, (rows + rim) / 9.0, rows).astype(pooled.dtype)
+    copies = [pltpu.make_async_copy(pooled, bottle_ref, sems.at[NY])]
     copies[0].start()
     for d in range(NY):
         g = lax.rem(y + d, NY)
@@ -202,9 +213,9 @@
         copy.wait()
 
 
-def finish(where, total, pooled, o_slots):
+def finish(where, total, pooled, rim, o_slots):
     in_specs = [pl.BlockSpec(memory_space=pltpu.SMEM)]
-    in_specs += [pl.BlockSpec(memory_space=pltpu.VMEM)] * (2 + len(o_slots))
+    in_specs += [pl.BlockSpec(memory_space=pltpu.VMEM)] * (3 + len(o_slots))
     return pl.pallas_call(
         finish_kernel,
         in_specs=in_specs,
@@ -213,10 +224,14 @@
             jax.ShapeDtypeStruct(total.shape, jnp.bfloat16),
             jax.ShapeDtypeStruct(pooled.shape, jnp.bfloat16),
         ],
-        scratch_shapes=[pltpu.VMEM(total.shape, jnp.bfloat16), pltpu.SemaphoreType.DMA((NY + 1,))],
+        scratch_shapes=[
+            pltpu.VMEM(total.shape, jnp.bfloat16),
+            pltpu.VMEM(pooled.shape, jnp.bfloat16),
+            pltpu.SemaphoreType.DMA((NY + 1,)),
+        ],
         compiler_params=pltpu.CompilerParams(vmem_limit_bytes=VMEM),
         cost_estimate=pl.CostEstimate(flops=total.size, bytes_accessed=8 * total.size, transcendentals=0),
-    )(where, total, pooled, *o_slots)
+    )(where, total, pooled, rim, *o_slots)
 
 
 def ring_step(step, ahead, back):
@@ -242,8 +257,10 @@
 
     pieces = pack(where, short_key[0], short_value[0])
     own = [pieces[0]] + [move(pieces[d], dy=d) for d in range(1, NY)]
-    other = [move(pieces[d], dy=d, dx=1) for d in range(NY)]
-    block = jnp.concatenate([jnp.stack(own), jnp.stack(other)], axis=2)
+    mine = jnp.stack(own)
+    other = [move(after(pieces[d], own[1]), dy=d, dx=1) for d in range(NY)]
+    others = jnp.stack(other)
+    block = jnp.concatenate([mine, others], axis=2)
 
     query_late = after(query_rows, block)
     q_slots = [
@@ -256,22 +273,24 @@
         results = attend(where, query_rows, q_slots, arrivals, *PHASES[phase])
         return results[0], [results[0]] + [move(results[d], dy=-d) for d in range(1, NY)]
 
-    rim = lax.ppermute(
-        after(stream_rows[rows - 8 :], block), "seq", [(i, i + 1) for i in range(NY * NZ * NX - 1)]
-    )
-    both = ring_steps([block], [1, 2])
-    ends = [after(v, rim) for v in both[-2:]]
+    first_in = [jnp.concatenate(pair, axis=2) for pair in zip(ring_step(1, mine, mine), ring_step(1, others, others))]
+    pooled = pool(stream_rows)
+    bottleneck = section_shift(after(pooled, mirrored), 1)
+    rim = next_rows(after(stream_rows[rows - 8 :], mirrored))
+    first_in = list(lax.optimization_barrier(tuple(first_in)))
+    both = [block, *[after(v, q_slots[0]) for v in first_in]]
+    both = ring_steps(both, [2])
+    ends = [after(v, q_slots[2]) for v in both[-2:]]
     a, b = [[v[..., first * HEAD : (first + heads) * HEAD] for v in ends] for first, heads in PHASES]
-    a = both + ring_steps(a, [3, 4])[2:]
+    a = both + ring_steps(a, [3])[2:]
+    a = ring_steps([*a[:-2], *[after(v, q_slots[1]) for v in a[-2:]]], [4])
     b = both + ring_steps(b, [3])[2:]
-    done, a_slots = attended(0, a)
-    b = ring_steps([*b[:-2], *[after(v, done) for v in b[-2:]]], [4])
-    pooled = pool(after(rim, done), stream_rows)
+    done, a_slots = attended(0, [after(a[0], mirrored), *a[1:]])
+    b = ring_steps([*b[:-2], *[after(v, done, rim, bottleneck) for v in b[-2:]]], [4])
     done, b_slots = attended(1, [after(b[0], mirrored), *b[1:]])
     o_slots = a_slots + b_slots
-    bottleneck = section_shift(after(pooled, done), 1)
     total = base(after(mirrored, done), short_out[0])
-    output, bottleneck = finish(where, total, bottleneck, o_slots)
+    output, bottleneck = finish(where, total, bottleneck, rim, o_slots)
     return (output[None], bottleneck[None])
 
 

time: 127 us -> 109 us (0.86); the launches traced: 126 us -> 109 us
  waiting for transfers between devices: 52.2 us -> 32.3 us
  starting transfers between devices: 46.1 us -> 57.4 us
  local copies, waits for them, and re-layouts: 8.76 us -> 2.16 us
  Pallas kernels: 17.3 us -> 15.8 us
    ppermute x1, waiting for transfers between devices: 16.2 us -> 0.01 us  [next_rows(): return lax.ppermute(block, ('section', 'seq'), pairs)]
    ppermute x28 -> x30, starting transfers between devices: 41.9 us -> 50.5 us  [move(): return lax.ppermute(block, 'seq', seq_pairs(dy, dz, dx))]
    ppermute x28 -> x30, waiting for transfers between devices: 36 us -> 31.5 us  [move(): return lax.ppermute(block, 'seq', seq_pairs(dy, dz, dx))]
    ppermute x1, starting transfers between devices: 1.91 us -> 4.83 us  [next_rows(): return lax.ppermute(block, ('section', 'seq'), pairs)]
    slice x4, local copies, waits for them, and re-layouts: 2.82 us -> 0.14 us  [body(): v[..., first * HEAD:(first + heads) * HEAD]]
    unnamed x22 -> x10, local copies, waits for them, and re-layouts: 4.47 us -> 1.85 us
    pallas_call x2, Pallas kernels: 14 us -> 12.5 us  [attend(): pl.pallas_call(functools.partial(attend_kernel, len(arrivals), first), in...]
    dynamic_slice x1, local copies, waits for them, and re-layouts: 1.41 us -> 0.11 us  [body(): lax.dynamic_slice_in_dim(query_late, (y + d) % NY * part, part, 1)]
  transfers between devices with their start and end apart: 31 -> 33, of which waited for: 12 -> 11; matrix products, arithmetic and copies ran while one was open for 3% -> 1% of each run, Pallas kernels for 12% -> 12%
where the time goes in v1:
time: 109 us
  starting transfers between devices  57.4 us (53%)
  waiting for transfers between devices  32.3 us (30%)
  Pallas kernels  15.8 us (14%)
  local copies, waits for them, and re-layouts  2.16 us (2%)
  between operations  1.14 us (1%)
    ppermute x30, starting transfers between devices, move(): return lax.ppermute(block, 'seq', seq_pairs(dy, dz, dx))  50.5 us
    ppermute x30, waiting for transfers between devices, move(): return lax.ppermute(block, 'seq', seq_pairs(dy, dz, dx))  31.5 us
    pallas_call x2, Pallas kernels, attend(): pl.pallas_call(functools.partial(attend_kernel, len(arrivals), first), in...  12.5 us
    ppermute x1, starting transfers between devices, next_rows(): return lax.ppermute(block, ('section', 'seq'), pairs)  4.83 us
  transfers between devices with their start and end apart: 33, of which 11 were waited for; matrix products, arithmetic and copies ran while one was open for 1% of the time, Pallas kernels for 12%

profile of v1, /device:TPU:2, one launch (start us, length us, event | category | flops | bytes accessed | tf_op | source)
XLA Modules:
  0.0 109.2 jit_solution(2970341345943233345)
XLA Ops:
  0.7 0.1 pad_add_fusion.where_ref
  0.7 0.9 copy-done.3
  1.7 0.9 copy-done.4
  2.6 0.6 shard_map.68
  3.2 1.7 %collective-permute-start = (bf16[2,32,640]{2,1,0:T(8,128)(2,1)S(1)}, bf16[2,32,640]{2,1,0:T(8,128)(2,1)S(1)}, u32[]{:S(2)}, u32[]{:S(2)}) collective-permute-start(bf16[2,32,640]{2,1,0:T(8,128)(2,1)S(1)} %get-tuple-element.41), channel_id=1, source_target_pairs={{0,16},{1,17},{2,18},{3,19},{4,20},{5,21},{6,22},{7,23},{8,24},{9,... | collective-permute-start | bytes 245768 | tf_op jit(solution)/shard_map/ppermute | solution.py:31
  4.8 2.9 %collective-permute-start.1 = (bf16[2,32,640]{2,1,0:T(8,128)(2,1)S(1)}, bf16[2,32,640]{2,1,0:T(8,128)(2,1)S(1)}, u32[]{:S(2)}, u32[]{:S(2)}) collective-permute-start(bf16[2,32,640]{2,1,0:T(8,128)(2,1)S(1)} %get-tuple-element.42), channel_id=1, source_target_pairs={{0,32},{1,33},{2,34},{3,35},{4,36},{5,37},{6,38},{7,39},{8,40},{9,... | collective-permute-start | bytes 245768 | tf_op jit(solution)/shard_map/ppermute | solution.py:31
  7.7 1.3 %collective-permute-start.2 = (bf16[2,32,640]{2,1,0:T(8,128)(2,1)S(1)}, bf16[2,32,640]{2,1,0:T(8,128)(2,1)S(1)}, u32[]{:S(2)}, u32[]{:S(2)}) collective-permute-start(bf16[2,32,640]{2,1,0:T(8,128)(2,1)S(1)} %get-tuple-element.43), channel_id=1, source_target_pairs={{0,48},{1,49},{2,50},{3,51},{4,52},{5,53},{6,54},{7,55},{8,56},{9,... | collective-permute-start | bytes 245768 | tf_op jit(solution)/shard_map/ppermute | solution.py:31
  9.1 3.3 %collective-permute-start.3 = (bf16[2,32,640]{2,1,0:T(8,128)(2,1)S(1)}, bf16[2,32,640]{2,1,0:T(8,128)(2,1)S(1)}, u32[]{:S(2)}, u32[]{:S(2)}) collective-permute-start(bf16[2,32,640]{2,1,0:T(8,128)(2,1)S(1)} %get-tuple-element.40), channel_id=1, source_target_pairs={{0,1},{1,0},{2,3},{3,2},{4,5},{5,4},{6,7},{7,6},{8,9},{9,8},{10,11... | collective-permute-start | bytes 245768 | tf_op jit(solution)/shard_map/ppermute | solution.py:31
  12.4 0.0 collective-permute-start.4
  12.4 1.8 %collective-permute-start.5 = (bf16[2,32,640]{2,1,0:T(8,128)(2,1)S(1)}, bf16[2,32,640]{2,1,0:T(8,128)(2,1)S(1)}, u32[]{:S(2)}, u32[]{:S(2)}) collective-permute-start(bf16[2,32,640]{2,1,0:T(8,128)(2,1)S(1)} %get-tuple-element.42), channel_id=1, source_target_pairs={{0,33},{1,32},{2,35},{3,34},{4,37},{5,36},{6,39},{7,38},{8,41},{9,... | collective-permute-start | bytes 245768 | tf_op jit(solution)/shard_map/ppermute | solution.py:31
  14.2 0.0 collective-permute-done.1
  14.2 2.3 %collective-permute-start.6 = (bf16[2,32,640]{2,1,0:T(8,128)(2,1)S(1)}, bf16[2,32,640]{2,1,0:T(8,128)(2,1)S(1)}, u32[]{:S(2)}, u32[]{:S(2)}) collective-permute-start(bf16[2,32,640]{2,1,0:T(8,128)(2,1)S(1)} %get-tuple-element.43), channel_id=1, source_target_pairs={{0,49},{1,48},{2,51},{3,50},{4,53},{5,52},{6,55},{7,54},{8,57},{9,... | collective-permute-start | bytes 245768 | tf_op jit(solution)/shard_map/ppermute | solution.py:31
  16.6 0.0 collective-permute-done.2
  16.6 0.1 pad_maximum_fusion.2
  16.6 1.3 %collective-permute-start.11 = (bf16[4,2,32,640]{3,2,1,0:T(8,128)(2,1)S(1)}, bf16[4,2,32,640]{3,2,1,0:T(8,128)(2,1)S(1)}, u32[]{:S(2)}, u32[]{:S(2)}) collective-permute-start(bf16[4,2,32,640]{3,2,1,0:T(8,128)(2,1)S(1)} %pad_maximum_fusion.2), channel_id=1, source_target_pairs={{0,2},{1,3},{2,4},{3,5},{4,6},{5,7},{6,8},{7,9},{8,10},{9,11},{10,... | collective-permute-start | bytes 983048 | tf_op jit(solution)/shard_map/ppermute | solution.py:31
  17.9 0.0 collective-permute-done.3
  17.9 4.0 %collective-permute-start.13 = (bf16[4,2,32,640]{3,2,1,0:T(8,128)(2,1)S(1)}, bf16[4,2,32,640]{3,2,1,0:T(8,128)(2,1)S(1)}, u32[]{:S(2)}, u32[]{:S(2)}) collective-permute-start(bf16[4,2,32,640]{3,2,1,0:T(8,128)(2,1)S(1)} %pad_maximum_fusion.2), channel_id=1, source_target_pairs={{0,14},{1,15},{2,0},{3,1},{4,2},{5,3},{6,4},{7,5},{8,6},{9,7},{10,... | collective-permute-start | bytes 983048 | tf_op jit(solution)/shard_map/ppermute | solution.py:31
  22.0 0.0 collective-permute-done.4
  22.0 0.0 collective-permute-done.5
  22.0 0.1 pad_maximum_fusion.3
  22.0 0.1 collective-permute-start.12
  22.1 3.5 %collective-permute-start.14 = (bf16[4,2,32,640]{3,2,1,0:T(8,128)(2,1)S(1)}, bf16[4,2,32,640]{3,2,1,0:T(8,128)(2,1)S(1)}, u32[]{:S(2)}, u32[]{:S(2)}) collective-permute-start(bf16[4,2,32,640]{3,2,1,0:T(8,128)(2,1)S(1)} %pad_maximum_fusion.3), channel_id=1, source_target_pairs={{0,14},{1,15},{2,0},{3,1},{4,2},{5,3},{6,4},{7,5},{8,6},{9,7},{10,... | collective-permute-start | bytes 983048 | tf_op jit(solution)/shard_map/ppermute | solution.py:31
  25.6 0.1 maximum_maximum_fusion.refs_4_
  25.7 0.1 constant_dynamic-slice_fusion
  25.8 0.0 copy-start
  25.8 1.1 %collective-permute-start.8 = (bf16[288,640]{1,0:T(8,128)(2,1)S(1)}, bf16[288,640]{1,0:T(8,128)(2,1)S(1)}, u32[]{:S(2)}, u32[]{:S(2)}) collective-permute-start(bf16[288,640]{1,0:T(8,128)(2,1)S(1)} %get-tuple-element.72), channel_id=1, source_target_pairs={{0,16},{1,17},{2,18},{3,19},{4,20},{5,21},{6,22},{7,23},{8,24},{9,... | collective-permute-start | bytes 1105928 | tf_op jit(solution)/shard_map/ppermute | solution.py:31
  26.9 3.6 %collective-permute-done.11 = bf16[4,2,32,640]{3,2,1,0:T(8,128)(2,1)S(1)} collective-permute-done((bf16[4,2,32,640]{3,2,1,0:T(8,128)(2,1)S(1)}, bf16[4,2,32,640]{3,2,1,0:T(8,128)(2,1)S(1)}, u32[]{:S(2)}, u32[]{:S(2)}) %collective-permute-start.11) | collective-permute-done | bytes 327712 | tf_op jit(solution)/shard_map/ppermute | solution.py:31
  30.5 3.8 %collective-permute-done.12 = bf16[4,2,32,640]{3,2,1,0:T(8,128)(2,1)S(1)} collective-permute-done((bf16[4,2,32,640]{3,2,1,0:T(8,128)(2,1)S(1)}, bf16[4,2,32,640]{3,2,1,0:T(8,128)(2,1)S(1)}, u32[]{:S(2)}, u32[]{:S(2)}) %collective-permute-start.12) | collective-permute-done | bytes 327712 | tf_op jit(solution)/shard_map/ppermute | solution.py:31
  34.3 0.1 pad_maximum_fusion.refs_5_
  34.4 0.0 collective-permute-done.13
  34.4 0.0 collective-permute-done.14
  34.4 0.1 pad_maximum_fusion.1.refs_6_
  34.5 0.2 collective-permute-done.8.refs_1_
  34.6 2.9 %collective-permute-start.16 = (bf16[4,2,64,640]{3,2,1,0:T(8,128)(2,1)S(1)}, bf16[4,2,64,640]{3,2,1,0:T(8,128)(2,1)S(1)}, u32[]{:S(2)}, u32[]{:S(2)}) collective-permute-start(bf16[4,2,64,640]{3,2,1,0:T(8,128)(2,1)S(1)} %pad_maximum_fusion.1.refs_6_), channel_id=1, source_target_pairs={{0,14},{1,15},{2,0},{3,1},{4,2},{5,3},{6,4},{7,5},{8,6},{9,7},{10,... | collective-permute-start | bytes 1966088 | tf_op jit(solution)/shard_map/ppermute | solution.py:31
  37.5 2.1 %collective-permute-start.7 = (bf16[288,2560]{1,0:T(8,128)(2,1)S(1)}, bf16[288,2560]{1,0:T(8,128)(2,1)S(1)}, u32[]{:S(2)}, u32[]{:S(2)}) collective-permute-start(bf16[288,2560]{1,0:T(8,128)(2,1)S(1)} %bitcast.20), channel_id=1, source_target_pairs={{0,128},{64,192},{128,0},{192,64},{1,129},{65,193},{129,1},{193,65... | collective-permute-start | bytes 4423688 | tf_op jit(solution)/shard_map/ppermute | solution.py:36
  39.7 0.6 collective-permute-start.10
  40.3 6.9 %collective-permute-done.10.refs_3_ = bf16[288,640]{1,0:T(8,128)(2,1)S(1)} collective-permute-done((bf16[288,640]{1,0:T(8,128)(2,1)S(1)}, bf16[288,640]{1,0:T(8,128)(2,1)S(1)}, u32[]{:S(2)}, u32[]{:S(2)}) %collective-permute-start.10) | collective-permute-done | bytes 368672 | tf_op jit(solution)/shard_map/ppermute | solution.py:31
  47.2 2.0 %collective-permute-done.16.refs_8_ = bf16[4,2,64,640]{3,2,1,0:T(8,128)(2,1)S(1)} collective-permute-done((bf16[4,2,64,640]{3,2,1,0:T(8,128)(2,1)S(1)}, bf16[4,2,64,640]{3,2,1,0:T(8,128)(2,1)S(1)}, u32[]{:S(2)}, u32[]{:S(2)}) %collective-permute-start.16) | collective-permute-done | bytes 655392 | tf_op jit(solution)/shard_map/ppermute | solution.py:31
  49.3 3.2 %collective-permute-start.19 = (bf16[4,2,64,384]{3,2,1,0:T(8,128)(2,1)S(1)}, bf16[4,2,64,384]{3,2,1,0:T(8,128)(2,1)S(1)}, u32[]{:S(2)}, u32[]{:S(2)}) collective-permute-start(bf16[4,2,64,384]{3,2,1,0:T(8,128)(2,1)S(1)} %slice.32), channel_id=1, source_target_pairs={{0,14},{1,15},{2,0},{3,1},{4,2},{5,3},{6,4},{7,5},{8,6},{9,7},{10,... | collective-permute-start | bytes 1179656 | tf_op jit(solution)/shard_map/ppermute | solution.py:31
  52.5 0.1 collective-permute-start.18
  52.6 2.3 %collective-permute-start.9 = (bf16[288,640]{1,0:T(8,128)(2,1)S(1)}, bf16[288,640]{1,0:T(8,128)(2,1)S(1)}, u32[]{:S(2)}, u32[]{:S(2)}) collective-permute-start(bf16[288,640]{1,0:T(8,128)(2,1)S(1)} %get-tuple-element.71), channel_id=1, source_target_pairs={{0,32},{1,33},{2,34},{3,35},{4,36},{5,37},{6,38},{7,39},{8,40},{9,... | collective-permute-start | bytes 1105928 | tf_op jit(solution)/shard_map/ppermute | solution.py:31
  54.9 6.8 %collective-permute-done.9.refs_2_ = bf16[288,640]{1,0:T(8,128)(2,1)S(1)} collective-permute-done((bf16[288,640]{1,0:T(8,128)(2,1)S(1)}, bf16[288,640]{1,0:T(8,128)(2,1)S(1)}, u32[]{:S(2)}, u32[]{:S(2)}) %collective-permute-start.9) | collective-permute-done | bytes 368672 | tf_op jit(solution)/shard_map/ppermute | solution.py:31
  61.7 3.2 %collective-permute-start.21 = (bf16[4,2,32,384]{3,2,1,0:T(8,128)(2,1)S(1)}, bf16[4,2,32,384]{3,2,1,0:T(8,128)(2,1)S(1)}, u32[]{:S(2)}, u32[]{:S(2)}) collective-permute-start(bf16[4,2,32,384]{3,2,1,0:T(8,128)(2,1)S(1)} %slice.34), channel_id=1, source_target_pairs={{0,14},{1,15},{2,0},{3,1},{4,2},{5,3},{6,4},{7,5},{8,6},{9,7},{10,... | collective-permute-start | bytes 589832 | tf_op jit(solution)/shard_map/ppermute | solution.py:31
  65.0 0.1 collective-permute-start.20
  65.1 0.4 shard_map.70
  65.5 3.3 %collective-permute-start.24 = (bf16[4,2,64,256]{3,2,1,0:T(8,128)(2,1)S(1)}, bf16[4,2,64,256]{3,2,1,0:T(8,128)(2,1)S(1)}, u32[]{:S(2)}, u32[]{:S(2)}) collective-permute-start(bf16[4,2,64,256]{3,2,1,0:T(8,128)(2,1)S(1)} %slice.37), channel_id=1, source_target_pairs={{0,14},{1,15},{2,0},{3,1},{4,2},{5,3},{6,4},{7,5},{8,6},{9,7},{10,... | collective-permute-start | bytes 786440 | tf_op jit(solution)/shard_map/ppermute | solution.py:31
  68.8 0.8 collective-permute-done.7.mirrored_ref
  69.6 4.8 %collective-permute-start.22 = (bf16[8,2560]{1,0:T(8,128)(2,1)S(1)}, bf16[8,2560]{1,0:T(8,128)(2,1)S(1)}, u32[]{:S(2)}, u32[]{:S(2)}) collective-permute-start(bf16[8,2560]{1,0:T(8,128)(2,1)S(1)} %slice_bitcast_fusion), channel_id=1, source_target_pairs={{0,65},{1,66},{2,67},{3,68},{4,69},{5,70},{6,71},{7,72},{8,73},{9,... | collective-permute-start | bytes 122888 | tf_op jit(solution)/shard_map/ppermute | solution.py:44
  74.5 7.4 %shard_map.69 = (bf16[288,384]{1,0:T(8,128)(2,1)S(1)}, bf16[288,384]{1,0:T(8,128)(2,1)S(1)}, bf16[288,384]{1,0:T(8,128)(2,1)S(1)}, bf16[288,384]{1,0:T(8,128)(2,1)S(1)}) custom-call(s32[3]{0:T(128)S(1)} %pad_add_fusion.where_ref, bf16[288,2560]{1,0:T(8,128)(2,1)S(1)} %bitcast.23, bf16[288,640]{1,0:T(8,128)(2,1)S(1)} %collective-permute-done.8.refs_1_, ...), custom_call_target="tpu_custom_call" | custom-call | flops 3397386240 | bytes 3145728 | tf_op jit(solution)/shard_map/pallas_call | solution.py:154
  81.9 4.2 %collective-permute-start.26 = (bf16[4,2,32,256]{3,2,1,0:T(8,128)(2,1)S(1)}, bf16[4,2,32,256]{3,2,1,0:T(8,128)(2,1)S(1)}, u32[]{:S(2)}, u32[]{:S(2)}) collective-permute-start(bf16[4,2,32,256]{3,2,1,0:T(8,128)(2,1)S(1)} %slice.39), channel_id=1, source_target_pairs={{0,14},{1,15},{2,0},{3,1},{4,2},{5,3},{6,4},{7,5},{8,6},{9,7},{10,... | collective-permute-start | bytes 393224 | tf_op jit(solution)/shard_map/ppermute | solution.py:31
  86.1 0.1 collective-permute-start.25
  86.2 0.4 collective-permute-start.27
  86.6 2.9 %collective-permute-start.28 = (bf16[288,384]{1,0:T(8,128)(2,1)S(1)}, bf16[288,384]{1,0:T(8,128)(2,1)S(1)}, u32[]{:S(2)}, u32[]{:S(2)}) collective-permute-start(bf16[288,384]{1,0:T(8,128)(2,1)S(1)} %get-tuple-element.63), channel_id=1, source_target_pairs={{0,32},{1,33},{2,34},{3,35},{4,36},{5,37},{6,38},{7,39},{8,40},{9,... | collective-permute-start | bytes 663560 | tf_op jit(solution)/shard_map/ppermute | solution.py:31
  89.5 0.2 collective-permute-start.29
  89.7 2.6 %collective-permute-done.25.refs_11_ = bf16[4,2,32,256]{3,2,1,0:T(8,128)(2,1)S(1)} collective-permute-done((bf16[4,2,32,256]{3,2,1,0:T(8,128)(2,1)S(1)}, bf16[4,2,32,256]{3,2,1,0:T(8,128)(2,1)S(1)}, u32[]{:S(2)}, u32[]{:S(2)}) %collective-permute-start.25) | collective-permute-done | bytes 131104 | tf_op jit(solution)/shard_map/ppermute | solution.py:31
  92.3 5.1 %shard_map.71 = (bf16[288,256]{1,0:T(8,128)(2,1)S(1)}, bf16[288,256]{1,0:T(8,128)(2,1)S(1)}, bf16[288,256]{1,0:T(8,128)(2,1)S(1)}, bf16[288,256]{1,0:T(8,128)(2,1)S(1)}) custom-call(s32[3]{0:T(128)S(1)} %pad_add_fusion.where_ref, bf16[288,2560]{1,0:T(8,128)(2,1)S(1)} %bitcast.24, bf16[288,640]{1,0:T(8,128)(2,1)S(1)} %collective-permute-done.8.refs_1_, ...), custom_call_target="tpu_custom_call" | custom-call | flops 2264924160 | bytes 2097152 | tf_op jit(solution)/shard_map/pallas_call | solution.py:154
  97.4 0.5 collective-permute-start.30
  98.0 2.8 %collective-permute-start.31 = (bf16[288,256]{1,0:T(8,128)(2,1)S(1)}, bf16[288,256]{1,0:T(8,128)(2,1)S(1)}, u32[]{:S(2)}, u32[]{:S(2)}) collective-permute-start(bf16[288,256]{1,0:T(8,128)(2,1)S(1)} %get-tuple-element.66), channel_id=1, source_target_pairs={{0,32},{1,33},{2,34},{3,35},{4,36},{5,37},{6,38},{7,39},{8,40},{9,... | collective-permute-start | bytes 442376 | tf_op jit(solution)/shard_map/ppermute | solution.py:31
  100.8 0.2 collective-permute-start.32
  101.0 0.5 shard_map.72.base_ref
  101.6 1.1 %collective-permute-done.30.refs_5_ = bf16[288,256]{1,0:T(8,128)(2,1)S(1)} collective-permute-done((bf16[288,256]{1,0:T(8,128)(2,1)S(1)}, bf16[288,256]{1,0:T(8,128)(2,1)S(1)}, u32[]{:S(2)}, u32[]{:S(2)}) %collective-permute-start.30) | collective-permute-done | bytes 147488 | tf_op jit(solution)/shard_map/ppermute | solution.py:31
  102.7 2.7 %collective-permute-done.31.refs_6_ = bf16[288,256]{1,0:T(8,128)(2,1)S(1)} collective-permute-done((bf16[288,256]{1,0:T(8,128)(2,1)S(1)}, bf16[288,256]{1,0:T(8,128)(2,1)S(1)}, u32[]{:S(2)}, u32[]{:S(2)}) %collective-permute-start.31) | collective-permute-done | bytes 147488 | tf_op jit(solution)/shard_map/ppermute | solution.py:31
  105.3 1.8 %collective-permute-done.32.refs_7_ = bf16[288,256]{1,0:T(8,128)(2,1)S(1)} collective-permute-done((bf16[288,256]{1,0:T(8,128)(2,1)S(1)}, bf16[288,256]{1,0:T(8,128)(2,1)S(1)}, u32[]{:S(2)}, u32[]{:S(2)}) %collective-permute-start.32) | collective-permute-done | bytes 147488 | tf_op jit(solution)/shard_map/ppermute | solution.py:31
  107.2 1.9 %shard_map.73 = (bf16[288,2560]{1,0:T(8,128)(2,1)}, bf16[32,2560]{1,0:T(8,128)(2,1)}) custom-call(s32[3]{0:T(128)S(1)} %pad_add_fusion.where_ref, f32[288,2560]{1,0:T(8,128)S(1)} %shard_map.72.base_ref, bf16[32,2560]{1,0:T(8,128)(2,1)S(1)} %collective-permute-done.23.pooled_ref, bf16[8,2560]{1,0:T(8,128)(2,1)S(1)} %collective-permute-done.22.rim_ref, ...), custom_call_target="tpu_custom_call" | custom-call | flops 737280 | bytes 5898240 | tf_op jit(solution)/shard_map/pallas_call | solution.py:219
  (34 shorter events, 0.3 us)
Async XLA Ops:
  0.7 0.9 copy-start.3
  1.7 0.9 copy-start.4
  3.2 5.9 %collective-permute-start = (bf16[2,32,640]{2,1,0:T(8,128)(2,1)S(1)}, bf16[2,32,640]{2,1,0:T(8,128)(2,1)S(1)}, u32[]{:S(2)}, u32[]{:S(2)}) collective-permute-start(bf16[2,32,640]{2,1,0:T(8,128)(2,1)S(1)} %get-tuple-element.41), channel_id=1, source_target_pairs={{0,16},{1,17},{2,18},{3,19},{4,20},{5,21},{6,22},{7,23},{8,24},{9,... | collective-permute-start | bytes 245768 | tf_op jit(solution)/shard_map/ppermute | solution.py:31
  4.8 9.4 %collective-permute-start.1 = (bf16[2,32,640]{2,1,0:T(8,128)(2,1)S(1)}, bf16[2,32,640]{2,1,0:T(8,128)(2,1)S(1)}, u32[]{:S(2)}, u32[]{:S(2)}) collective-permute-start(bf16[2,32,640]{2,1,0:T(8,128)(2,1)S(1)} %get-tuple-element.42), channel_id=1, source_target_pairs={{0,32},{1,33},{2,34},{3,35},{4,36},{5,37},{6,38},{7,39},{8,40},{9,... | collective-permute-start | bytes 245768 | tf_op jit(solution)/shard_map/ppermute | solution.py:31
  7.7 8.8 %collective-permute-start.2 = (bf16[2,32,640]{2,1,0:T(8,128)(2,1)S(1)}, bf16[2,32,640]{2,1,0:T(8,128)(2,1)S(1)}, u32[]{:S(2)}, u32[]{:S(2)}) collective-permute-start(bf16[2,32,640]{2,1,0:T(8,128)(2,1)S(1)} %get-tuple-element.43), channel_id=1, source_target_pairs={{0,48},{1,49},{2,50},{3,51},{4,52},{5,53},{6,54},{7,55},{8,56},{9,... | collective-permute-start | bytes 245768 | tf_op jit(solution)/shard_map/ppermute | solution.py:31
  9.1 8.9 %collective-permute-start.3 = (bf16[2,32,640]{2,1,0:T(8,128)(2,1)S(1)}, bf16[2,32,640]{2,1,0:T(8,128)(2,1)S(1)}, u32[]{:S(2)}, u32[]{:S(2)}) collective-permute-start(bf16[2,32,640]{2,1,0:T(8,128)(2,1)S(1)} %get-tuple-element.40), channel_id=1, source_target_pairs={{0,1},{1,0},{2,3},{3,2},{4,5},{5,4},{6,7},{7,6},{8,9},{9,8},{10,11... | collective-permute-start | bytes 245768 | tf_op jit(solution)/shard_map/ppermute | solution.py:31
  12.4 9.6 %collective-permute-start.4 = (bf16[2,32,640]{2,1,0:T(8,128)(2,1)S(1)}, bf16[2,32,640]{2,1,0:T(8,128)(2,1)S(1)}, u32[]{:S(2)}, u32[]{:S(2)}) collective-permute-start(bf16[2,32,640]{2,1,0:T(8,128)(2,1)S(1)} %get-tuple-element.41), channel_id=1, source_target_pairs={{0,17},{1,16},{2,19},{3,18},{4,21},{5,20},{6,23},{7,22},{8,25},{9,... | collective-permute-start | bytes 245768 | tf_op jit(solution)/shard_map/ppermute | solution.py:31
  12.4 9.6 %collective-permute-start.5 = (bf16[2,32,640]{2,1,0:T(8,128)(2,1)S(1)}, bf16[2,32,640]{2,1,0:T(8,128)(2,1)S(1)}, u32[]{:S(2)}, u32[]{:S(2)}) collective-permute-start(bf16[2,32,640]{2,1,0:T(8,128)(2,1)S(1)} %get-tuple-element.42), channel_id=1, source_target_pairs={{0,33},{1,32},{2,35},{3,34},{4,37},{5,36},{6,39},{7,38},{8,41},{9,... | collective-permute-start | bytes 245768 | tf_op jit(solution)/shard_map/ppermute | solution.py:31
  14.2 7.8 %collective-permute-start.6 = (bf16[2,32,640]{2,1,0:T(8,128)(2,1)S(1)}, bf16[2,32,640]{2,1,0:T(8,128)(2,1)S(1)}, u32[]{:S(2)}, u32[]{:S(2)}) collective-permute-start(bf16[2,32,640]{2,1,0:T(8,128)(2,1)S(1)} %get-tuple-element.43), channel_id=1, source_target_pairs={{0,49},{1,48},{2,51},{3,50},{4,53},{5,52},{6,55},{7,54},{8,57},{9,... | collective-permute-start | bytes 245768 | tf_op jit(solution)/shard_map/ppermute | solution.py:31
  16.6 9.2 %copy-start.1 = (bf16[1,288,2560]{2,1,0:T(8,128)(2,1)S(1)}, bf16[1,288,2560]{2,1,0:T(8,128)(2,1)}, u32[]{:S(2)}) copy-start(bf16[1,288,2560]{2,1,0:T(8,128)(2,1)} %param.6) | copy-start | bytes 4423684
  16.6 13.9 %collective-permute-start.11 = (bf16[4,2,32,640]{3,2,1,0:T(8,128)(2,1)S(1)}, bf16[4,2,32,640]{3,2,1,0:T(8,128)(2,1)S(1)}, u32[]{:S(2)}, u32[]{:S(2)}) collective-permute-start(bf16[4,2,32,640]{3,2,1,0:T(8,128)(2,1)S(1)} %pad_maximum_fusion.2), channel_id=1, source_target_pairs={{0,2},{1,3},{2,4},{3,5},{4,6},{5,7},{6,8},{7,9},{8,10},{9,11},{10,... | collective-permute-start | bytes 983048 | tf_op jit(solution)/shard_map/ppermute | solution.py:31
  17.9 16.5 %collective-permute-start.13 = (bf16[4,2,32,640]{3,2,1,0:T(8,128)(2,1)S(1)}, bf16[4,2,32,640]{3,2,1,0:T(8,128)(2,1)S(1)}, u32[]{:S(2)}, u32[]{:S(2)}) collective-permute-start(bf16[4,2,32,640]{3,2,1,0:T(8,128)(2,1)S(1)} %pad_maximum_fusion.2), channel_id=1, source_target_pairs={{0,14},{1,15},{2,0},{3,1},{4,2},{5,3},{6,4},{7,5},{8,6},{9,7},{10,... | collective-permute-start | bytes 983048 | tf_op jit(solution)/shard_map/ppermute | solution.py:31
  22.0 12.3 %collective-permute-start.12 = (bf16[4,2,32,640]{3,2,1,0:T(8,128)(2,1)S(1)}, bf16[4,2,32,640]{3,2,1,0:T(8,128)(2,1)S(1)}, u32[]{:S(2)}, u32[]{:S(2)}) collective-permute-start(bf16[4,2,32,640]{3,2,1,0:T(8,128)(2,1)S(1)} %pad_maximum_fusion.3), channel_id=1, source_target_pairs={{0,2},{1,3},{2,4},{3,5},{4,6},{5,7},{6,8},{7,9},{8,10},{9,11},{10,... | collective-permute-start | bytes 983048 | tf_op jit(solution)/shard_map/ppermute | solution.py:31
  22.1 12.3 %collective-permute-start.14 = (bf16[4,2,32,640]{3,2,1,0:T(8,128)(2,1)S(1)}, bf16[4,2,32,640]{3,2,1,0:T(8,128)(2,1)S(1)}, u32[]{:S(2)}, u32[]{:S(2)}) collective-permute-start(bf16[4,2,32,640]{3,2,1,0:T(8,128)(2,1)S(1)} %pad_maximum_fusion.3), channel_id=1, source_target_pairs={{0,14},{1,15},{2,0},{3,1},{4,2},{5,3},{6,4},{7,5},{8,6},{9,7},{10,... | collective-permute-start | bytes 983048 | tf_op jit(solution)/shard_map/ppermute | solution.py:31
  25.8 11.7 %copy-start = (bf16[1,288,2560]{2,1,0:T(8,128)(2,1)S(1)}, bf16[1,288,2560]{2,1,0:T(8,128)(2,1)}, u32[]{:S(2)}) copy-start(bf16[1,288,2560]{2,1,0:T(8,128)(2,1)} %param.5) | copy-start | bytes 4423684
  25.8 8.8 %collective-permute-start.8 = (bf16[288,640]{1,0:T(8,128)(2,1)S(1)}, bf16[288,640]{1,0:T(8,128)(2,1)S(1)}, u32[]{:S(2)}, u32[]{:S(2)}) collective-permute-start(bf16[288,640]{1,0:T(8,128)(2,1)S(1)} %get-tuple-element.72), channel_id=1, source_target_pairs={{0,16},{1,17},{2,18},{3,19},{4,20},{5,21},{6,22},{7,23},{8,24},{9,... | collective-permute-start | bytes 1105928 | tf_op jit(solution)/shard_map/ppermute | solution.py:31
  34.6 14.6 %collective-permute-start.16 = (bf16[4,2,64,640]{3,2,1,0:T(8,128)(2,1)S(1)}, bf16[4,2,64,640]{3,2,1,0:T(8,128)(2,1)S(1)}, u32[]{:S(2)}, u32[]{:S(2)}) collective-permute-start(bf16[4,2,64,640]{3,2,1,0:T(8,128)(2,1)S(1)} %pad_maximum_fusion.1.refs_6_), channel_id=1, source_target_pairs={{0,14},{1,15},{2,0},{3,1},{4,2},{5,3},{6,4},{7,5},{8,6},{9,7},{10,... | collective-permute-start | bytes 1966088 | tf_op jit(solution)/shard_map/ppermute | solution.py:31
  37.5 14.9 %collective-permute-start.15 = (bf16[4,2,64,640]{3,2,1,0:T(8,128)(2,1)S(1)}, bf16[4,2,64,640]{3,2,1,0:T(8,128)(2,1)S(1)}, u32[]{:S(2)}, u32[]{:S(2)}) collective-permute-start(bf16[4,2,64,640]{3,2,1,0:T(8,128)(2,1)S(1)} %pad_maximum_fusion.refs_5_), channel_id=1, source_target_pairs={{0,2},{1,3},{2,4},{3,5},{4,6},{5,7},{6,8},{7,9},{8,10},{9,11},{10,... | collective-permute-start | bytes 1966088 | tf_op jit(solution)/shard_map/ppermute | solution.py:31
  37.5 32.1 %collective-permute-start.7 = (bf16[288,2560]{1,0:T(8,128)(2,1)S(1)}, bf16[288,2560]{1,0:T(8,128)(2,1)S(1)}, u32[]{:S(2)}, u32[]{:S(2)}) collective-permute-start(bf16[288,2560]{1,0:T(8,128)(2,1)S(1)} %bitcast.20), channel_id=1, source_target_pairs={{0,128},{64,192},{128,0},{192,64},{1,129},{65,193},{129,1},{193,65... | collective-permute-start | bytes 4423688 | tf_op jit(solution)/shard_map/ppermute | solution.py:36
  39.7 7.5 %collective-permute-start.10 = (bf16[288,640]{1,0:T(8,128)(2,1)S(1)}, bf16[288,640]{1,0:T(8,128)(2,1)S(1)}, u32[]{:S(2)}, u32[]{:S(2)}) collective-permute-start(bf16[288,640]{1,0:T(8,128)(2,1)S(1)} %get-tuple-element.70), channel_id=1, source_target_pairs={{0,48},{1,49},{2,50},{3,51},{4,52},{5,53},{6,54},{7,55},{8,56},{9,... | collective-permute-start | bytes 1105928 | tf_op jit(solution)/shard_map/ppermute | solution.py:31
  49.3 12.4 %collective-permute-start.19 = (bf16[4,2,64,384]{3,2,1,0:T(8,128)(2,1)S(1)}, bf16[4,2,64,384]{3,2,1,0:T(8,128)(2,1)S(1)}, u32[]{:S(2)}, u32[]{:S(2)}) collective-permute-start(bf16[4,2,64,384]{3,2,1,0:T(8,128)(2,1)S(1)} %slice.32), channel_id=1, source_target_pairs={{0,14},{1,15},{2,0},{3,1},{4,2},{5,3},{6,4},{7,5},{8,6},{9,7},{10,... | collective-permute-start | bytes 1179656 | tf_op jit(solution)/shard_map/ppermute | solution.py:31
  52.5 12.4 %collective-permute-start.18 = (bf16[4,2,64,384]{3,2,1,0:T(8,128)(2,1)S(1)}, bf16[4,2,64,384]{3,2,1,0:T(8,128)(2,1)S(1)}, u32[]{:S(2)}, u32[]{:S(2)}) collective-permute-start(bf16[4,2,64,384]{3,2,1,0:T(8,128)(2,1)S(1)} %slice.31), channel_id=1, source_target_pairs={{0,2},{1,3},{2,4},{3,5},{4,6},{5,7},{6,8},{7,9},{8,10},{9,11},{10,... | collective-permute-start | bytes 1179656 | tf_op jit(solution)/shard_map/ppermute | solution.py:31
  52.6 9.1 %collective-permute-start.9 = (bf16[288,640]{1,0:T(8,128)(2,1)S(1)}, bf16[288,640]{1,0:T(8,128)(2,1)S(1)}, u32[]{:S(2)}, u32[]{:S(2)}) collective-permute-start(bf16[288,640]{1,0:T(8,128)(2,1)S(1)} %get-tuple-element.71), channel_id=1, source_target_pairs={{0,32},{1,33},{2,34},{3,35},{4,36},{5,37},{6,38},{7,39},{8,40},{9,... | collective-permute-start | bytes 1105928 | tf_op jit(solution)/shard_map/ppermute | solution.py:31
  61.7 7.9 %collective-permute-start.21 = (bf16[4,2,32,384]{3,2,1,0:T(8,128)(2,1)S(1)}, bf16[4,2,32,384]{3,2,1,0:T(8,128)(2,1)S(1)}, u32[]{:S(2)}, u32[]{:S(2)}) collective-permute-start(bf16[4,2,32,384]{3,2,1,0:T(8,128)(2,1)S(1)} %slice.34), channel_id=1, source_target_pairs={{0,14},{1,15},{2,0},{3,1},{4,2},{5,3},{6,4},{7,5},{8,6},{9,7},{10,... | collective-permute-start | bytes 589832 | tf_op jit(solution)/shard_map/ppermute | solution.py:31
  65.0 9.5 %collective-permute-start.20 = (bf16[4,2,32,384]{3,2,1,0:T(8,128)(2,1)S(1)}, bf16[4,2,32,384]{3,2,1,0:T(8,128)(2,1)S(1)}, u32[]{:S(2)}, u32[]{:S(2)}) collective-permute-start(bf16[4,2,32,384]{3,2,1,0:T(8,128)(2,1)S(1)} %slice.33), channel_id=1, source_target_pairs={{0,2},{1,3},{2,4},{3,5},{4,6},{5,7},{6,8},{7,9},{8,10},{9,11},{10,... | collective-permute-start | bytes 589832 | tf_op jit(solution)/shard_map/ppermute | solution.py:31
  65.5 16.3 %collective-permute-start.24 = (bf16[4,2,64,256]{3,2,1,0:T(8,128)(2,1)S(1)}, bf16[4,2,64,256]{3,2,1,0:T(8,128)(2,1)S(1)}, u32[]{:S(2)}, u32[]{:S(2)}) collective-permute-start(bf16[4,2,64,256]{3,2,1,0:T(8,128)(2,1)S(1)} %slice.37), channel_id=1, source_target_pairs={{0,14},{1,15},{2,0},{3,1},{4,2},{5,3},{6,4},{7,5},{8,6},{9,7},{10,... | collective-permute-start | bytes 786440 | tf_op jit(solution)/shard_map/ppermute | solution.py:31
  68.8 17.3 %collective-permute-start.17 = (bf16[4,2,64,256]{3,2,1,0:T(8,128)(2,1)S(1)}, bf16[4,2,64,256]{3,2,1,0:T(8,128)(2,1)S(1)}, u32[]{:S(2)}, u32[]{:S(2)}) collective-permute-start(bf16[4,2,64,256]{3,2,1,0:T(8,128)(2,1)S(1)} %slice.30), channel_id=1, source_target_pairs={{0,2},{1,3},{2,4},{3,5},{4,6},{5,7},{6,8},{7,9},{8,10},{9,11},{10,... | collective-permute-start | bytes 786440 | tf_op jit(solution)/shard_map/ppermute | solution.py:31
  69.6 12.3 %collective-permute-start.23 = (bf16[32,2560]{1,0:T(8,128)(2,1)S(1)}, bf16[32,2560]{1,0:T(8,128)(2,1)S(1)}, u32[]{:S(2)}, u32[]{:S(2)}) collective-permute-start(bf16[32,2560]{1,0:T(8,128)(2,1)S(1)} %shard_map.70), channel_id=1, source_target_pairs={{0,64},{64,128},{128,192},{192,0},{1,65},{65,129},{129,193},{193,1... | collective-permute-start | bytes 491528 | tf_op jit(solution)/shard_map/ppermute | solution.py:36
  69.6 12.2 %collective-permute-start.22 = (bf16[8,2560]{1,0:T(8,128)(2,1)S(1)}, bf16[8,2560]{1,0:T(8,128)(2,1)S(1)}, u32[]{:S(2)}, u32[]{:S(2)}) collective-permute-start(bf16[8,2560]{1,0:T(8,128)(2,1)S(1)} %slice_bitcast_fusion), channel_id=1, source_target_pairs={{0,65},{1,66},{2,67},{3,68},{4,69},{5,70},{6,71},{7,72},{8,73},{9,... | collective-permute-start | bytes 122888 | tf_op jit(solution)/shard_map/ppermute | solution.py:44
  81.9 7.8 %collective-permute-start.26 = (bf16[4,2,32,256]{3,2,1,0:T(8,128)(2,1)S(1)}, bf16[4,2,32,256]{3,2,1,0:T(8,128)(2,1)S(1)}, u32[]{:S(2)}, u32[]{:S(2)}) collective-permute-start(bf16[4,2,32,256]{3,2,1,0:T(8,128)(2,1)S(1)} %slice.39), channel_id=1, source_target_pairs={{0,14},{1,15},{2,0},{3,1},{4,2},{5,3},{6,4},{7,5},{8,6},{9,7},{10,... | collective-permute-start | bytes 393224 | tf_op jit(solution)/shard_map/ppermute | solution.py:31
  86.1 6.3 %collective-permute-start.25 = (bf16[4,2,32,256]{3,2,1,0:T(8,128)(2,1)S(1)}, bf16[4,2,32,256]{3,2,1,0:T(8,128)(2,1)S(1)}, u32[]{:S(2)}, u32[]{:S(2)}) collective-permute-start(bf16[4,2,32,256]{3,2,1,0:T(8,128)(2,1)S(1)} %slice.38), channel_id=1, source_target_pairs={{0,2},{1,3},{2,4},{3,5},{4,6},{5,7},{6,8},{7,9},{8,10},{9,11},{10,... | collective-permute-start | bytes 393224 | tf_op jit(solution)/shard_map/ppermute | solution.py:31
  86.2 14.6 %collective-permute-start.27 = (bf16[288,384]{1,0:T(8,128)(2,1)S(1)}, bf16[288,384]{1,0:T(8,128)(2,1)S(1)}, u32[]{:S(2)}, u32[]{:S(2)}) collective-permute-start(bf16[288,384]{1,0:T(8,128)(2,1)S(1)} %get-tuple-element.62), channel_id=1, source_target_pairs={{0,48},{1,49},{2,50},{3,51},{4,52},{5,53},{6,54},{7,55},{8,56},{9,... | collective-permute-start | bytes 663560 | tf_op jit(solution)/shard_map/ppermute | solution.py:31
  86.6 15.0 %collective-permute-start.28 = (bf16[288,384]{1,0:T(8,128)(2,1)S(1)}, bf16[288,384]{1,0:T(8,128)(2,1)S(1)}, u32[]{:S(2)}, u32[]{:S(2)}) collective-permute-start(bf16[288,384]{1,0:T(8,128)(2,1)S(1)} %get-tuple-element.63), channel_id=1, source_target_pairs={{0,32},{1,33},{2,34},{3,35},{4,36},{5,37},{6,38},{7,39},{8,40},{9,... | collective-permute-start | bytes 663560 | tf_op jit(solution)/shard_map/ppermute | solution.py:31
  89.5 11.5 %copy-start.2 = (bf16[1,32,2560]{2,1,0:T(8,128)(2,1)S(1)}, bf16[1,32,2560]{2,1,0:T(8,128)(2,1)}, u32[]{:S(2)}) copy-start(bf16[1,32,2560]{2,1,0:T(8,128)(2,1)} %param.9) | copy-start | bytes 491524
  89.5 12.0 %collective-permute-start.29 = (bf16[288,384]{1,0:T(8,128)(2,1)S(1)}, bf16[288,384]{1,0:T(8,128)(2,1)S(1)}, u32[]{:S(2)}, u32[]{:S(2)}) collective-permute-start(bf16[288,384]{1,0:T(8,128)(2,1)S(1)} %get-tuple-element.64), channel_id=1, source_target_pairs={{0,16},{1,17},{2,18},{3,19},{4,20},{5,21},{6,22},{7,23},{8,24},{9,... | collective-permute-start | bytes 663560 | tf_op jit(solution)/shard_map/ppermute | solution.py:31
  97.4 5.2 %collective-permute-start.30 = (bf16[288,256]{1,0:T(8,128)(2,1)S(1)}, bf16[288,256]{1,0:T(8,128)(2,1)S(1)}, u32[]{:S(2)}, u32[]{:S(2)}) collective-permute-start(bf16[288,256]{1,0:T(8,128)(2,1)S(1)} %get-tuple-element.65), channel_id=1, source_target_pairs={{0,48},{1,49},{2,50},{3,51},{4,52},{5,53},{6,54},{7,55},{8,56},{9,... | collective-permute-start | bytes 442376 | tf_op jit(solution)/shard_map/ppermute | solution.py:31
  98.0 7.4 %collective-permute-start.31 = (bf16[288,256]{1,0:T(8,128)(2,1)S(1)}, bf16[288,256]{1,0:T(8,128)(2,1)S(1)}, u32[]{:S(2)}, u32[]{:S(2)}) collective-permute-start(bf16[288,256]{1,0:T(8,128)(2,1)S(1)} %get-tuple-element.66), channel_id=1, source_target_pairs={{0,32},{1,33},{2,34},{3,35},{4,36},{5,37},{6,38},{7,39},{8,40},{9,... | collective-permute-start | bytes 442376 | tf_op jit(solution)/shard_map/ppermute | solution.py:31
  100.8 6.4 %collective-permute-start.32 = (bf16[288,256]{1,0:T(8,128)(2,1)S(1)}, bf16[288,256]{1,0:T(8,128)(2,1)S(1)}, u32[]{:S(2)}, u32[]{:S(2)}) collective-permute-start(bf16[288,256]{1,0:T(8,128)(2,1)S(1)} %get-tuple-element.67), channel_id=1, source_target_pairs={{0,16},{1,17},{2,18},{3,19},{4,20},{5,21},{6,22},{7,23},{8,24},{9,... | collective-permute-start | bytes 442376 | tf_op jit(solution)/shard_map/ppermute | solution.py:31

commit v2 on v1

--- a/solution.py
+++ b/solution.py
@@ -274,21 +274,20 @@
         return results[0], [results[0]] + [move(results[d], dy=-d) for d in range(1, NY)]
 
     first_in = [jnp.concatenate(pair, axis=2) for pair in zip(ring_step(1, mine, mine), ring_step(1, others, others))]
-    pooled = pool(stream_rows)
-    bottleneck = section_shift(after(pooled, mirrored), 1)
-    rim = next_rows(after(stream_rows[rows - 8 :], mirrored))
     first_in = list(lax.optimization_barrier(tuple(first_in)))
     both = [block, *[after(v, q_slots[0]) for v in first_in]]
     both = ring_steps(both, [2])
     ends = [after(v, q_slots[2]) for v in both[-2:]]
     a, b = [[v[..., first * HEAD : (first + heads) * HEAD] for v in ends] for first, heads in PHASES]
-    a = both + ring_steps(a, [3])[2:]
-    a = ring_steps([*a[:-2], *[after(v, q_slots[1]) for v in a[-2:]]], [4])
+    a = both + ring_steps(a, [3, 4])[2:]
     b = both + ring_steps(b, [3])[2:]
-    done, a_slots = attended(0, [after(a[0], mirrored), *a[1:]])
-    b = ring_steps([*b[:-2], *[after(v, done, rim, bottleneck) for v in b[-2:]]], [4])
+    done, a_slots = attended(0, a)
+    b = ring_steps([*b[:-2], *[after(v, done) for v in b[-2:]]], [4])
     done, b_slots = attended(1, [after(b[0], mirrored), *b[1:]])
     o_slots = a_slots + b_slots
+    pooled = pool(stream_rows)
+    bottleneck = section_shift(after(pooled, done, *a_slots[1:]), 1)
+    rim = next_rows(after(stream_rows[rows - 8 :], done, *a_slots[1:]))
     total = base(after(mirrored, done), short_out[0])
     output, bottleneck = finish(where, total, bottleneck, rim, o_slots)
     return (output[None], bottleneck[None])

time: 109 us -> 108 us (level)
  the two profiles are of different devices: /device:TPU:2 before, /device:TPU:9 now
where the time goes in v2:
time: 108 us
  starting transfers between devices  59.8 us (55%)
  waiting for transfers between devices  28.4 us (26%)
  Pallas kernels  15.9 us (15%)
  local copies, waits for them, and re-layouts  2.15 us (2%)
  between operations  1.11 us (1%)
    ppermute x30, starting transfers between devices, move(): return lax.ppermute(block, 'seq', seq_pairs(dy, dz, dx))  44.1 us
    ppermute x30, waiting for transfers between devices, move(): return lax.ppermute(block, 'seq', seq_pairs(dy, dz, dx))  22.5 us
    ppermute x2, starting transfers between devices, section_shift(): lax.ppermute(block, 'section', [(i, (i + by) % count) for i in range(coun...  13.8 us
    pallas_call x2, Pallas kernels, attend(): pl.pallas_call(functools.partial(attend_kernel, len(arrivals), first), in...  12.5 us
    ppermute x1, waiting for transfers between devices, next_rows(): return lax.ppermute(block, ('section', 'seq'), pairs)  5.87 us
  transfers between devices with their start and end apart: 33, of which 8 were waited for; matrix products, arithmetic and copies ran while one was open for 1% of the time, Pallas kernels for 12%

profile of v2, /device:TPU:9, one launch (start us, length us, event | category | flops | bytes accessed | tf_op | source)
XLA Modules:
  0.0 107.6 jit_solution(11919121709852129535)
XLA Ops:
  0.7 0.1 pad_add_fusion.where_ref
  0.7 0.9 copy-done.3
  1.7 0.9 copy-done.4
  2.6 0.6 shard_map.68
  3.2 1.4 %collective-permute-start = (bf16[2,32,640]{2,1,0:T(8,128)(2,1)S(1)}, bf16[2,32,640]{2,1,0:T(8,128)(2,1)S(1)}, u32[]{:S(2)}, u32[]{:S(2)}) collective-permute-start(bf16[2,32,640]{2,1,0:T(8,128)(2,1)S(1)} %get-tuple-element.39), channel_id=1, source_target_pairs={{0,16},{1,17},{2,18},{3,19},{4,20},{5,21},{6,22},{7,23},{8,24},{9,... | collective-permute-start | bytes 245768 | tf_op jit(solution)/shard_map/ppermute | solution.py:31
  4.5 0.8 collective-permute-start.1
  5.4 2.0 %collective-permute-start.2 = (bf16[2,32,640]{2,1,0:T(8,128)(2,1)S(1)}, bf16[2,32,640]{2,1,0:T(8,128)(2,1)S(1)}, u32[]{:S(2)}, u32[]{:S(2)}) collective-permute-start(bf16[2,32,640]{2,1,0:T(8,128)(2,1)S(1)} %get-tuple-element.41), channel_id=1, source_target_pairs={{0,48},{1,49},{2,50},{3,51},{4,52},{5,53},{6,54},{7,55},{8,56},{9,... | collective-permute-start | bytes 245768 | tf_op jit(solution)/shard_map/ppermute | solution.py:31
  7.3 0.0 collective-permute-done
  7.3 1.2 %collective-permute-start.3 = (bf16[2,32,640]{2,1,0:T(8,128)(2,1)S(1)}, bf16[2,32,640]{2,1,0:T(8,128)(2,1)S(1)}, u32[]{:S(2)}, u32[]{:S(2)}) collective-permute-start(bf16[2,32,640]{2,1,0:T(8,128)(2,1)S(1)} %get-tuple-element.38), channel_id=1, source_target_pairs={{0,1},{1,0},{2,3},{3,2},{4,5},{5,4},{6,7},{7,6},{8,9},{9,8},{10,11... | collective-permute-start | bytes 245768 | tf_op jit(solution)/shard_map/ppermute | solution.py:31
  8.5 0.5 collective-permute-start.4
  9.0 3.3 %collective-permute-start.5 = (bf16[2,32,640]{2,1,0:T(8,128)(2,1)S(1)}, bf16[2,32,640]{2,1,0:T(8,128)(2,1)S(1)}, u32[]{:S(2)}, u32[]{:S(2)}) collective-permute-start(bf16[2,32,640]{2,1,0:T(8,128)(2,1)S(1)} %get-tuple-element.40), channel_id=1, source_target_pairs={{0,33},{1,32},{2,35},{3,34},{4,37},{5,36},{6,39},{7,38},{8,41},{9,... | collective-permute-start | bytes 245768 | tf_op jit(solution)/shard_map/ppermute | solution.py:31
  12.3 0.0 collective-permute-done.1
  12.3 0.4 collective-permute-start.6
  12.7 0.0 collective-permute-done.2
  12.7 0.1 pad_maximum_fusion.2
  12.8 1.7 %collective-permute-start.11 = (bf16[4,2,32,640]{3,2,1,0:T(8,128)(2,1)S(1)}, bf16[4,2,32,640]{3,2,1,0:T(8,128)(2,1)S(1)}, u32[]{:S(2)}, u32[]{:S(2)}) collective-permute-start(bf16[4,2,32,640]{3,2,1,0:T(8,128)(2,1)S(1)} %pad_maximum_fusion.2), channel_id=1, source_target_pairs={{0,2},{1,3},{2,4},{3,5},{4,6},{5,7},{6,8},{7,9},{8,10},{9,11},{10,... | collective-permute-start | bytes 983048 | tf_op jit(solution)/shard_map/ppermute | solution.py:31
  14.5 0.0 collective-permute-done.3
  14.5 4.0 %collective-permute-start.13 = (bf16[4,2,32,640]{3,2,1,0:T(8,128)(2,1)S(1)}, bf16[4,2,32,640]{3,2,1,0:T(8,128)(2,1)S(1)}, u32[]{:S(2)}, u32[]{:S(2)}) collective-permute-start(bf16[4,2,32,640]{3,2,1,0:T(8,128)(2,1)S(1)} %pad_maximum_fusion.2), channel_id=1, source_target_pairs={{0,14},{1,15},{2,0},{3,1},{4,2},{5,3},{6,4},{7,5},{8,6},{9,7},{10,... | collective-permute-start | bytes 983048 | tf_op jit(solution)/shard_map/ppermute | solution.py:31
  18.5 0.0 collective-permute-done.4
  18.5 0.0 collective-permute-done.5
  18.5 0.0 collective-permute-done.6
  18.5 0.1 pad_maximum_fusion.3
  18.6 0.5 collective-permute-start.12
  19.1 4.0 %collective-permute-start.14 = (bf16[4,2,32,640]{3,2,1,0:T(8,128)(2,1)S(1)}, bf16[4,2,32,640]{3,2,1,0:T(8,128)(2,1)S(1)}, u32[]{:S(2)}, u32[]{:S(2)}) collective-permute-start(bf16[4,2,32,640]{3,2,1,0:T(8,128)(2,1)S(1)} %pad_maximum_fusion.3), channel_id=1, source_target_pairs={{0,14},{1,15},{2,0},{3,1},{4,2},{5,3},{6,4},{7,5},{8,6},{9,7},{10,... | collective-permute-start | bytes 983048 | tf_op jit(solution)/shard_map/ppermute | solution.py:31
  23.1 0.1 maximum_maximum_fusion.refs_4_
  23.2 0.1 constant_dynamic-slice_fusion
  23.3 0.0 copy-start
  23.3 1.0 collective-permute-start.8
  24.3 7.0 %collective-permute-done.12 = bf16[4,2,32,640]{3,2,1,0:T(8,128)(2,1)S(1)} collective-permute-done((bf16[4,2,32,640]{3,2,1,0:T(8,128)(2,1)S(1)}, bf16[4,2,32,640]{3,2,1,0:T(8,128)(2,1)S(1)}, u32[]{:S(2)}, u32[]{:S(2)}) %collective-permute-start.12) | collective-permute-done | bytes 327712 | tf_op jit(solution)/shard_map/ppermute | solution.py:31
  31.3 0.1 pad_maximum_fusion.refs_5_
  31.3 0.1 pad_maximum_fusion.1.refs_6_
  31.4 2.7 %collective-permute-start.16 = (bf16[4,2,64,640]{3,2,1,0:T(8,128)(2,1)S(1)}, bf16[4,2,64,640]{3,2,1,0:T(8,128)(2,1)S(1)}, u32[]{:S(2)}, u32[]{:S(2)}) collective-permute-start(bf16[4,2,64,640]{3,2,1,0:T(8,128)(2,1)S(1)} %pad_maximum_fusion.1.refs_6_), channel_id=1, source_target_pairs={{0,14},{1,15},{2,0},{3,1},{4,2},{5,3},{6,4},{7,5},{8,6},{9,7},{10,... | collective-permute-start | bytes 1966088 | tf_op jit(solution)/shard_map/ppermute | solution.py:31
  34.1 2.5 %collective-permute-start.7 = (bf16[288,2560]{1,0:T(8,128)(2,1)S(1)}, bf16[288,2560]{1,0:T(8,128)(2,1)S(1)}, u32[]{:S(2)}, u32[]{:S(2)}) collective-permute-start(bf16[288,2560]{1,0:T(8,128)(2,1)S(1)} %bitcast.20), channel_id=1, source_target_pairs={{0,128},{64,192},{128,0},{192,64},{1,129},{65,193},{129,1},{193,65... | collective-permute-start | bytes 4423688 | tf_op jit(solution)/shard_map/ppermute | solution.py:36
  36.6 0.5 collective-permute-start.10
  37.2 6.1 %collective-permute-done.10.refs_3_ = bf16[288,640]{1,0:T(8,128)(2,1)S(1)} collective-permute-done((bf16[288,640]{1,0:T(8,128)(2,1)S(1)}, bf16[288,640]{1,0:T(8,128)(2,1)S(1)}, u32[]{:S(2)}, u32[]{:S(2)}) %collective-permute-start.10) | collective-permute-done | bytes 368672 | tf_op jit(solution)/shard_map/ppermute | solution.py:31
  43.3 1.4 %collective-permute-done.16.refs_8_ = bf16[4,2,64,640]{3,2,1,0:T(8,128)(2,1)S(1)} collective-permute-done((bf16[4,2,64,640]{3,2,1,0:T(8,128)(2,1)S(1)}, bf16[4,2,64,640]{3,2,1,0:T(8,128)(2,1)S(1)}, u32[]{:S(2)}, u32[]{:S(2)}) %collective-permute-start.16) | collective-permute-done | bytes 655392 | tf_op jit(solution)/shard_map/ppermute | solution.py:31
  44.8 3.7 %collective-permute-start.19 = (bf16[4,2,64,384]{3,2,1,0:T(8,128)(2,1)S(1)}, bf16[4,2,64,384]{3,2,1,0:T(8,128)(2,1)S(1)}, u32[]{:S(2)}, u32[]{:S(2)}) collective-permute-start(bf16[4,2,64,384]{3,2,1,0:T(8,128)(2,1)S(1)} %slice.32), channel_id=1, source_target_pairs={{0,14},{1,15},{2,0},{3,1},{4,2},{5,3},{6,4},{7,5},{8,6},{9,7},{10,... | collective-permute-start | bytes 1179656 | tf_op jit(solution)/shard_map/ppermute | solution.py:31
  48.5 0.1 collective-permute-start.18
  48.6 1.3 %collective-permute-start.9 = (bf16[288,640]{1,0:T(8,128)(2,1)S(1)}, bf16[288,640]{1,0:T(8,128)(2,1)S(1)}, u32[]{:S(2)}, u32[]{:S(2)}) collective-permute-start(bf16[288,640]{1,0:T(8,128)(2,1)S(1)} %get-tuple-element.67), channel_id=1, source_target_pairs={{0,32},{1,33},{2,34},{3,35},{4,36},{5,37},{6,38},{7,39},{8,40},{9,... | collective-permute-start | bytes 1105928 | tf_op jit(solution)/shard_map/ppermute | solution.py:31
  49.9 3.2 %collective-permute-done.19.refs_10_ = bf16[4,2,64,384]{3,2,1,0:T(8,128)(2,1)S(1)} collective-permute-done((bf16[4,2,64,384]{3,2,1,0:T(8,128)(2,1)S(1)}, bf16[4,2,64,384]{3,2,1,0:T(8,128)(2,1)S(1)}, u32[]{:S(2)}, u32[]{:S(2)}) %collective-permute-start.19) | collective-permute-done | bytes 393248 | tf_op jit(solution)/shard_map/ppermute | solution.py:31
  53.2 3.5 %collective-permute-start.21 = (bf16[4,2,32,384]{3,2,1,0:T(8,128)(2,1)S(1)}, bf16[4,2,32,384]{3,2,1,0:T(8,128)(2,1)S(1)}, u32[]{:S(2)}, u32[]{:S(2)}) collective-permute-start(bf16[4,2,32,384]{3,2,1,0:T(8,128)(2,1)S(1)} %slice.41), channel_id=1, source_target_pairs={{0,14},{1,15},{2,0},{3,1},{4,2},{5,3},{6,4},{7,5},{8,6},{9,7},{10,... | collective-permute-start | bytes 589832 | tf_op jit(solution)/shard_map/ppermute | solution.py:31
  56.7 0.0 collective-permute-done.18.refs_9_
  56.7 0.1 collective-permute-start.20
  56.9 2.7 %collective-permute-start.22 = (bf16[4,2,64,256]{3,2,1,0:T(8,128)(2,1)S(1)}, bf16[4,2,64,256]{3,2,1,0:T(8,128)(2,1)S(1)}, u32[]{:S(2)}, u32[]{:S(2)}) collective-permute-start(bf16[4,2,64,256]{3,2,1,0:T(8,128)(2,1)S(1)} %slice.35), channel_id=1, source_target_pairs={{0,14},{1,15},{2,0},{3,1},{4,2},{5,3},{6,4},{7,5},{8,6},{9,7},{10,... | collective-permute-start | bytes 786440 | tf_op jit(solution)/shard_map/ppermute | solution.py:31
  59.6 0.5 collective-permute-done.21.refs_12_
  60.1 3.8 %collective-permute-done.20.refs_11_ = bf16[4,2,32,384]{3,2,1,0:T(8,128)(2,1)S(1)} collective-permute-done((bf16[4,2,32,384]{3,2,1,0:T(8,128)(2,1)S(1)}, bf16[4,2,32,384]{3,2,1,0:T(8,128)(2,1)S(1)}, u32[]{:S(2)}, u32[]{:S(2)}) %collective-permute-start.20) | collective-permute-done | bytes 196640 | tf_op jit(solution)/shard_map/ppermute | solution.py:31
  63.9 7.4 %shard_map.69 = (bf16[288,384]{1,0:T(8,128)(2,1)S(1)}, bf16[288,384]{1,0:T(8,128)(2,1)S(1)}, bf16[288,384]{1,0:T(8,128)(2,1)S(1)}, bf16[288,384]{1,0:T(8,128)(2,1)S(1)}) custom-call(s32[3]{0:T(128)S(1)} %pad_add_fusion.where_ref, bf16[288,2560]{1,0:T(8,128)(2,1)S(1)} %bitcast.23, bf16[288,640]{1,0:T(8,128)(2,1)S(1)} %collective-permute-done.8.refs_1_, ...), custom_call_target="tpu_custom_call" | custom-call | flops 3397386240 | bytes 3145728 | tf_op jit(solution)/shard_map/pallas_call | solution.py:154
  71.3 0.3 collective-permute-start.24
  71.6 1.5 %collective-permute-start.23 = (bf16[4,2,32,256]{3,2,1,0:T(8,128)(2,1)S(1)}, bf16[4,2,32,256]{3,2,1,0:T(8,128)(2,1)S(1)}, u32[]{:S(2)}, u32[]{:S(2)}) collective-permute-start(bf16[4,2,32,256]{3,2,1,0:T(8,128)(2,1)S(1)} %slice.36), channel_id=1, source_target_pairs={{0,2},{1,3},{2,4},{3,5},{4,6},{5,7},{6,8},{7,9},{8,10},{9,11},{10,... | collective-permute-start | bytes 393224 | tf_op jit(solution)/shard_map/ppermute | solution.py:31
  73.2 0.4 collective-permute-start.25
  73.6 1.8 %collective-permute-start.26 = (bf16[288,384]{1,0:T(8,128)(2,1)S(1)}, bf16[288,384]{1,0:T(8,128)(2,1)S(1)}, u32[]{:S(2)}, u32[]{:S(2)}) collective-permute-start(bf16[288,384]{1,0:T(8,128)(2,1)S(1)} %get-tuple-element.57), channel_id=1, source_target_pairs={{0,32},{1,33},{2,34},{3,35},{4,36},{5,37},{6,38},{7,39},{8,40},{9,... | collective-permute-start | bytes 663560 | tf_op jit(solution)/shard_map/ppermute | solution.py:31
  75.4 0.6 collective-permute-start.27
  75.9 0.4 shard_map.72
  76.3 0.0 copy-start.2
  76.3 0.4 collective-permute-done.23.refs_11_
  76.8 5.2 %shard_map.70 = (bf16[288,256]{1,0:T(8,128)(2,1)S(1)}, bf16[288,256]{1,0:T(8,128)(2,1)S(1)}, bf16[288,256]{1,0:T(8,128)(2,1)S(1)}, bf16[288,256]{1,0:T(8,128)(2,1)S(1)}) custom-call(s32[3]{0:T(128)S(1)} %pad_add_fusion.where_ref, bf16[288,2560]{1,0:T(8,128)(2,1)S(1)} %bitcast.24, bf16[288,640]{1,0:T(8,128)(2,1)S(1)} %collective-permute-done.8.refs_1_, ...), custom_call_target="tpu_custom_call" | custom-call | flops 2264924160 | bytes 2097152 | tf_op jit(solution)/shard_map/pallas_call | solution.py:154
  81.9 0.6 collective-permute-start.30
  82.5 1.7 %collective-permute-start.31 = (bf16[288,256]{1,0:T(8,128)(2,1)S(1)}, bf16[288,256]{1,0:T(8,128)(2,1)S(1)}, u32[]{:S(2)}, u32[]{:S(2)}) collective-permute-start(bf16[288,256]{1,0:T(8,128)(2,1)S(1)} %get-tuple-element.62), channel_id=1, source_target_pairs={{0,32},{1,33},{2,34},{3,35},{4,36},{5,37},{6,38},{7,39},{8,40},{9,... | collective-permute-start | bytes 442376 | tf_op jit(solution)/shard_map/ppermute | solution.py:31
  84.2 1.8 %collective-permute-start.32 = (bf16[288,256]{1,0:T(8,128)(2,1)S(1)}, bf16[288,256]{1,0:T(8,128)(2,1)S(1)}, u32[]{:S(2)}, u32[]{:S(2)}) collective-permute-start(bf16[288,256]{1,0:T(8,128)(2,1)S(1)} %get-tuple-element.63), channel_id=1, source_target_pairs={{0,16},{1,17},{2,18},{3,19},{4,20},{5,21},{6,22},{7,23},{8,24},{9,... | collective-permute-start | bytes 442376 | tf_op jit(solution)/shard_map/ppermute | solution.py:31
  86.0 11.3 %collective-permute-start.28 = (bf16[32,2560]{1,0:T(8,128)(2,1)S(1)}, bf16[32,2560]{1,0:T(8,128)(2,1)S(1)}, u32[]{:S(2)}, u32[]{:S(2)}) collective-permute-start(bf16[32,2560]{1,0:T(8,128)(2,1)S(1)} %shard_map.72), channel_id=1, source_target_pairs={{0,64},{64,128},{128,192},{192,0},{1,65},{65,129},{129,193},{193,1... | collective-permute-start | bytes 491528 | tf_op jit(solution)/shard_map/ppermute | solution.py:36
  97.3 1.9 %collective-permute-start.29 = (bf16[8,2560]{1,0:T(8,128)(2,1)S(1)}, bf16[8,2560]{1,0:T(8,128)(2,1)S(1)}, u32[]{:S(2)}, u32[]{:S(2)}) collective-permute-start(bf16[8,2560]{1,0:T(8,128)(2,1)S(1)} %slice_bitcast_fusion), channel_id=1, source_target_pairs={{0,65},{1,66},{2,67},{3,68},{4,69},{5,70},{6,71},{7,72},{8,73},{9,... | collective-permute-start | bytes 122888 | tf_op jit(solution)/shard_map/ppermute | solution.py:44
  99.2 0.5 shard_map.71.base_ref
  99.7 5.9 %collective-permute-done.29.rim_ref = bf16[8,2560]{1,0:T(8,128)(2,1)S(1)} collective-permute-done((bf16[8,2560]{1,0:T(8,128)(2,1)S(1)}, bf16[8,2560]{1,0:T(8,128)(2,1)S(1)}, u32[]{:S(2)}, u32[]{:S(2)}) %collective-permute-start.29) | collective-permute-done | bytes 40992 | tf_op jit(solution)/shard_map/ppermute | solution.py:44
  105.6 1.9 %shard_map.73 = (bf16[288,2560]{1,0:T(8,128)(2,1)}, bf16[32,2560]{1,0:T(8,128)(2,1)}) custom-call(s32[3]{0:T(128)S(1)} %pad_add_fusion.where_ref, f32[288,2560]{1,0:T(8,128)S(1)} %shard_map.71.base_ref, bf16[32,2560]{1,0:T(8,128)(2,1)S(1)} %collective-permute-done.28.pooled_ref, bf16[8,2560]{1,0:T(8,128)(2,1)S(1)} %collective-permute-done.29.rim_ref, ...), custom_call_target="tpu_custom_call" | custom-call | flops 737280 | bytes 5898240 | tf_op jit(solution)/shard_map/pallas_call | solution.py:219
  (34 shorter events, 0.2 us)
Async XLA Ops:
  0.7 0.9 copy-start.3
  1.7 0.9 copy-start.4
  3.2 4.2 %collective-permute-start = (bf16[2,32,640]{2,1,0:T(8,128)(2,1)S(1)}, bf16[2,32,640]{2,1,0:T(8,128)(2,1)S(1)}, u32[]{:S(2)}, u32[]{:S(2)}) collective-permute-start(bf16[2,32,640]{2,1,0:T(8,128)(2,1)S(1)} %get-tuple-element.39), channel_id=1, source_target_pairs={{0,16},{1,17},{2,18},{3,19},{4,20},{5,21},{6,22},{7,23},{8,24},{9,... | collective-permute-start | bytes 245768 | tf_op jit(solution)/shard_map/ppermute | solution.py:31
  4.5 7.8 %collective-permute-start.1 = (bf16[2,32,640]{2,1,0:T(8,128)(2,1)S(1)}, bf16[2,32,640]{2,1,0:T(8,128)(2,1)S(1)}, u32[]{:S(2)}, u32[]{:S(2)}) collective-permute-start(bf16[2,32,640]{2,1,0:T(8,128)(2,1)S(1)} %get-tuple-element.40), channel_id=1, source_target_pairs={{0,32},{1,33},{2,34},{3,35},{4,36},{5,37},{6,38},{7,39},{8,40},{9,... | collective-permute-start | bytes 245768 | tf_op jit(solution)/shard_map/ppermute | solution.py:31
  5.4 7.4 %collective-permute-start.2 = (bf16[2,32,640]{2,1,0:T(8,128)(2,1)S(1)}, bf16[2,32,640]{2,1,0:T(8,128)(2,1)S(1)}, u32[]{:S(2)}, u32[]{:S(2)}) collective-permute-start(bf16[2,32,640]{2,1,0:T(8,128)(2,1)S(1)} %get-tuple-element.41), channel_id=1, source_target_pairs={{0,48},{1,49},{2,50},{3,51},{4,52},{5,53},{6,54},{7,55},{8,56},{9,... | collective-permute-start | bytes 245768 | tf_op jit(solution)/shard_map/ppermute | solution.py:31
  7.3 7.2 %collective-permute-start.3 = (bf16[2,32,640]{2,1,0:T(8,128)(2,1)S(1)}, bf16[2,32,640]{2,1,0:T(8,128)(2,1)S(1)}, u32[]{:S(2)}, u32[]{:S(2)}) collective-permute-start(bf16[2,32,640]{2,1,0:T(8,128)(2,1)S(1)} %get-tuple-element.38), channel_id=1, source_target_pairs={{0,1},{1,0},{2,3},{3,2},{4,5},{5,4},{6,7},{7,6},{8,9},{9,8},{10,11... | collective-permute-start | bytes 245768 | tf_op jit(solution)/shard_map/ppermute | solution.py:31
  8.5 10.0 %collective-permute-start.4 = (bf16[2,32,640]{2,1,0:T(8,128)(2,1)S(1)}, bf16[2,32,640]{2,1,0:T(8,128)(2,1)S(1)}, u32[]{:S(2)}, u32[]{:S(2)}) collective-permute-start(bf16[2,32,640]{2,1,0:T(8,128)(2,1)S(1)} %get-tuple-element.39), channel_id=1, source_target_pairs={{0,17},{1,16},{2,19},{3,18},{4,21},{5,20},{6,23},{7,22},{8,25},{9,... | collective-permute-start | bytes 245768 | tf_op jit(solution)/shard_map/ppermute | solution.py:31
  9.0 9.5 %collective-permute-start.5 = (bf16[2,32,640]{2,1,0:T(8,128)(2,1)S(1)}, bf16[2,32,640]{2,1,0:T(8,128)(2,1)S(1)}, u32[]{:S(2)}, u32[]{:S(2)}) collective-permute-start(bf16[2,32,640]{2,1,0:T(8,128)(2,1)S(1)} %get-tuple-element.40), channel_id=1, source_target_pairs={{0,33},{1,32},{2,35},{3,34},{4,37},{5,36},{6,39},{7,38},{8,41},{9,... | collective-permute-start | bytes 245768 | tf_op jit(solution)/shard_map/ppermute | solution.py:31
  12.3 6.2 %collective-permute-start.6 = (bf16[2,32,640]{2,1,0:T(8,128)(2,1)S(1)}, bf16[2,32,640]{2,1,0:T(8,128)(2,1)S(1)}, u32[]{:S(2)}, u32[]{:S(2)}) collective-permute-start(bf16[2,32,640]{2,1,0:T(8,128)(2,1)S(1)} %get-tuple-element.41), channel_id=1, source_target_pairs={{0,49},{1,48},{2,51},{3,50},{4,53},{5,52},{6,55},{7,54},{8,57},{9,... | collective-permute-start | bytes 245768 | tf_op jit(solution)/shard_map/ppermute | solution.py:31
  12.7 10.5 %copy-start.1 = (bf16[1,288,2560]{2,1,0:T(8,128)(2,1)S(1)}, bf16[1,288,2560]{2,1,0:T(8,128)(2,1)}, u32[]{:S(2)}) copy-start(bf16[1,288,2560]{2,1,0:T(8,128)(2,1)} %param.6) | copy-start | bytes 4423684
  12.8 11.5 %collective-permute-start.11 = (bf16[4,2,32,640]{3,2,1,0:T(8,128)(2,1)S(1)}, bf16[4,2,32,640]{3,2,1,0:T(8,128)(2,1)S(1)}, u32[]{:S(2)}, u32[]{:S(2)}) collective-permute-start(bf16[4,2,32,640]{3,2,1,0:T(8,128)(2,1)S(1)} %pad_maximum_fusion.2), channel_id=1, source_target_pairs={{0,2},{1,3},{2,4},{3,5},{4,6},{5,7},{6,8},{7,9},{8,10},{9,11},{10,... | collective-permute-start | bytes 983048 | tf_op jit(solution)/shard_map/ppermute | solution.py:31
  14.5 16.8 %collective-permute-start.13 = (bf16[4,2,32,640]{3,2,1,0:T(8,128)(2,1)S(1)}, bf16[4,2,32,640]{3,2,1,0:T(8,128)(2,1)S(1)}, u32[]{:S(2)}, u32[]{:S(2)}) collective-permute-start(bf16[4,2,32,640]{3,2,1,0:T(8,128)(2,1)S(1)} %pad_maximum_fusion.2), channel_id=1, source_target_pairs={{0,14},{1,15},{2,0},{3,1},{4,2},{5,3},{6,4},{7,5},{8,6},{9,7},{10,... | collective-permute-start | bytes 983048 | tf_op jit(solution)/shard_map/ppermute | solution.py:31
  18.6 12.7 %collective-permute-start.12 = (bf16[4,2,32,640]{3,2,1,0:T(8,128)(2,1)S(1)}, bf16[4,2,32,640]{3,2,1,0:T(8,128)(2,1)S(1)}, u32[]{:S(2)}, u32[]{:S(2)}) collective-permute-start(bf16[4,2,32,640]{3,2,1,0:T(8,128)(2,1)S(1)} %pad_maximum_fusion.3), channel_id=1, source_target_pairs={{0,2},{1,3},{2,4},{3,5},{4,6},{5,7},{6,8},{7,9},{8,10},{9,11},{10,... | collective-permute-start | bytes 983048 | tf_op jit(solution)/shard_map/ppermute | solution.py:31
  19.1 12.3 %collective-permute-start.14 = (bf16[4,2,32,640]{3,2,1,0:T(8,128)(2,1)S(1)}, bf16[4,2,32,640]{3,2,1,0:T(8,128)(2,1)S(1)}, u32[]{:S(2)}, u32[]{:S(2)}) collective-permute-start(bf16[4,2,32,640]{3,2,1,0:T(8,128)(2,1)S(1)} %pad_maximum_fusion.3), channel_id=1, source_target_pairs={{0,14},{1,15},{2,0},{3,1},{4,2},{5,3},{6,4},{7,5},{8,6},{9,7},{10,... | collective-permute-start | bytes 983048 | tf_op jit(solution)/shard_map/ppermute | solution.py:31
  23.3 10.8 %copy-start = (bf16[1,288,2560]{2,1,0:T(8,128)(2,1)S(1)}, bf16[1,288,2560]{2,1,0:T(8,128)(2,1)}, u32[]{:S(2)}) copy-start(bf16[1,288,2560]{2,1,0:T(8,128)(2,1)} %param.5) | copy-start | bytes 4423684
  23.3 8.1 %collective-permute-start.8 = (bf16[288,640]{1,0:T(8,128)(2,1)S(1)}, bf16[288,640]{1,0:T(8,128)(2,1)S(1)}, u32[]{:S(2)}, u32[]{:S(2)}) collective-permute-start(bf16[288,640]{1,0:T(8,128)(2,1)S(1)} %get-tuple-element.68), channel_id=1, source_target_pairs={{0,16},{1,17},{2,18},{3,19},{4,20},{5,21},{6,22},{7,23},{8,24},{9,... | collective-permute-start | bytes 1105928 | tf_op jit(solution)/shard_map/ppermute | solution.py:31
  31.4 13.3 %collective-permute-start.16 = (bf16[4,2,64,640]{3,2,1,0:T(8,128)(2,1)S(1)}, bf16[4,2,64,640]{3,2,1,0:T(8,128)(2,1)S(1)}, u32[]{:S(2)}, u32[]{:S(2)}) collective-permute-start(bf16[4,2,64,640]{3,2,1,0:T(8,128)(2,1)S(1)} %pad_maximum_fusion.1.refs_6_), channel_id=1, source_target_pairs={{0,14},{1,15},{2,0},{3,1},{4,2},{5,3},{6,4},{7,5},{8,6},{9,7},{10,... | collective-permute-start | bytes 1966088 | tf_op jit(solution)/shard_map/ppermute | solution.py:31
  34.1 14.3 %collective-permute-start.15 = (bf16[4,2,64,640]{3,2,1,0:T(8,128)(2,1)S(1)}, bf16[4,2,64,640]{3,2,1,0:T(8,128)(2,1)S(1)}, u32[]{:S(2)}, u32[]{:S(2)}) collective-permute-start(bf16[4,2,64,640]{3,2,1,0:T(8,128)(2,1)S(1)} %pad_maximum_fusion.refs_5_), channel_id=1, source_target_pairs={{0,2},{1,3},{2,4},{3,5},{4,6},{5,7},{6,8},{7,9},{8,10},{9,11},{10,... | collective-permute-start | bytes 1966088 | tf_op jit(solution)/shard_map/ppermute | solution.py:31
  34.1 41.2 %collective-permute-start.7 = (bf16[288,2560]{1,0:T(8,128)(2,1)S(1)}, bf16[288,2560]{1,0:T(8,128)(2,1)S(1)}, u32[]{:S(2)}, u32[]{:S(2)}) collective-permute-start(bf16[288,2560]{1,0:T(8,128)(2,1)S(1)} %bitcast.20), channel_id=1, source_target_pairs={{0,128},{64,192},{128,0},{192,64},{1,129},{65,193},{129,1},{193,65... | collective-permute-start | bytes 4423688 | tf_op jit(solution)/shard_map/ppermute | solution.py:36
  36.6 6.7 %collective-permute-start.10 = (bf16[288,640]{1,0:T(8,128)(2,1)S(1)}, bf16[288,640]{1,0:T(8,128)(2,1)S(1)}, u32[]{:S(2)}, u32[]{:S(2)}) collective-permute-start(bf16[288,640]{1,0:T(8,128)(2,1)S(1)} %get-tuple-element.66), channel_id=1, source_target_pairs={{0,48},{1,49},{2,50},{3,51},{4,52},{5,53},{6,54},{7,55},{8,56},{9,... | collective-permute-start | bytes 1105928 | tf_op jit(solution)/shard_map/ppermute | solution.py:31
  44.8 8.4 %collective-permute-start.19 = (bf16[4,2,64,384]{3,2,1,0:T(8,128)(2,1)S(1)}, bf16[4,2,64,384]{3,2,1,0:T(8,128)(2,1)S(1)}, u32[]{:S(2)}, u32[]{:S(2)}) collective-permute-start(bf16[4,2,64,384]{3,2,1,0:T(8,128)(2,1)S(1)} %slice.32), channel_id=1, source_target_pairs={{0,14},{1,15},{2,0},{3,1},{4,2},{5,3},{6,4},{7,5},{8,6},{9,7},{10,... | collective-permute-start | bytes 1179656 | tf_op jit(solution)/shard_map/ppermute | solution.py:31
  48.5 8.2 %collective-permute-start.18 = (bf16[4,2,64,384]{3,2,1,0:T(8,128)(2,1)S(1)}, bf16[4,2,64,384]{3,2,1,0:T(8,128)(2,1)S(1)}, u32[]{:S(2)}, u32[]{:S(2)}) collective-permute-start(bf16[4,2,64,384]{3,2,1,0:T(8,128)(2,1)S(1)} %slice.31), channel_id=1, source_target_pairs={{0,2},{1,3},{2,4},{3,5},{4,6},{5,7},{6,8},{7,9},{8,10},{9,11},{10,... | collective-permute-start | bytes 1179656 | tf_op jit(solution)/shard_map/ppermute | solution.py:31
  48.6 11.0 %collective-permute-start.9 = (bf16[288,640]{1,0:T(8,128)(2,1)S(1)}, bf16[288,640]{1,0:T(8,128)(2,1)S(1)}, u32[]{:S(2)}, u32[]{:S(2)}) collective-permute-start(bf16[288,640]{1,0:T(8,128)(2,1)S(1)} %get-tuple-element.67), channel_id=1, source_target_pairs={{0,32},{1,33},{2,34},{3,35},{4,36},{5,37},{6,38},{7,39},{8,40},{9,... | collective-permute-start | bytes 1105928 | tf_op jit(solution)/shard_map/ppermute | solution.py:31
  53.2 6.9 %collective-permute-start.21 = (bf16[4,2,32,384]{3,2,1,0:T(8,128)(2,1)S(1)}, bf16[4,2,32,384]{3,2,1,0:T(8,128)(2,1)S(1)}, u32[]{:S(2)}, u32[]{:S(2)}) collective-permute-start(bf16[4,2,32,384]{3,2,1,0:T(8,128)(2,1)S(1)} %slice.41), channel_id=1, source_target_pairs={{0,14},{1,15},{2,0},{3,1},{4,2},{5,3},{6,4},{7,5},{8,6},{9,7},{10,... | collective-permute-start | bytes 589832 | tf_op jit(solution)/shard_map/ppermute | solution.py:31
  56.7 7.2 %collective-permute-start.20 = (bf16[4,2,32,384]{3,2,1,0:T(8,128)(2,1)S(1)}, bf16[4,2,32,384]{3,2,1,0:T(8,128)(2,1)S(1)}, u32[]{:S(2)}, u32[]{:S(2)}) collective-permute-start(bf16[4,2,32,384]{3,2,1,0:T(8,128)(2,1)S(1)} %slice.40), channel_id=1, source_target_pairs={{0,2},{1,3},{2,4},{3,5},{4,6},{5,7},{6,8},{7,9},{8,10},{9,11},{10,... | collective-permute-start | bytes 589832 | tf_op jit(solution)/shard_map/ppermute | solution.py:31
  56.9 14.4 %collective-permute-start.22 = (bf16[4,2,64,256]{3,2,1,0:T(8,128)(2,1)S(1)}, bf16[4,2,64,256]{3,2,1,0:T(8,128)(2,1)S(1)}, u32[]{:S(2)}, u32[]{:S(2)}) collective-permute-start(bf16[4,2,64,256]{3,2,1,0:T(8,128)(2,1)S(1)} %slice.35), channel_id=1, source_target_pairs={{0,14},{1,15},{2,0},{3,1},{4,2},{5,3},{6,4},{7,5},{8,6},{9,7},{10,... | collective-permute-start | bytes 786440 | tf_op jit(solution)/shard_map/ppermute | solution.py:31
  59.6 12.0 %collective-permute-start.17 = (bf16[4,2,64,256]{3,2,1,0:T(8,128)(2,1)S(1)}, bf16[4,2,64,256]{3,2,1,0:T(8,128)(2,1)S(1)}, u32[]{:S(2)}, u32[]{:S(2)}) collective-permute-start(bf16[4,2,64,256]{3,2,1,0:T(8,128)(2,1)S(1)} %slice.30), channel_id=1, source_target_pairs={{0,2},{1,3},{2,4},{3,5},{4,6},{5,7},{6,8},{7,9},{8,10},{9,11},{10,... | collective-permute-start | bytes 786440 | tf_op jit(solution)/shard_map/ppermute | solution.py:31
  71.3 5.0 %collective-permute-start.24 = (bf16[4,2,32,256]{3,2,1,0:T(8,128)(2,1)S(1)}, bf16[4,2,32,256]{3,2,1,0:T(8,128)(2,1)S(1)}, u32[]{:S(2)}, u32[]{:S(2)}) collective-permute-start(bf16[4,2,32,256]{3,2,1,0:T(8,128)(2,1)S(1)} %slice.37), channel_id=1, source_target_pairs={{0,14},{1,15},{2,0},{3,1},{4,2},{5,3},{6,4},{7,5},{8,6},{9,7},{10,... | collective-permute-start | bytes 393224 | tf_op jit(solution)/shard_map/ppermute | solution.py:31
  71.6 5.1 %collective-permute-start.23 = (bf16[4,2,32,256]{3,2,1,0:T(8,128)(2,1)S(1)}, bf16[4,2,32,256]{3,2,1,0:T(8,128)(2,1)S(1)}, u32[]{:S(2)}, u32[]{:S(2)}) collective-permute-start(bf16[4,2,32,256]{3,2,1,0:T(8,128)(2,1)S(1)} %slice.36), channel_id=1, source_target_pairs={{0,2},{1,3},{2,4},{3,5},{4,6},{5,7},{6,8},{7,9},{8,10},{9,11},{10,... | collective-permute-start | bytes 393224 | tf_op jit(solution)/shard_map/ppermute | solution.py:31
  73.2 11.0 %collective-permute-start.25 = (bf16[288,384]{1,0:T(8,128)(2,1)S(1)}, bf16[288,384]{1,0:T(8,128)(2,1)S(1)}, u32[]{:S(2)}, u32[]{:S(2)}) collective-permute-start(bf16[288,384]{1,0:T(8,128)(2,1)S(1)} %get-tuple-element.56), channel_id=1, source_target_pairs={{0,48},{1,49},{2,50},{3,51},{4,52},{5,53},{6,54},{7,55},{8,56},{9,... | collective-permute-start | bytes 663560 | tf_op jit(solution)/shard_map/ppermute | solution.py:31
  73.6 12.4 %collective-permute-start.26 = (bf16[288,384]{1,0:T(8,128)(2,1)S(1)}, bf16[288,384]{1,0:T(8,128)(2,1)S(1)}, u32[]{:S(2)}, u32[]{:S(2)}) collective-permute-start(bf16[288,384]{1,0:T(8,128)(2,1)S(1)} %get-tuple-element.57), channel_id=1, source_target_pairs={{0,32},{1,33},{2,34},{3,35},{4,36},{5,37},{6,38},{7,39},{8,40},{9,... | collective-permute-start | bytes 663560 | tf_op jit(solution)/shard_map/ppermute | solution.py:31
  75.4 10.6 %collective-permute-start.27 = (bf16[288,384]{1,0:T(8,128)(2,1)S(1)}, bf16[288,384]{1,0:T(8,128)(2,1)S(1)}, u32[]{:S(2)}, u32[]{:S(2)}) collective-permute-start(bf16[288,384]{1,0:T(8,128)(2,1)S(1)} %get-tuple-element.58), channel_id=1, source_target_pairs={{0,16},{1,17},{2,18},{3,19},{4,20},{5,21},{6,22},{7,23},{8,24},{9,... | collective-permute-start | bytes 663560 | tf_op jit(solution)/shard_map/ppermute | solution.py:31
  76.3 22.9 %copy-start.2 = (bf16[1,32,2560]{2,1,0:T(8,128)(2,1)S(1)}, bf16[1,32,2560]{2,1,0:T(8,128)(2,1)}, u32[]{:S(2)}) copy-start(bf16[1,32,2560]{2,1,0:T(8,128)(2,1)} %param.9) | copy-start | bytes 491524
  81.9 23.7 %collective-permute-start.30 = (bf16[288,256]{1,0:T(8,128)(2,1)S(1)}, bf16[288,256]{1,0:T(8,128)(2,1)S(1)}, u32[]{:S(2)}, u32[]{:S(2)}) collective-permute-start(bf16[288,256]{1,0:T(8,128)(2,1)S(1)} %get-tuple-element.61), channel_id=1, source_target_pairs={{0,48},{1,49},{2,50},{3,51},{4,52},{5,53},{6,54},{7,55},{8,56},{9,... | collective-permute-start | bytes 442376 | tf_op jit(solution)/shard_map/ppermute | solution.py:31
  82.5 23.1 %collective-permute-start.31 = (bf16[288,256]{1,0:T(8,128)(2,1)S(1)}, bf16[288,256]{1,0:T(8,128)(2,1)S(1)}, u32[]{:S(2)}, u32[]{:S(2)}) collective-permute-start(bf16[288,256]{1,0:T(8,128)(2,1)S(1)} %get-tuple-element.62), channel_id=1, source_target_pairs={{0,32},{1,33},{2,34},{3,35},{4,36},{5,37},{6,38},{7,39},{8,40},{9,... | collective-permute-start | bytes 442376 | tf_op jit(solution)/shard_map/ppermute | solution.py:31
  84.2 21.4 %collective-permute-start.32 = (bf16[288,256]{1,0:T(8,128)(2,1)S(1)}, bf16[288,256]{1,0:T(8,128)(2,1)S(1)}, u32[]{:S(2)}, u32[]{:S(2)}) collective-permute-start(bf16[288,256]{1,0:T(8,128)(2,1)S(1)} %get-tuple-element.63), channel_id=1, source_target_pairs={{0,16},{1,17},{2,18},{3,19},{4,20},{5,21},{6,22},{7,23},{8,24},{9,... | collective-permute-start | bytes 442376 | tf_op jit(solution)/shard_map/ppermute | solution.py:31
  86.0 19.6 %collective-permute-start.28 = (bf16[32,2560]{1,0:T(8,128)(2,1)S(1)}, bf16[32,2560]{1,0:T(8,128)(2,1)S(1)}, u32[]{:S(2)}, u32[]{:S(2)}) collective-permute-start(bf16[32,2560]{1,0:T(8,128)(2,1)S(1)} %shard_map.72), channel_id=1, source_target_pairs={{0,64},{64,128},{128,192},{192,0},{1,65},{65,129},{129,193},{193,1... | collective-permute-start | bytes 491528 | tf_op jit(solution)/shard_map/ppermute | solution.py:36
  97.3 8.3 %collective-permute-start.29 = (bf16[8,2560]{1,0:T(8,128)(2,1)S(1)}, bf16[8,2560]{1,0:T(8,128)(2,1)S(1)}, u32[]{:S(2)}, u32[]{:S(2)}) collective-permute-start(bf16[8,2560]{1,0:T(8,128)(2,1)S(1)} %slice_bitcast_fusion), channel_id=1, source_target_pairs={{0,65},{1,66},{2,67},{3,68},{4,69},{5,70},{6,71},{7,72},{8,73},{9,... | collective-permute-start | bytes 122888 | tf_op jit(solution)/shard_map/ppermute | solution.py:44

commit v3 on v2

--- a/solution.py
+++ b/solution.py
@@ -269,9 +269,10 @@
     ]
     mirrored = section_shift(after(stream_rows, block), 2)
 
-    def attended(phase, arrivals):
+    def attended(phase, arrivals, *needed):
         results = attend(where, query_rows, q_slots, arrivals, *PHASES[phase])
-        return results[0], [results[0]] + [move(results[d], dy=-d) for d in range(1, NY)]
+        sent = [move(after(results[d], *needed) if needed else results[d], dy=-d) for d in range(1, NY)]
+        return results[0], [results[0]] + sent
 
     first_in = [jnp.concatenate(pair, axis=2) for pair in zip(ring_step(1, mine, mine), ring_step(1, others, others))]
     first_in = list(lax.optimization_barrier(tuple(first_in)))
@@ -283,10 +284,9 @@
     b = both + ring_steps(b, [3])[2:]
     done, a_slots = attended(0, a)
     b = ring_steps([*b[:-2], *[after(v, done) for v in b[-2:]]], [4])
-    done, b_slots = attended(1, [after(b[0], mirrored), *b[1:]])
+    bottleneck = section_shift(after(pool(stream_rows), done, mirrored), 1)
+    done, b_slots = attended(1, [after(b[0], mirrored), *b[1:]], bottleneck)
     o_slots = a_slots + b_slots
-    pooled = pool(stream_rows)
-    bottleneck = section_shift(after(pooled, done, *a_slots[1:]), 1)
     rim = next_rows(after(stream_rows[rows - 8 :], done, *a_slots[1:]))
     total = base(after(mirrored, done), short_out[0])
     output, bottleneck = finish(where, total, bottleneck, rim, o_slots)

time: 108 us -> 105 us (0.972)
  the two profiles are of different devices: /device:TPU:9 before, /device:TPU:2 now
where the time goes in v3:
time: 105 us; the launch traced here: 104 us
  starting transfers between devices  56.8 us (54%)
  waiting for transfers between devices  27.4 us (26%)
  Pallas kernels  15.9 us (15%)
  local copies, waits for them, and re-layouts  2.14 us (2%)
  between operations  1.13 us (1%)
    ppermute x30, starting transfers between devices, move(): return lax.ppermute(block, 'seq', seq_pairs(dy, dz, dx))  52.3 us
    ppermute x30, waiting for transfers between devices, move(): return lax.ppermute(block, 'seq', seq_pairs(dy, dz, dx))  24.9 us
    pallas_call x2, Pallas kernels, attend(): pl.pallas_call(functools.partial(attend_kernel, len(arrivals), first), in...  12.6 us
    ppermute x1, waiting for transfers between devices, next_rows(): return lax.ppermute(block, ('section', 'seq'), pairs)  2.47 us
    ppermute x1, starting transfers between devices, next_rows(): return lax.ppermute(block, ('section', 'seq'), pairs)  2.29 us
    ppermute x2, starting transfers between devices, section_shift(): lax.ppermute(block, 'section', [(i, (i + by) % count) for i in range(coun...  2.21 us
  transfers between devices with their start and end apart: 33, of which 10 were waited for; matrix products, arithmetic and copies ran while one was open for 1% of the time, Pallas kernels for 13%

profile of v3, /device:TPU:2, one launch (start us, length us, event | category | flops | bytes accessed | tf_op | source)
XLA Modules:
  0.0 103.7 jit_solution(12598306200271840608)
XLA Ops:
  0.7 0.1 pad_add_fusion.where_ref
  0.7 0.9 copy-done.3
  1.7 0.9 copy-done.4
  2.6 0.6 shard_map.68
  3.2 1.7 %collective-permute-start = (bf16[2,32,640]{2,1,0:T(8,128)(2,1)S(1)}, bf16[2,32,640]{2,1,0:T(8,128)(2,1)S(1)}, u32[]{:S(2)}, u32[]{:S(2)}) collective-permute-start(bf16[2,32,640]{2,1,0:T(8,128)(2,1)S(1)} %get-tuple-element.42), channel_id=1, source_target_pairs={{0,16},{1,17},{2,18},{3,19},{4,20},{5,21},{6,22},{7,23},{8,24},{9,... | collective-permute-start | bytes 245768 | tf_op jit(solution)/shard_map/ppermute | solution.py:31
  4.8 1.7 %collective-permute-start.2 = (bf16[2,32,640]{2,1,0:T(8,128)(2,1)S(1)}, bf16[2,32,640]{2,1,0:T(8,128)(2,1)S(1)}, u32[]{:S(2)}, u32[]{:S(2)}) collective-permute-start(bf16[2,32,640]{2,1,0:T(8,128)(2,1)S(1)} %get-tuple-element.44), channel_id=1, source_target_pairs={{0,48},{1,49},{2,50},{3,51},{4,52},{5,53},{6,54},{7,55},{8,56},{9,... | collective-permute-start | bytes 245768 | tf_op jit(solution)/shard_map/ppermute | solution.py:31
  6.5 2.0 %collective-permute-start.1 = (bf16[2,32,640]{2,1,0:T(8,128)(2,1)S(1)}, bf16[2,32,640]{2,1,0:T(8,128)(2,1)S(1)}, u32[]{:S(2)}, u32[]{:S(2)}) collective-permute-start(bf16[2,32,640]{2,1,0:T(8,128)(2,1)S(1)} %get-tuple-element.43), channel_id=1, source_target_pairs={{0,32},{1,33},{2,34},{3,35},{4,36},{5,37},{6,38},{7,39},{8,40},{9,... | collective-permute-start | bytes 245768 | tf_op jit(solution)/shard_map/ppermute | solution.py:31
  8.5 0.4 collective-permute-done
  8.9 2.2 %collective-permute-start.6 = (bf16[2,32,640]{2,1,0:T(8,128)(2,1)S(1)}, bf16[2,32,640]{2,1,0:T(8,128)(2,1)S(1)}, u32[]{:S(2)}, u32[]{:S(2)}) collective-permute-start(bf16[2,32,640]{2,1,0:T(8,128)(2,1)S(1)} %get-tuple-element.44), channel_id=1, source_target_pairs={{0,49},{1,48},{2,51},{3,50},{4,53},{5,52},{6,55},{7,54},{8,57},{9,... | collective-permute-start | bytes 245768 | tf_op jit(solution)/shard_map/ppermute | solution.py:31
  11.1 1.2 %collective-permute-start.5 = (bf16[2,32,640]{2,1,0:T(8,128)(2,1)S(1)}, bf16[2,32,640]{2,1,0:T(8,128)(2,1)S(1)}, u32[]{:S(2)}, u32[]{:S(2)}) collective-permute-start(bf16[2,32,640]{2,1,0:T(8,128)(2,1)S(1)} %get-tuple-element.43), channel_id=1, source_target_pairs={{0,33},{1,32},{2,35},{3,34},{4,37},{5,36},{6,39},{7,38},{8,41},{9,... | collective-permute-start | bytes 245768 | tf_op jit(solution)/shard_map/ppermute | solution.py:31
  12.2 1.8 %collective-permute-start.4 = (bf16[2,32,640]{2,1,0:T(8,128)(2,1)S(1)}, bf16[2,32,640]{2,1,0:T(8,128)(2,1)S(1)}, u32[]{:S(2)}, u32[]{:S(2)}) collective-permute-start(bf16[2,32,640]{2,1,0:T(8,128)(2,1)S(1)} %get-tuple-element.42), channel_id=1, source_target_pairs={{0,17},{1,16},{2,19},{3,18},{4,21},{5,20},{6,23},{7,22},{8,25},{9,... | collective-permute-start | bytes 245768 | tf_op jit(solution)/shard_map/ppermute | solution.py:31
  14.0 0.0 collective-permute-done.2
  14.0 0.9 collective-permute-start.3
  15.0 0.1 pad_maximum_fusion.2
  15.0 1.7 %collective-permute-start.11 = (bf16[4,2,32,640]{3,2,1,0:T(8,128)(2,1)S(1)}, bf16[4,2,32,640]{3,2,1,0:T(8,128)(2,1)S(1)}, u32[]{:S(2)}, u32[]{:S(2)}) collective-permute-start(bf16[4,2,32,640]{3,2,1,0:T(8,128)(2,1)S(1)} %pad_maximum_fusion.2), channel_id=1, source_target_pairs={{0,2},{1,3},{2,4},{3,5},{4,6},{5,7},{6,8},{7,9},{8,10},{9,11},{10,... | collective-permute-start | bytes 983048 | tf_op jit(solution)/shard_map/ppermute | solution.py:31
  16.7 0.0 collective-permute-done.6
  16.7 4.0 %collective-permute-start.13 = (bf16[4,2,32,640]{3,2,1,0:T(8,128)(2,1)S(1)}, bf16[4,2,32,640]{3,2,1,0:T(8,128)(2,1)S(1)}, u32[]{:S(2)}, u32[]{:S(2)}) collective-permute-start(bf16[4,2,32,640]{3,2,1,0:T(8,128)(2,1)S(1)} %pad_maximum_fusion.2), channel_id=1, source_target_pairs={{0,14},{1,15},{2,0},{3,1},{4,2},{5,3},{6,4},{7,5},{8,6},{9,7},{10,... | collective-permute-start | bytes 983048 | tf_op jit(solution)/shard_map/ppermute | solution.py:31
  20.8 0.0 collective-permute-done.5
  20.8 0.0 collective-permute-done.4
  20.8 0.0 collective-permute-done.3
  20.8 0.1 pad_maximum_fusion.3
  20.8 0.3 collective-permute-start.12
  21.2 4.0 %collective-permute-start.14 = (bf16[4,2,32,640]{3,2,1,0:T(8,128)(2,1)S(1)}, bf16[4,2,32,640]{3,2,1,0:T(8,128)(2,1)S(1)}, u32[]{:S(2)}, u32[]{:S(2)}) collective-permute-start(bf16[4,2,32,640]{3,2,1,0:T(8,128)(2,1)S(1)} %pad_maximum_fusion.3), channel_id=1, source_target_pairs={{0,14},{1,15},{2,0},{3,1},{4,2},{5,3},{6,4},{7,5},{8,6},{9,7},{10,... | collective-permute-start | bytes 983048 | tf_op jit(solution)/shard_map/ppermute | solution.py:31
  25.2 0.1 maximum_maximum_fusion.refs_4_
  25.3 0.1 constant_dynamic-slice_fusion
  25.4 0.0 copy-start
  25.4 1.1 %collective-permute-start.8 = (bf16[288,640]{1,0:T(8,128)(2,1)S(1)}, bf16[288,640]{1,0:T(8,128)(2,1)S(1)}, u32[]{:S(2)}, u32[]{:S(2)}) collective-permute-start(bf16[288,640]{1,0:T(8,128)(2,1)S(1)} %get-tuple-element.74), channel_id=1, source_target_pairs={{0,16},{1,17},{2,18},{3,19},{4,20},{5,21},{6,22},{7,23},{8,24},{9,... | collective-permute-start | bytes 1105928 | tf_op jit(solution)/shard_map/ppermute | solution.py:31
  26.5 2.6 %collective-permute-done.11 = bf16[4,2,32,640]{3,2,1,0:T(8,128)(2,1)S(1)} collective-permute-done((bf16[4,2,32,640]{3,2,1,0:T(8,128)(2,1)S(1)}, bf16[4,2,32,640]{3,2,1,0:T(8,128)(2,1)S(1)}, u32[]{:S(2)}, u32[]{:S(2)}) %collective-permute-start.11) | collective-permute-done | bytes 327712 | tf_op jit(solution)/shard_map/ppermute | solution.py:31
  29.1 4.0 %collective-permute-done.12 = bf16[4,2,32,640]{3,2,1,0:T(8,128)(2,1)S(1)} collective-permute-done((bf16[4,2,32,640]{3,2,1,0:T(8,128)(2,1)S(1)}, bf16[4,2,32,640]{3,2,1,0:T(8,128)(2,1)S(1)}, u32[]{:S(2)}, u32[]{:S(2)}) %collective-permute-start.12) | collective-permute-done | bytes 327712 | tf_op jit(solution)/shard_map/ppermute | solution.py:31
  33.1 0.1 pad_maximum_fusion.refs_5_
  33.2 0.1 pad_maximum_fusion.1.refs_6_
  33.3 0.9 collective-permute-done.8.refs_1_
  34.2 3.2 %collective-permute-start.16 = (bf16[4,2,64,640]{3,2,1,0:T(8,128)(2,1)S(1)}, bf16[4,2,64,640]{3,2,1,0:T(8,128)(2,1)S(1)}, u32[]{:S(2)}, u32[]{:S(2)}) collective-permute-start(bf16[4,2,64,640]{3,2,1,0:T(8,128)(2,1)S(1)} %pad_maximum_fusion.1.refs_6_), channel_id=1, source_target_pairs={{0,14},{1,15},{2,0},{3,1},{4,2},{5,3},{6,4},{7,5},{8,6},{9,7},{10,... | collective-permute-start | bytes 1966088 | tf_op jit(solution)/shard_map/ppermute | solution.py:31
  37.4 2.1 %collective-permute-start.7 = (bf16[288,2560]{1,0:T(8,128)(2,1)S(1)}, bf16[288,2560]{1,0:T(8,128)(2,1)S(1)}, u32[]{:S(2)}, u32[]{:S(2)}) collective-permute-start(bf16[288,2560]{1,0:T(8,128)(2,1)S(1)} %bitcast.20), channel_id=1, source_target_pairs={{0,128},{64,192},{128,0},{192,64},{1,129},{65,193},{129,1},{193,65... | collective-permute-start | bytes 4423688 | tf_op jit(solution)/shard_map/ppermute | solution.py:36
  39.6 2.1 %collective-permute-start.10 = (bf16[288,640]{1,0:T(8,128)(2,1)S(1)}, bf16[288,640]{1,0:T(8,128)(2,1)S(1)}, u32[]{:S(2)}, u32[]{:S(2)}) collective-permute-start(bf16[288,640]{1,0:T(8,128)(2,1)S(1)} %get-tuple-element.72), channel_id=1, source_target_pairs={{0,48},{1,49},{2,50},{3,51},{4,52},{5,53},{6,54},{7,55},{8,56},{9,... | collective-permute-start | bytes 1105928 | tf_op jit(solution)/shard_map/ppermute | solution.py:31
  41.7 5.4 %collective-permute-done.10.refs_3_ = bf16[288,640]{1,0:T(8,128)(2,1)S(1)} collective-permute-done((bf16[288,640]{1,0:T(8,128)(2,1)S(1)}, bf16[288,640]{1,0:T(8,128)(2,1)S(1)}, u32[]{:S(2)}, u32[]{:S(2)}) %collective-permute-start.10) | collective-permute-done | bytes 368672 | tf_op jit(solution)/shard_map/ppermute | solution.py:31
  47.1 1.7 %collective-permute-done.15.refs_7_ = bf16[4,2,64,640]{3,2,1,0:T(8,128)(2,1)S(1)} collective-permute-done((bf16[4,2,64,640]{3,2,1,0:T(8,128)(2,1)S(1)}, bf16[4,2,64,640]{3,2,1,0:T(8,128)(2,1)S(1)}, u32[]{:S(2)}, u32[]{:S(2)}) %collective-permute-start.15) | collective-permute-done | bytes 655392 | tf_op jit(solution)/shard_map/ppermute | solution.py:31
  48.8 0.3 collective-permute-start.18
  49.2 3.3 %collective-permute-start.19 = (bf16[4,2,64,384]{3,2,1,0:T(8,128)(2,1)S(1)}, bf16[4,2,64,384]{3,2,1,0:T(8,128)(2,1)S(1)}, u32[]{:S(2)}, u32[]{:S(2)}) collective-permute-start(bf16[4,2,64,384]{3,2,1,0:T(8,128)(2,1)S(1)} %slice.32), channel_id=1, source_target_pairs={{0,14},{1,15},{2,0},{3,1},{4,2},{5,3},{6,4},{7,5},{8,6},{9,7},{10,... | collective-permute-start | bytes 1179656 | tf_op jit(solution)/shard_map/ppermute | solution.py:31
  52.5 2.2 %collective-permute-start.9 = (bf16[288,640]{1,0:T(8,128)(2,1)S(1)}, bf16[288,640]{1,0:T(8,128)(2,1)S(1)}, u32[]{:S(2)}, u32[]{:S(2)}) collective-permute-start(bf16[288,640]{1,0:T(8,128)(2,1)S(1)} %get-tuple-element.73), channel_id=1, source_target_pairs={{0,32},{1,33},{2,34},{3,35},{4,36},{5,37},{6,38},{7,39},{8,40},{9,... | collective-permute-start | bytes 1105928 | tf_op jit(solution)/shard_map/ppermute | solution.py:31
  54.7 5.1 %collective-permute-done.18.refs_9_ = bf16[4,2,64,384]{3,2,1,0:T(8,128)(2,1)S(1)} collective-permute-done((bf16[4,2,64,384]{3,2,1,0:T(8,128)(2,1)S(1)}, bf16[4,2,64,384]{3,2,1,0:T(8,128)(2,1)S(1)}, u32[]{:S(2)}, u32[]{:S(2)}) %collective-permute-start.18) | collective-permute-done | bytes 393248 | tf_op jit(solution)/shard_map/ppermute | solution.py:31
  59.8 0.1 collective-permute-start.20
  59.9 3.6 %collective-permute-start.21 = (bf16[4,2,32,384]{3,2,1,0:T(8,128)(2,1)S(1)}, bf16[4,2,32,384]{3,2,1,0:T(8,128)(2,1)S(1)}, u32[]{:S(2)}, u32[]{:S(2)}) collective-permute-start(bf16[4,2,32,384]{3,2,1,0:T(8,128)(2,1)S(1)} %slice.41), channel_id=1, source_target_pairs={{0,14},{1,15},{2,0},{3,1},{4,2},{5,3},{6,4},{7,5},{8,6},{9,7},{10,... | collective-permute-start | bytes 589832 | tf_op jit(solution)/shard_map/ppermute | solution.py:31
  63.6 0.1 collective-permute-start.17
  63.7 3.2 %collective-permute-start.22 = (bf16[4,2,64,256]{3,2,1,0:T(8,128)(2,1)S(1)}, bf16[4,2,64,256]{3,2,1,0:T(8,128)(2,1)S(1)}, u32[]{:S(2)}, u32[]{:S(2)}) collective-permute-start(bf16[4,2,64,256]{3,2,1,0:T(8,128)(2,1)S(1)} %slice.35), channel_id=1, source_target_pairs={{0,14},{1,15},{2,0},{3,1},{4,2},{5,3},{6,4},{7,5},{8,6},{9,7},{10,... | collective-permute-start | bytes 786440 | tf_op jit(solution)/shard_map/ppermute | solution.py:31
  66.9 7.4 %shard_map.69 = (bf16[288,384]{1,0:T(8,128)(2,1)S(1)}, bf16[288,384]{1,0:T(8,128)(2,1)S(1)}, bf16[288,384]{1,0:T(8,128)(2,1)S(1)}, bf16[288,384]{1,0:T(8,128)(2,1)S(1)}) custom-call(s32[3]{0:T(128)S(1)} %pad_add_fusion.where_ref, bf16[288,2560]{1,0:T(8,128)(2,1)S(1)} %bitcast.23, bf16[288,640]{1,0:T(8,128)(2,1)S(1)} %collective-permute-done.8.refs_1_, ...), custom_call_target="tpu_custom_call" | custom-call | flops 3397386240 | bytes 3145728 | tf_op jit(solution)/shard_map/pallas_call | solution.py:154
  74.3 1.4 %collective-permute-start.23 = (bf16[4,2,32,256]{3,2,1,0:T(8,128)(2,1)S(1)}, bf16[4,2,32,256]{3,2,1,0:T(8,128)(2,1)S(1)}, u32[]{:S(2)}, u32[]{:S(2)}) collective-permute-start(bf16[4,2,32,256]{3,2,1,0:T(8,128)(2,1)S(1)} %slice.36), channel_id=1, source_target_pairs={{0,2},{1,3},{2,4},{3,5},{4,6},{5,7},{6,8},{7,9},{8,10},{9,11},{10,... | collective-permute-start | bytes 393224 | tf_op jit(solution)/shard_map/ppermute | solution.py:31
  75.8 2.5 %collective-permute-start.24 = (bf16[4,2,32,256]{3,2,1,0:T(8,128)(2,1)S(1)}, bf16[4,2,32,256]{3,2,1,0:T(8,128)(2,1)S(1)}, u32[]{:S(2)}, u32[]{:S(2)}) collective-permute-start(bf16[4,2,32,256]{3,2,1,0:T(8,128)(2,1)S(1)} %slice.37), channel_id=1, source_target_pairs={{0,14},{1,15},{2,0},{3,1},{4,2},{5,3},{6,4},{7,5},{8,6},{9,7},{10,... | collective-permute-start | bytes 393224 | tf_op jit(solution)/shard_map/ppermute | solution.py:31
  78.2 1.2 %collective-permute-start.26 = (bf16[288,384]{1,0:T(8,128)(2,1)S(1)}, bf16[288,384]{1,0:T(8,128)(2,1)S(1)}, u32[]{:S(2)}, u32[]{:S(2)}) collective-permute-start(bf16[288,384]{1,0:T(8,128)(2,1)S(1)} %get-tuple-element.60), channel_id=1, source_target_pairs={{0,48},{1,49},{2,50},{3,51},{4,52},{5,53},{6,54},{7,55},{8,56},{9,... | collective-permute-start | bytes 663560 | tf_op jit(solution)/shard_map/ppermute | solution.py:31
  79.5 0.4 shard_map.72
  79.8 0.0 collective-permute-done.7.mirrored_ref
  79.9 0.1 collective-permute-start.25
  80.0 1.8 %collective-permute-start.27 = (bf16[288,384]{1,0:T(8,128)(2,1)S(1)}, bf16[288,384]{1,0:T(8,128)(2,1)S(1)}, u32[]{:S(2)}, u32[]{:S(2)}) collective-permute-start(bf16[288,384]{1,0:T(8,128)(2,1)S(1)} %get-tuple-element.61), channel_id=1, source_target_pairs={{0,32},{1,33},{2,34},{3,35},{4,36},{5,37},{6,38},{7,39},{8,40},{9,... | collective-permute-start | bytes 663560 | tf_op jit(solution)/shard_map/ppermute | solution.py:31
  81.8 0.2 collective-permute-start.28
  82.0 5.2 %shard_map.70 = (bf16[288,256]{1,0:T(8,128)(2,1)S(1)}, bf16[288,256]{1,0:T(8,128)(2,1)S(1)}, bf16[288,256]{1,0:T(8,128)(2,1)S(1)}, bf16[288,256]{1,0:T(8,128)(2,1)S(1)}) custom-call(s32[3]{0:T(128)S(1)} %pad_add_fusion.where_ref, bf16[288,2560]{1,0:T(8,128)(2,1)S(1)} %bitcast.24, bf16[288,640]{1,0:T(8,128)(2,1)S(1)} %collective-permute-done.8.refs_1_, ...), custom_call_target="tpu_custom_call" | custom-call | flops 2264924160 | bytes 2097152 | tf_op jit(solution)/shard_map/pallas_call | solution.py:154
  87.2 3.1 %collective-permute-start.30 = (bf16[288,256]{1,0:T(8,128)(2,1)S(1)}, bf16[288,256]{1,0:T(8,128)(2,1)S(1)}, u32[]{:S(2)}, u32[]{:S(2)}) collective-permute-start(bf16[288,256]{1,0:T(8,128)(2,1)S(1)} %get-tuple-element.65), channel_id=1, source_target_pairs={{0,48},{1,49},{2,50},{3,51},{4,52},{5,53},{6,54},{7,55},{8,56},{9,... | collective-permute-start | bytes 442376 | tf_op jit(solution)/shard_map/ppermute | solution.py:31
  90.3 0.6 collective-permute-start.31
  90.9 0.8 collective-permute-start.32
  91.7 2.8 %collective-permute-done.28.refs_3_ = bf16[288,384]{1,0:T(8,128)(2,1)S(1)} collective-permute-done((bf16[288,384]{1,0:T(8,128)(2,1)S(1)}, bf16[288,384]{1,0:T(8,128)(2,1)S(1)}, u32[]{:S(2)}, u32[]{:S(2)}) %collective-permute-start.28) | collective-permute-done | bytes 221216 | tf_op jit(solution)/shard_map/ppermute | solution.py:31
  94.5 2.3 %collective-permute-start.29 = (bf16[8,2560]{1,0:T(8,128)(2,1)S(1)}, bf16[8,2560]{1,0:T(8,128)(2,1)S(1)}, u32[]{:S(2)}, u32[]{:S(2)}) collective-permute-start(bf16[8,2560]{1,0:T(8,128)(2,1)S(1)} %slice_bitcast_fusion), channel_id=1, source_target_pairs={{0,65},{1,66},{2,67},{3,68},{4,69},{5,70},{6,71},{7,72},{8,73},{9,... | collective-permute-start | bytes 122888 | tf_op jit(solution)/shard_map/ppermute | solution.py:44
  96.8 0.5 shard_map.71.base_ref
  97.3 2.5 %collective-permute-done.29.rim_ref = bf16[8,2560]{1,0:T(8,128)(2,1)S(1)} collective-permute-done((bf16[8,2560]{1,0:T(8,128)(2,1)S(1)}, bf16[8,2560]{1,0:T(8,128)(2,1)S(1)}, u32[]{:S(2)}, u32[]{:S(2)}) %collective-permute-start.29) | collective-permute-done | bytes 40992 | tf_op jit(solution)/shard_map/ppermute | solution.py:44
  99.8 1.8 %collective-permute-done.32.refs_7_ = bf16[288,256]{1,0:T(8,128)(2,1)S(1)} collective-permute-done((bf16[288,256]{1,0:T(8,128)(2,1)S(1)}, bf16[288,256]{1,0:T(8,128)(2,1)S(1)}, u32[]{:S(2)}, u32[]{:S(2)}) %collective-permute-start.32) | collective-permute-done | bytes 147488 | tf_op jit(solution)/shard_map/ppermute | solution.py:31
  101.7 1.9 %shard_map.73 = (bf16[288,2560]{1,0:T(8,128)(2,1)}, bf16[32,2560]{1,0:T(8,128)(2,1)}) custom-call(s32[3]{0:T(128)S(1)} %pad_add_fusion.where_ref, f32[288,2560]{1,0:T(8,128)S(1)} %shard_map.71.base_ref, bf16[32,2560]{1,0:T(8,128)(2,1)S(1)} %collective-permute-done.25.pooled_ref, bf16[8,2560]{1,0:T(8,128)(2,1)S(1)} %collective-permute-done.29.rim_ref, ...), custom_call_target="tpu_custom_call" | custom-call | flops 737280 | bytes 5898240 | tf_op jit(solution)/shard_map/pallas_call | solution.py:219
  (34 shorter events, 0.2 us)
Async XLA Ops:
  0.7 0.9 copy-start.3
  1.7 0.9 copy-start.4
  3.2 5.7 %collective-permute-start = (bf16[2,32,640]{2,1,0:T(8,128)(2,1)S(1)}, bf16[2,32,640]{2,1,0:T(8,128)(2,1)S(1)}, u32[]{:S(2)}, u32[]{:S(2)}) collective-permute-start(bf16[2,32,640]{2,1,0:T(8,128)(2,1)S(1)} %get-tuple-element.42), channel_id=1, source_target_pairs={{0,16},{1,17},{2,18},{3,19},{4,20},{5,21},{6,22},{7,23},{8,24},{9,... | collective-permute-start | bytes 245768 | tf_op jit(solution)/shard_map/ppermute | solution.py:31
  4.8 9.2 %collective-permute-start.2 = (bf16[2,32,640]{2,1,0:T(8,128)(2,1)S(1)}, bf16[2,32,640]{2,1,0:T(8,128)(2,1)S(1)}, u32[]{:S(2)}, u32[]{:S(2)}) collective-permute-start(bf16[2,32,640]{2,1,0:T(8,128)(2,1)S(1)} %get-tuple-element.44), channel_id=1, source_target_pairs={{0,48},{1,49},{2,50},{3,51},{4,52},{5,53},{6,54},{7,55},{8,56},{9,... | collective-permute-start | bytes 245768 | tf_op jit(solution)/shard_map/ppermute | solution.py:31
  6.5 8.5 %collective-permute-start.1 = (bf16[2,32,640]{2,1,0:T(8,128)(2,1)S(1)}, bf16[2,32,640]{2,1,0:T(8,128)(2,1)S(1)}, u32[]{:S(2)}, u32[]{:S(2)}) collective-permute-start(bf16[2,32,640]{2,1,0:T(8,128)(2,1)S(1)} %get-tuple-element.43), channel_id=1, source_target_pairs={{0,32},{1,33},{2,34},{3,35},{4,36},{5,37},{6,38},{7,39},{8,40},{9,... | collective-permute-start | bytes 245768 | tf_op jit(solution)/shard_map/ppermute | solution.py:31
  8.9 7.8 %collective-permute-start.6 = (bf16[2,32,640]{2,1,0:T(8,128)(2,1)S(1)}, bf16[2,32,640]{2,1,0:T(8,128)(2,1)S(1)}, u32[]{:S(2)}, u32[]{:S(2)}) collective-permute-start(bf16[2,32,640]{2,1,0:T(8,128)(2,1)S(1)} %get-tuple-element.44), channel_id=1, source_target_pairs={{0,49},{1,48},{2,51},{3,50},{4,53},{5,52},{6,55},{7,54},{8,57},{9,... | collective-permute-start | bytes 245768 | tf_op jit(solution)/shard_map/ppermute | solution.py:31
  11.1 9.7 %collective-permute-start.5 = (bf16[2,32,640]{2,1,0:T(8,128)(2,1)S(1)}, bf16[2,32,640]{2,1,0:T(8,128)(2,1)S(1)}, u32[]{:S(2)}, u32[]{:S(2)}) collective-permute-start(bf16[2,32,640]{2,1,0:T(8,128)(2,1)S(1)} %get-tuple-element.43), channel_id=1, source_target_pairs={{0,33},{1,32},{2,35},{3,34},{4,37},{5,36},{6,39},{7,38},{8,41},{9,... | collective-permute-start | bytes 245768 | tf_op jit(solution)/shard_map/ppermute | solution.py:31
  12.2 8.5 %collective-permute-start.4 = (bf16[2,32,640]{2,1,0:T(8,128)(2,1)S(1)}, bf16[2,32,640]{2,1,0:T(8,128)(2,1)S(1)}, u32[]{:S(2)}, u32[]{:S(2)}) collective-permute-start(bf16[2,32,640]{2,1,0:T(8,128)(2,1)S(1)} %get-tuple-element.42), channel_id=1, source_target_pairs={{0,17},{1,16},{2,19},{3,18},{4,21},{5,20},{6,23},{7,22},{8,25},{9,... | collective-permute-start | bytes 245768 | tf_op jit(solution)/shard_map/ppermute | solution.py:31
  14.0 6.7 %collective-permute-start.3 = (bf16[2,32,640]{2,1,0:T(8,128)(2,1)S(1)}, bf16[2,32,640]{2,1,0:T(8,128)(2,1)S(1)}, u32[]{:S(2)}, u32[]{:S(2)}) collective-permute-start(bf16[2,32,640]{2,1,0:T(8,128)(2,1)S(1)} %get-tuple-element.41), channel_id=1, source_target_pairs={{0,1},{1,0},{2,3},{3,2},{4,5},{5,4},{6,7},{7,6},{8,9},{9,8},{10,11... | collective-permute-start | bytes 245768 | tf_op jit(solution)/shard_map/ppermute | solution.py:31
  15.0 10.3 %copy-start.1 = (bf16[1,288,2560]{2,1,0:T(8,128)(2,1)S(1)}, bf16[1,288,2560]{2,1,0:T(8,128)(2,1)}, u32[]{:S(2)}) copy-start(bf16[1,288,2560]{2,1,0:T(8,128)(2,1)} %param.6) | copy-start | bytes 4423684
  15.0 14.1 %collective-permute-start.11 = (bf16[4,2,32,640]{3,2,1,0:T(8,128)(2,1)S(1)}, bf16[4,2,32,640]{3,2,1,0:T(8,128)(2,1)S(1)}, u32[]{:S(2)}, u32[]{:S(2)}) collective-permute-start(bf16[4,2,32,640]{3,2,1,0:T(8,128)(2,1)S(1)} %pad_maximum_fusion.2), channel_id=1, source_target_pairs={{0,2},{1,3},{2,4},{3,5},{4,6},{5,7},{6,8},{7,9},{8,10},{9,11},{10,... | collective-permute-start | bytes 983048 | tf_op jit(solution)/shard_map/ppermute | solution.py:31
  16.7 16.5 %collective-permute-start.13 = (bf16[4,2,32,640]{3,2,1,0:T(8,128)(2,1)S(1)}, bf16[4,2,32,640]{3,2,1,0:T(8,128)(2,1)S(1)}, u32[]{:S(2)}, u32[]{:S(2)}) collective-permute-start(bf16[4,2,32,640]{3,2,1,0:T(8,128)(2,1)S(1)} %pad_maximum_fusion.2), channel_id=1, source_target_pairs={{0,14},{1,15},{2,0},{3,1},{4,2},{5,3},{6,4},{7,5},{8,6},{9,7},{10,... | collective-permute-start | bytes 983048 | tf_op jit(solution)/shard_map/ppermute | solution.py:31
  20.8 12.3 %collective-permute-start.12 = (bf16[4,2,32,640]{3,2,1,0:T(8,128)(2,1)S(1)}, bf16[4,2,32,640]{3,2,1,0:T(8,128)(2,1)S(1)}, u32[]{:S(2)}, u32[]{:S(2)}) collective-permute-start(bf16[4,2,32,640]{3,2,1,0:T(8,128)(2,1)S(1)} %pad_maximum_fusion.3), channel_id=1, source_target_pairs={{0,2},{1,3},{2,4},{3,5},{4,6},{5,7},{6,8},{7,9},{8,10},{9,11},{10,... | collective-permute-start | bytes 983048 | tf_op jit(solution)/shard_map/ppermute | solution.py:31
  21.2 12.0 %collective-permute-start.14 = (bf16[4,2,32,640]{3,2,1,0:T(8,128)(2,1)S(1)}, bf16[4,2,32,640]{3,2,1,0:T(8,128)(2,1)S(1)}, u32[]{:S(2)}, u32[]{:S(2)}) collective-permute-start(bf16[4,2,32,640]{3,2,1,0:T(8,128)(2,1)S(1)} %pad_maximum_fusion.3), channel_id=1, source_target_pairs={{0,14},{1,15},{2,0},{3,1},{4,2},{5,3},{6,4},{7,5},{8,6},{9,7},{10,... | collective-permute-start | bytes 983048 | tf_op jit(solution)/shard_map/ppermute | solution.py:31
  25.4 12.1 %copy-start = (bf16[1,288,2560]{2,1,0:T(8,128)(2,1)S(1)}, bf16[1,288,2560]{2,1,0:T(8,128)(2,1)}, u32[]{:S(2)}) copy-start(bf16[1,288,2560]{2,1,0:T(8,128)(2,1)} %param.5) | copy-start | bytes 4423684
  25.4 8.8 %collective-permute-start.8 = (bf16[288,640]{1,0:T(8,128)(2,1)S(1)}, bf16[288,640]{1,0:T(8,128)(2,1)S(1)}, u32[]{:S(2)}, u32[]{:S(2)}) collective-permute-start(bf16[288,640]{1,0:T(8,128)(2,1)S(1)} %get-tuple-element.74), channel_id=1, source_target_pairs={{0,16},{1,17},{2,18},{3,19},{4,20},{5,21},{6,22},{7,23},{8,24},{9,... | collective-permute-start | bytes 1105928 | tf_op jit(solution)/shard_map/ppermute | solution.py:31
  34.2 14.6 %collective-permute-start.15 = (bf16[4,2,64,640]{3,2,1,0:T(8,128)(2,1)S(1)}, bf16[4,2,64,640]{3,2,1,0:T(8,128)(2,1)S(1)}, u32[]{:S(2)}, u32[]{:S(2)}) collective-permute-start(bf16[4,2,64,640]{3,2,1,0:T(8,128)(2,1)S(1)} %pad_maximum_fusion.refs_5_), channel_id=1, source_target_pairs={{0,2},{1,3},{2,4},{3,5},{4,6},{5,7},{6,8},{7,9},{8,10},{9,11},{10,... | collective-permute-start | bytes 1966088 | tf_op jit(solution)/shard_map/ppermute | solution.py:31
  34.2 14.9 %collective-permute-start.16 = (bf16[4,2,64,640]{3,2,1,0:T(8,128)(2,1)S(1)}, bf16[4,2,64,640]{3,2,1,0:T(8,128)(2,1)S(1)}, u32[]{:S(2)}, u32[]{:S(2)}) collective-permute-start(bf16[4,2,64,640]{3,2,1,0:T(8,128)(2,1)S(1)} %pad_maximum_fusion.1.refs_6_), channel_id=1, source_target_pairs={{0,14},{1,15},{2,0},{3,1},{4,2},{5,3},{6,4},{7,5},{8,6},{9,7},{10,... | collective-permute-start | bytes 1966088 | tf_op jit(solution)/shard_map/ppermute | solution.py:31
  37.4 42.4 %collective-permute-start.7 = (bf16[288,2560]{1,0:T(8,128)(2,1)S(1)}, bf16[288,2560]{1,0:T(8,128)(2,1)S(1)}, u32[]{:S(2)}, u32[]{:S(2)}) collective-permute-start(bf16[288,2560]{1,0:T(8,128)(2,1)S(1)} %bitcast.20), channel_id=1, source_target_pairs={{0,128},{64,192},{128,0},{192,64},{1,129},{65,193},{129,1},{193,65... | collective-permute-start | bytes 4423688 | tf_op jit(solution)/shard_map/ppermute | solution.py:36
  39.6 7.5 %collective-permute-start.10 = (bf16[288,640]{1,0:T(8,128)(2,1)S(1)}, bf16[288,640]{1,0:T(8,128)(2,1)S(1)}, u32[]{:S(2)}, u32[]{:S(2)}) collective-permute-start(bf16[288,640]{1,0:T(8,128)(2,1)S(1)} %get-tuple-element.72), channel_id=1, source_target_pairs={{0,48},{1,49},{2,50},{3,51},{4,52},{5,53},{6,54},{7,55},{8,56},{9,... | collective-permute-start | bytes 1105928 | tf_op jit(solution)/shard_map/ppermute | solution.py:31
  48.8 10.9 %collective-permute-start.18 = (bf16[4,2,64,384]{3,2,1,0:T(8,128)(2,1)S(1)}, bf16[4,2,64,384]{3,2,1,0:T(8,128)(2,1)S(1)}, u32[]{:S(2)}, u32[]{:S(2)}) collective-permute-start(bf16[4,2,64,384]{3,2,1,0:T(8,128)(2,1)S(1)} %slice.31), channel_id=1, source_target_pairs={{0,2},{1,3},{2,4},{3,5},{4,6},{5,7},{6,8},{7,9},{8,10},{9,11},{10,... | collective-permute-start | bytes 1179656 | tf_op jit(solution)/shard_map/ppermute | solution.py:31
  49.2 10.7 %collective-permute-start.19 = (bf16[4,2,64,384]{3,2,1,0:T(8,128)(2,1)S(1)}, bf16[4,2,64,384]{3,2,1,0:T(8,128)(2,1)S(1)}, u32[]{:S(2)}, u32[]{:S(2)}) collective-permute-start(bf16[4,2,64,384]{3,2,1,0:T(8,128)(2,1)S(1)} %slice.32), channel_id=1, source_target_pairs={{0,14},{1,15},{2,0},{3,1},{4,2},{5,3},{6,4},{7,5},{8,6},{9,7},{10,... | collective-permute-start | bytes 1179656 | tf_op jit(solution)/shard_map/ppermute | solution.py:31
  52.5 11.2 %collective-permute-start.9 = (bf16[288,640]{1,0:T(8,128)(2,1)S(1)}, bf16[288,640]{1,0:T(8,128)(2,1)S(1)}, u32[]{:S(2)}, u32[]{:S(2)}) collective-permute-start(bf16[288,640]{1,0:T(8,128)(2,1)S(1)} %get-tuple-element.73), channel_id=1, source_target_pairs={{0,32},{1,33},{2,34},{3,35},{4,36},{5,37},{6,38},{7,39},{8,40},{9,... | collective-permute-start | bytes 1105928 | tf_op jit(solution)/shard_map/ppermute | solution.py:31
  59.8 7.1 %collective-permute-start.20 = (bf16[4,2,32,384]{3,2,1,0:T(8,128)(2,1)S(1)}, bf16[4,2,32,384]{3,2,1,0:T(8,128)(2,1)S(1)}, u32[]{:S(2)}, u32[]{:S(2)}) collective-permute-start(bf16[4,2,32,384]{3,2,1,0:T(8,128)(2,1)S(1)} %slice.40), channel_id=1, source_target_pairs={{0,2},{1,3},{2,4},{3,5},{4,6},{5,7},{6,8},{7,9},{8,10},{9,11},{10,... | collective-permute-start | bytes 589832 | tf_op jit(solution)/shard_map/ppermute | solution.py:31
  59.9 7.0 %collective-permute-start.21 = (bf16[4,2,32,384]{3,2,1,0:T(8,128)(2,1)S(1)}, bf16[4,2,32,384]{3,2,1,0:T(8,128)(2,1)S(1)}, u32[]{:S(2)}, u32[]{:S(2)}) collective-permute-start(bf16[4,2,32,384]{3,2,1,0:T(8,128)(2,1)S(1)} %slice.41), channel_id=1, source_target_pairs={{0,14},{1,15},{2,0},{3,1},{4,2},{5,3},{6,4},{7,5},{8,6},{9,7},{10,... | collective-permute-start | bytes 589832 | tf_op jit(solution)/shard_map/ppermute | solution.py:31
  63.6 10.7 %collective-permute-start.17 = (bf16[4,2,64,256]{3,2,1,0:T(8,128)(2,1)S(1)}, bf16[4,2,64,256]{3,2,1,0:T(8,128)(2,1)S(1)}, u32[]{:S(2)}, u32[]{:S(2)}) collective-permute-start(bf16[4,2,64,256]{3,2,1,0:T(8,128)(2,1)S(1)} %slice.30), channel_id=1, source_target_pairs={{0,2},{1,3},{2,4},{3,5},{4,6},{5,7},{6,8},{7,9},{8,10},{9,11},{10,... | collective-permute-start | bytes 786440 | tf_op jit(solution)/shard_map/ppermute | solution.py:31
  63.7 10.6 %collective-permute-start.22 = (bf16[4,2,64,256]{3,2,1,0:T(8,128)(2,1)S(1)}, bf16[4,2,64,256]{3,2,1,0:T(8,128)(2,1)S(1)}, u32[]{:S(2)}, u32[]{:S(2)}) collective-permute-start(bf16[4,2,64,256]{3,2,1,0:T(8,128)(2,1)S(1)} %slice.35), channel_id=1, source_target_pairs={{0,14},{1,15},{2,0},{3,1},{4,2},{5,3},{6,4},{7,5},{8,6},{9,7},{10,... | collective-permute-start | bytes 786440 | tf_op jit(solution)/shard_map/ppermute | solution.py:31
  74.3 7.5 %collective-permute-start.23 = (bf16[4,2,32,256]{3,2,1,0:T(8,128)(2,1)S(1)}, bf16[4,2,32,256]{3,2,1,0:T(8,128)(2,1)S(1)}, u32[]{:S(2)}, u32[]{:S(2)}) collective-permute-start(bf16[4,2,32,256]{3,2,1,0:T(8,128)(2,1)S(1)} %slice.36), channel_id=1, source_target_pairs={{0,2},{1,3},{2,4},{3,5},{4,6},{5,7},{6,8},{7,9},{8,10},{9,11},{10,... | collective-permute-start | bytes 393224 | tf_op jit(solution)/shard_map/ppermute | solution.py:31
  75.8 6.2 %collective-permute-start.24 = (bf16[4,2,32,256]{3,2,1,0:T(8,128)(2,1)S(1)}, bf16[4,2,32,256]{3,2,1,0:T(8,128)(2,1)S(1)}, u32[]{:S(2)}, u32[]{:S(2)}) collective-permute-start(bf16[4,2,32,256]{3,2,1,0:T(8,128)(2,1)S(1)} %slice.37), channel_id=1, source_target_pairs={{0,14},{1,15},{2,0},{3,1},{4,2},{5,3},{6,4},{7,5},{8,6},{9,7},{10,... | collective-permute-start | bytes 393224 | tf_op jit(solution)/shard_map/ppermute | solution.py:31
  78.2 12.6 %collective-permute-start.26 = (bf16[288,384]{1,0:T(8,128)(2,1)S(1)}, bf16[288,384]{1,0:T(8,128)(2,1)S(1)}, u32[]{:S(2)}, u32[]{:S(2)}) collective-permute-start(bf16[288,384]{1,0:T(8,128)(2,1)S(1)} %get-tuple-element.60), channel_id=1, source_target_pairs={{0,48},{1,49},{2,50},{3,51},{4,52},{5,53},{6,54},{7,55},{8,56},{9,... | collective-permute-start | bytes 663560 | tf_op jit(solution)/shard_map/ppermute | solution.py:31
  79.9 7.3 %collective-permute-start.25 = (bf16[32,2560]{1,0:T(8,128)(2,1)S(1)}, bf16[32,2560]{1,0:T(8,128)(2,1)S(1)}, u32[]{:S(2)}, u32[]{:S(2)}) collective-permute-start(bf16[32,2560]{1,0:T(8,128)(2,1)S(1)} %shard_map.72), channel_id=1, source_target_pairs={{0,64},{64,128},{128,192},{192,0},{1,65},{65,129},{129,193},{193,1... | collective-permute-start | bytes 491528 | tf_op jit(solution)/shard_map/ppermute | solution.py:36
  80.0 11.7 %collective-permute-start.27 = (bf16[288,384]{1,0:T(8,128)(2,1)S(1)}, bf16[288,384]{1,0:T(8,128)(2,1)S(1)}, u32[]{:S(2)}, u32[]{:S(2)}) collective-permute-start(bf16[288,384]{1,0:T(8,128)(2,1)S(1)} %get-tuple-element.61), channel_id=1, source_target_pairs={{0,32},{1,33},{2,34},{3,35},{4,36},{5,37},{6,38},{7,39},{8,40},{9,... | collective-permute-start | bytes 663560 | tf_op jit(solution)/shard_map/ppermute | solution.py:31
  81.8 15.0 %copy-start.2 = (bf16[1,32,2560]{2,1,0:T(8,128)(2,1)S(1)}, bf16[1,32,2560]{2,1,0:T(8,128)(2,1)}, u32[]{:S(2)}) copy-start(bf16[1,32,2560]{2,1,0:T(8,128)(2,1)} %param.9) | copy-start | bytes 491524
  81.8 12.7 %collective-permute-start.28 = (bf16[288,384]{1,0:T(8,128)(2,1)S(1)}, bf16[288,384]{1,0:T(8,128)(2,1)S(1)}, u32[]{:S(2)}, u32[]{:S(2)}) collective-permute-start(bf16[288,384]{1,0:T(8,128)(2,1)S(1)} %get-tuple-element.62), channel_id=1, source_target_pairs={{0,16},{1,17},{2,18},{3,19},{4,20},{5,21},{6,22},{7,23},{8,24},{9,... | collective-permute-start | bytes 663560 | tf_op jit(solution)/shard_map/ppermute | solution.py:31
  87.2 12.6 %collective-permute-start.30 = (bf16[288,256]{1,0:T(8,128)(2,1)S(1)}, bf16[288,256]{1,0:T(8,128)(2,1)S(1)}, u32[]{:S(2)}, u32[]{:S(2)}) collective-permute-start(bf16[288,256]{1,0:T(8,128)(2,1)S(1)} %get-tuple-element.65), channel_id=1, source_target_pairs={{0,48},{1,49},{2,50},{3,51},{4,52},{5,53},{6,54},{7,55},{8,56},{9,... | collective-permute-start | bytes 442376 | tf_op jit(solution)/shard_map/ppermute | solution.py:31
  90.3 9.5 %collective-permute-start.31 = (bf16[288,256]{1,0:T(8,128)(2,1)S(1)}, bf16[288,256]{1,0:T(8,128)(2,1)S(1)}, u32[]{:S(2)}, u32[]{:S(2)}) collective-permute-start(bf16[288,256]{1,0:T(8,128)(2,1)S(1)} %get-tuple-element.67), channel_id=1, source_target_pairs={{0,32},{1,33},{2,34},{3,35},{4,36},{5,37},{6,38},{7,39},{8,40},{9,... | collective-permute-start | bytes 442376 | tf_op jit(solution)/shard_map/ppermute | solution.py:31
  90.9 10.8 %collective-permute-start.32 = (bf16[288,256]{1,0:T(8,128)(2,1)S(1)}, bf16[288,256]{1,0:T(8,128)(2,1)S(1)}, u32[]{:S(2)}, u32[]{:S(2)}) collective-permute-start(bf16[288,256]{1,0:T(8,128)(2,1)S(1)} %get-tuple-element.69), channel_id=1, source_target_pairs={{0,16},{1,17},{2,18},{3,19},{4,20},{5,21},{6,22},{7,23},{8,24},{9,... | collective-permute-start | bytes 442376 | tf_op jit(solution)/shard_map/ppermute | solution.py:31
  94.5 5.3 %collective-permute-start.29 = (bf16[8,2560]{1,0:T(8,128)(2,1)S(1)}, bf16[8,2560]{1,0:T(8,128)(2,1)S(1)}, u32[]{:S(2)}, u32[]{:S(2)}) collective-permute-start(bf16[8,2560]{1,0:T(8,128)(2,1)S(1)} %slice_bitcast_fusion), channel_id=1, source_target_pairs={{0,65},{1,66},{2,67},{3,68},{4,69},{5,70},{6,71},{7,72},{8,73},{9,... | collective-permute-start | bytes 122888 | tf_op jit(solution)/shard_map/ppermute | solution.py:44
